TPU v7x, 256 devices: a whole 4x4x8 slice. The times are simulated.
256 devices in a mesh: segment: 4 (over x), seq: 64 (over z, y, core).
Axes of the slice: x: 4, y: 4, z: 8, core: 2. Of those that a mesh axis runs over, the one named last changes fastest.
Arguments:
- layer_inputs: bfloat16 [4, 65536, 512], P('segment', 'seq'), may hold values from -6 to 6
- first_blocks: bfloat16 [4, 256, 256, 256], P('segment', 'seq'), may hold values from -0.375 to 0.375
- second_blocks: bfloat16 [4, 256, 256, 256], P('segment', 'seq'), may hold values from -0.375 to 0.375
- gate_scale: float32 [4, 512], P('segment'), may hold values from -4 to 4
- gate_shift: float32 [4, 512], P('segment'), may hold values from -4 to 4
- top_grads: bfloat16 [65536, 512], P('seq'), may hold values from -1.5 to 1.5
Outputs:
- input_grads: bfloat16 [4, 65536, 512], P('segment', 'seq')
- second_grads: float32 [4, 256, 256, 256], P('segment', 'seq')
All inputs are finite; a program needn't handle non-finite values.
Results may differ from a plain program's by a relative error of at most 0.015.
Values may be sent and summed in bfloat16 or wider, within the bound.
No kernel may reach another device: no remote copies, remote signals or barrier semaphores. Data moves between devices by JAX's collectives and lax.ppermute only.
A program may use at most 64 MiB of HBM per device.

v0:
```python
import functools

import jax
import jax.numpy as jnp
from jax import lax
from jax.experimental import pallas as pl
from jax.experimental.pallas import tpu as pltpu
from jax.sharding import PartitionSpec as P

BF = jnp.bfloat16
F32 = jnp.float32
VMEM_LIMIT = 16 * 1024 * 1024


def dot(a, b):
    return lax.dot_general(a, b, (((1,), (0,)), ((), ())), preferred_element_type=F32)


def dot_first(a, b):
    return lax.dot_general(a, b, (((0,), (0,)), ((), ())), preferred_element_type=F32)


def dot_last(a, b):
    return lax.dot_general(a, b, (((1,), (1,)), ((), ())), preferred_element_type=F32)


def spread(block, chunks, row):
    for col in range(4):
        chunks[pl.ds(row * 4 + col, 64, stride=16), :] = block[pl.ds(col, 64, stride=4), :]


def collect(chunks, block, row):
    for col in range(4):
        block[pl.ds(col, 64, stride=4), :] = chunks[pl.ds(row * 4 + col, 64, stride=16), :]


def first_kernel(firsts, inputs, out, block, chunks):
    for part in range(4):
        for row in range(4):
            block[...] = dot(firsts[row], inputs[row, :, part * 128:(part + 1) * 128])
            spread(block, chunks, row)
        out[part * 1024:(part + 1) * 1024, :] = chunks[...].astype(BF)


def gate_kernel(plane, upstream, own, near, far, last, own_v, near_v, far_v, last_v, out, held, vectors, block, chunks):
    index = plane[0]
    for step, (part, vector) in enumerate(((own, own_v), (near, near_v), (far, far_v), (last, last_v))):
        layer = (index + 4 - step) % 4
        held[layer] = part[...]
        vectors[layer] = vector[...]
    for row in range(4):
        rows = slice(row * 256, (row + 1) * 256)
        gate = jax.nn.sigmoid(held[3, rows, :].astype(F32) * vectors[3, 0:1, :] + vectors[3, 1:2, :])
        block[...] = upstream[rows, :].astype(F32) * gate
        spread(block, chunks, row)
    out[...] = chunks[...].astype(BF)


def column_kernel(layer, seconds, grads, firsts_out, out, wide_grads, wide_firsts, back, mixed):
    wide_grads[...] = grads[...].astype(F32)
    wide_firsts[...] = firsts_out[layer * 1024:(layer + 1) * 1024, :].astype(F32)
    for col in range(4):
        rows = pl.ds(col, 256, stride=4)
        weight = seconds[layer, col]
        back[rows, :] = dot_first(weight, wide_grads[rows, :].astype(BF))
        mixed[rows, :] = dot(weight, wide_firsts[rows, :].astype(BF))
    out[:, :16, :] = back[...].astype(BF).reshape(64, 16, 128)
    out[:, 16:, :] = mixed[...].astype(BF).reshape(64, 16, 128)


def second_kernel(grads0, grads1, grads2, grads3, firsts_out, out, wide_grads, wide_firsts):
    for layer, grads in enumerate((grads0, grads1, grads2, grads3)):
        wide_grads[...] = grads[...].astype(F32)
        wide_firsts[...] = firsts_out[layer * 1024:(layer + 1) * 1024, :].astype(F32)
        for col in range(4):
            rows = pl.ds(col, 256, stride=4)
            out[layer, col] = dot_last(
                wide_grads[rows, :].astype(BF), wide_firsts[rows, :].astype(BF)
            ).astype(BF)


def row_kernel(layer, received, firsts, upstream, held, vectors, *rest):
    last = layer == 0
    if last:
        out, chunks, mixed_chunks, block, mixed_block = rest
    else:
        out, next_out, chunks, mixed_chunks, block, mixed_block, next_chunks = rest
    chunks[...] = received[:, :16, :].reshape(1024, 128).astype(F32)
    mixed_chunks[...] = received[:, 16:, :].reshape(1024, 128).astype(F32)
    scale, shift = vectors[layer, 0:1, :], vectors[layer, 1:2, :]
    for row in range(4):
        rows = slice(row * 256, (row + 1) * 256)
        collect(chunks, block, row)
        collect(mixed_chunks, mixed_block, row)
        through = dot_first(firsts[layer, row], block[...].astype(BF))
        up = upstream[rows, :].astype(F32)
        gate = jax.nn.sigmoid(held[layer, rows, :].astype(F32) * scale + shift)
        slope = (up * gate * (1.0 - gate)).astype(BF).astype(F32)
        gate_grad = (slope * mixed_block[...]).astype(BF).astype(F32)
        result = (up + through + gate_grad * scale).astype(BF)
        out[rows, :] = result
        if not last:
            after = layer - 1
            gate = jax.nn.sigmoid(
                held[after, rows, :].astype(F32) * vectors[after, 0:1, :] + vectors[after, 1:2, :]
            )
            block[...] = result.astype(F32) * gate
            spread(block, next_chunks, row)
    if not last:
        next_out[...] = next_chunks[...].astype(BF)


def final_kernel(own, near, far, last, out):
    for part, value in enumerate((own, near, far, last)):
        out[:, part * 128:(part + 1) * 128] = value[...]


IN_VMEM = pl.BlockSpec(memory_space=pltpu.VMEM)
IN_SMEM = pl.BlockSpec(memory_space=pltpu.SMEM)


def call(kernel, count, out_shapes, scratch, flops, scalars=0):
    outs = [jax.ShapeDtypeStruct(s, d) for s, d in out_shapes]
    single = len(outs) == 1
    return pl.pallas_call(
        kernel,
        in_specs=[IN_SMEM] * scalars + [IN_VMEM] * count,
        out_shape=outs[0] if single else outs,
        out_specs=IN_VMEM if single else [IN_VMEM] * len(outs),
        scratch_shapes=[pltpu.VMEM(s, F32) for s in scratch],
        compiler_params=pltpu.CompilerParams(vmem_limit_bytes=VMEM_LIMIT),
        cost_estimate=pl.CostEstimate(flops=flops, bytes_accessed=2 << 20, transcendentals=0),
    )


TALL = (1024, 128)
BLOCK = (256, 128)
FLOPS = 2 * 4 * 256 * 256 * 128


def body(layer_inputs, first_blocks, second_blocks, gate_scale, gate_shift, top_grads):
    plane = lax.axis_index("segment")
    index = plane.astype(jnp.int32).reshape(1)
    inputs = layer_inputs[0]
    vectors = jnp.concatenate([gate_scale, gate_shift], 0)

    seconds_all = lax.all_gather(second_blocks, "segment", tiled=True)
    firsts_all = lax.all_gather(first_blocks, "segment", tiled=True)

    parts, own_vectors = [], []
    for step in range(4):
        start = ((plane + step) % 4) * 128
        part = lax.dynamic_slice_in_dim(inputs, start, 128, 1)
        vector = lax.dynamic_slice_in_dim(vectors, start, 128, 1)
        if step > 0:
            ring = [(i, (i + step) % 4) for i in range(4)]
            part = lax.ppermute(part, "segment", ring)
            vector = lax.ppermute(vector, "segment", ring)
        parts.append(part)
        own_vectors.append(vector)

    firsts_out = call(first_kernel, 2, [((4096, 128), BF)], [BLOCK, TALL], 4 * FLOPS)(
        first_blocks[0], inputs.reshape(4, 256, 512)
    )
    firsts_cols = lax.all_to_all(
        firsts_out.reshape(256, 16, 128), ("segment", "seq"), 0, 0, tiled=True
    ).reshape(4096, 128)

    upstream = lax.dynamic_slice_in_dim(top_grads, plane * 128, 128, 1)
    sends, held, vectors = call(
        gate_kernel,
        9,
        [(TALL, BF), ((4, 1024, 128), BF), ((4, 2, 128), F32)],
        [BLOCK, TALL],
        1 << 20,
        scalars=1,
    )(index, upstream, *parts, *own_vectors)

    results, grads = [None] * 4, [None] * 4
    for l in (3, 2, 1, 0):
        grads[l] = lax.all_to_all(sends.reshape(64, 16, 128), "seq", 0, 0, tiled=True).reshape(TALL)
        payload = call(
            functools.partial(column_kernel, l), 3, [((64, 32, 128), BF)], [TALL] * 4, 2 * FLOPS
        )(seconds_all, grads[l], firsts_cols)
        received = lax.all_to_all(payload, "seq", 0, 0, tiled=True)
        outs, scratch = [(TALL, BF)], [TALL, TALL, BLOCK, BLOCK]
        if l > 0:
            outs, scratch = outs + [(TALL, BF)], scratch + [TALL]
        made = call(functools.partial(row_kernel, l), 5, outs, scratch, FLOPS)(
            received, firsts_all, upstream, held, vectors
        )
        upstream, sends = (made, None) if l == 0 else made
        results[l] = upstream

    partials = call(second_kernel, 5, [((4, 4, 256, 256), BF)], [TALL, TALL], 4 * FLOPS)(
        *grads, firsts_cols
    )
    second = lax.psum_scatter(partials, "segment", scatter_dimension=0, tiled=True)
    back = lax.all_to_all(jnp.stack(results), "segment", 0, 0, tiled=True)
    grads_out = call(final_kernel, 4, [((1024, 512), BF)], [], 1 << 20)(*[back[i] for i in range(4)])
    return grads_out[None], second.astype(F32)


def solution(mesh):
    placed = (
        P("segment", "seq", None),
        P("segment", "seq", None, None),
        P("segment", "seq", None, None),
        P("segment", None),
        P("segment", None),
        P("seq", None),
    )
    return jax.shard_map(
        body,
        mesh=mesh,
        in_specs=placed,
        out_specs=(P("segment", "seq", None), P("segment", "seq", None, None)),
        check_vma=False,
    )
```

profile of v0, /device:TPU:1, one launch (start us, length us, event | category | flops | bytes accessed | tf_op | source)
XLA Modules:
  0.0 293.9 jit_solution(10989426237720261056)
XLA Ops:
  8.0 2.2 dynamic-slice_bitcast_fusion
  10.2 3.3 %collective-permute-start.2 = (bf16[1024,128]{1,0:T(8,128)(2,1)}, bf16[1024,128]{1,0:T(8,128)(2,1)S(1)}, u32[]{:S(2)}, u32[]{:S(2)}) collective-permute-start(bf16[1024,128]{1,0:T(8,128)(2,1)} %get-tuple-element.24), channel_id=1, source_target_pairs={{0,192},{64,0},{128,64},{192,128},{1,193},{65,1},{129,65},{193,129... | collective-permute-start | bytes 786440 | tf_op jit(solution)/shard_map/ppermute | solution.py:157
  14.8 2.1 collective-permute-start.5
  16.9 7.4 %collective-permute-done.5.last_v = f32[2,128]{1,0:T(2,128)S(1)} collective-permute-done((f32[2,128]{1,0:T(2,128)S(1)}, f32[2,128]{1,0:T(2,128)S(1)}, u32[]{:S(2)}, u32[]{:S(2)}) %collective-permute-start.5) | collective-permute-done | bytes 1056 | tf_op jit(solution)/shard_map/ppermute | solution.py:158
  24.2 2.6 collective-permute-start.4
  26.9 2.3 collective-permute-done.3.near_v
  36.1 14.3 %all-to-all-start = ((bf16[64,16,128]{2,1,0:T(8,128)(2,1)}), bf16[64,16,128]{2,1,0:T(8,128)(2,1)}, u32[]{:S(2)}, u32[]{:S(2)}) async-start(bf16[64,16,128]{2,1,0:T(8,128)(2,1)} %bitcast.52), calls=%async_computation | async-start | bytes 524288 | tf_op jit(solution)/shard_map/all_to_all | solution.py:181
  54.4 9.0 %all-to-all-done = bf16[64,16,128]{2,1,0:T(8,128)(2,1)} async-done(((bf16[64,16,128]{2,1,0:T(8,128)(2,1)}), bf16[64,16,128]{2,1,0:T(8,128)(2,1)}, u32[]{:S(2)}, u32[]{:S(2)}) %all-to-all-start) | async-done | bytes 262176 | tf_op jit(solution)/shard_map/all_to_all | solution.py:181
  63.5 38.8 %all_to_all.50 = bf16[256,16,128]{2,1,0:T(8,128)(2,1)S(1)} all-to-all(bf16[256,16,128]{2,1,0:T(8,128)(2,1)} %bitcast.40), channel_id=1, replica_groups=mesh['segment'=4,'seq'=64] {'segment','seq'}, dimensions={0} | all-to-all | bytes 2097152 | tf_op jit(solution)/shard_map/all_to_all | solution.py:165
  102.3 1.6 copy-done.4
  106.2 6.1 %all-to-all-start.2 = ((bf16[64,32,128]{2,1,0:T(8,128)(2,1)}), bf16[64,32,128]{2,1,0:T(8,128)(2,1)}, u32[]{:S(2)}, u32[]{:S(2)}) async-start(bf16[64,32,128]{2,1,0:T(8,128)(2,1)} %copy-done.11), calls=%async_computation.2 | async-start | bytes 1048576 | tf_op jit(solution)/shard_map/all_to_all | solution.py:185
  112.3 17.6 %all-to-all-done.2.received = bf16[64,32,128]{2,1,0:T(8,128)(2,1)} async-done(((bf16[64,32,128]{2,1,0:T(8,128)(2,1)}), bf16[64,32,128]{2,1,0:T(8,128)(2,1)}, u32[]{:S(2)}, u32[]{:S(2)}) %all-to-all-start.2) | async-done | bytes 524320 | tf_op jit(solution)/shard_map/all_to_all | solution.py:185
  129.9 1.6 copy-done.1
  131.5 2.4 shard_map.80
  133.9 18.7 %all_to_all.51 = bf16[64,16,128]{2,1,0:T(8,128)(2,1)S(1)} all-to-all(bf16[64,16,128]{2,1,0:T(8,128)(2,1)S(1)} %bitcast.53), channel_id=1, replica_groups=mesh['segment'=4,'seq'=64] {'seq'}, dimensions={0} | all-to-all | bytes 524288 | tf_op jit(solution)/shard_map/all_to_all | solution.py:181
  153.1 22.4 %all_to_all.52.received = bf16[64,32,128]{2,1,0:T(8,128)(2,1)S(1)} all-to-all(bf16[64,32,128]{2,1,0:T(8,128)(2,1)S(1)} %shard_map.81), channel_id=1, replica_groups=mesh['segment'=4,'seq'=64] {'seq'}, dimensions={0} | all-to-all | bytes 1048576 | tf_op jit(solution)/shard_map/all_to_all | solution.py:185
  176.7 18.7 %all_to_all.53 = bf16[64,16,128]{2,1,0:T(8,128)(2,1)S(1)} all-to-all(bf16[64,16,128]{2,1,0:T(8,128)(2,1)S(1)} %bitcast.54), channel_id=1, replica_groups=mesh['segment'=4,'seq'=64] {'seq'}, dimensions={0} | all-to-all | bytes 524288 | tf_op jit(solution)/shard_map/all_to_all | solution.py:181
  195.9 22.2 %all_to_all.54.received = bf16[64,32,128]{2,1,0:T(8,128)(2,1)S(1)} all-to-all(bf16[64,32,128]{2,1,0:T(8,128)(2,1)S(1)} %shard_map.83), channel_id=1, replica_groups=mesh['segment'=4,'seq'=64] {'seq'}, dimensions={0} | all-to-all | bytes 1048576 | tf_op jit(solution)/shard_map/all_to_all | solution.py:185
  219.4 18.7 %all_to_all.55 = bf16[64,16,128]{2,1,0:T(8,128)(2,1)S(1)} all-to-all(bf16[64,16,128]{2,1,0:T(8,128)(2,1)S(1)} %bitcast.55), channel_id=1, replica_groups=mesh['segment'=4,'seq'=64] {'seq'}, dimensions={0} | all-to-all | bytes 524288 | tf_op jit(solution)/shard_map/all_to_all | solution.py:181
  238.1 1.7 shard_map.88
  241.2 1.6 copy-done.6
  243.3 22.4 %all_to_all.56.received = bf16[64,32,128]{2,1,0:T(8,128)(2,1)S(1)} all-to-all(bf16[64,32,128]{2,1,0:T(8,128)(2,1)S(1)} %shard_map.85), channel_id=1, replica_groups=mesh['segment'=4,'seq'=64] {'seq'}, dimensions={0} | all-to-all | bytes 1048576 | tf_op jit(solution)/shard_map/all_to_all | solution.py:185
  266.8 17.2 %all_to_all.57 = bf16[4,1024,128]{2,1,0:T(8,128)(2,1)S(1)} all-to-all(bf16[4,1024,128]{2,1,0:T(8,128)(2,1)S(1)} %pad_maximum_fusion), channel_id=1, replica_groups=mesh['segment'=4,'seq'=64] {'segment'}, dimensions={0} | all-to-all | bytes 2097152 | tf_op jit(solution)/shard_map/all_to_all | solution.py:199
  285.3 2.1 convert_element_type.3
  (83 shorter events, 23.0 us)
Async XLA Ops:
  7.2 19.7 %copy-start = (bf16[1024,512]{1,0:T(8,128)(2,1)S(1)}, bf16[1024,512]{1,0:T(8,128)(2,1)}, u32[]{:S(2)}) copy-start(bf16[1024,512]{1,0:T(8,128)(2,1)} %param.11) | copy-start | bytes 3145732
  7.2 7.5 %copy-start.27 = (f32[1,512]{1,0:T(1,128)S(1)}, f32[1,512]{1,0:T(1,128)}, u32[]{:S(2)}) copy-start(f32[1,512]{1,0:T(1,128)} %param.10) | copy-start | bytes 6148
  7.2 7.5 %copy-start.26 = (f32[1,512]{1,0:T(1,128)S(1)}, f32[1,512]{1,0:T(1,128)}, u32[]{:S(2)}) copy-start(f32[1,512]{1,0:T(1,128)} %param.9) | copy-start | bytes 6148
  7.2 95.1 %all-gather.3.cloned.1.call-start = ((), (), s32[]{:S(2)}) async-start(), calls=%async_computation.11 | async-start | bytes 2621440 | tf_op jit(solution)/shard_map/all_gather | solution.py:147
  8.0 43.2 %copy-start.8 = (bf16[1,1024,512]{2,1,0:T(8,128)(2,1)S(1)}, bf16[1,1024,512]{2,1,0:T(8,128)(2,1)}, u32[]{:S(2)}) copy-start(bf16[1,1024,512]{2,1,0:T(8,128)(2,1)} %param.6) | copy-start | bytes 3145732
  10.2 18.9 %collective-permute-start.2 = (bf16[1024,128]{1,0:T(8,128)(2,1)}, bf16[1024,128]{1,0:T(8,128)(2,1)S(1)}, u32[]{:S(2)}, u32[]{:S(2)}) collective-permute-start(bf16[1024,128]{1,0:T(8,128)(2,1)} %get-tuple-element.24), channel_id=1, source_target_pairs={{0,192},{64,0},{128,64},{192,128},{1,193},{65,1},{129,65},{193,129... | collective-permute-start | bytes 786440 | tf_op jit(solution)/shard_map/ppermute | solution.py:157
  13.5 16.3 %collective-permute-start.1 = (bf16[1024,128]{1,0:T(8,128)(2,1)}, bf16[1024,128]{1,0:T(8,128)(2,1)S(1)}, u32[]{:S(2)}, u32[]{:S(2)}) collective-permute-start(bf16[1024,128]{1,0:T(8,128)(2,1)} %get-tuple-element.25), channel_id=1, source_target_pairs={{0,128},{64,192},{128,0},{192,64},{1,129},{65,193},{129,1},{193,65... | collective-permute-start | bytes 786440 | tf_op jit(solution)/shard_map/ppermute | solution.py:157
  14.1 16.5 %collective-permute-start = (bf16[1024,128]{1,0:T(8,128)(2,1)S(1)}, bf16[1024,128]{1,0:T(8,128)(2,1)S(1)}, u32[]{:S(2)}, u32[]{:S(2)}) collective-permute-start(bf16[1024,128]{1,0:T(8,128)(2,1)S(1)} %get-tuple-element.26), channel_id=1, source_target_pairs={{0,64},{64,128},{128,192},{192,0},{1,65},{65,129},{129,193},{193,1... | collective-permute-start | bytes 786440 | tf_op jit(solution)/shard_map/ppermute | solution.py:157
  14.8 9.5 %collective-permute-start.5 = (f32[2,128]{1,0:T(2,128)S(1)}, f32[2,128]{1,0:T(2,128)S(1)}, u32[]{:S(2)}, u32[]{:S(2)}) collective-permute-start(f32[2,128]{1,0:T(2,128)S(1)} %get-tuple-element.28), channel_id=1, source_target_pairs={{0,192},{64,0},{128,64},{192,128},{1,193},{65,1},{129,65},{193,129... | collective-permute-start | bytes 3080 | tf_op jit(solution)/shard_map/ppermute | solution.py:158
  16.9 12.3 %collective-permute-start.3 = (f32[2,128]{1,0:T(2,128)S(1)}, f32[2,128]{1,0:T(2,128)S(1)}, u32[]{:S(2)}, u32[]{:S(2)}) collective-permute-start(f32[2,128]{1,0:T(2,128)S(1)} %get-tuple-element.30), channel_id=1, source_target_pairs={{0,64},{64,128},{128,192},{192,0},{1,65},{65,129},{129,193},{193,1... | collective-permute-start | bytes 3080 | tf_op jit(solution)/shard_map/ppermute | solution.py:158
  24.2 4.9 %collective-permute-start.4 = (f32[2,128]{1,0:T(2,128)S(1)}, f32[2,128]{1,0:T(2,128)S(1)}, u32[]{:S(2)}, u32[]{:S(2)}) collective-permute-start(f32[2,128]{1,0:T(2,128)S(1)} %get-tuple-element.31), channel_id=1, source_target_pairs={{0,128},{64,192},{128,0},{192,64},{1,129},{65,193},{129,1},{193,65... | collective-permute-start | bytes 3080 | tf_op jit(solution)/shard_map/ppermute | solution.py:158
  36.1 27.4 %all-to-all-start = ((bf16[64,16,128]{2,1,0:T(8,128)(2,1)}), bf16[64,16,128]{2,1,0:T(8,128)(2,1)}, u32[]{:S(2)}, u32[]{:S(2)}) async-start(bf16[64,16,128]{2,1,0:T(8,128)(2,1)} %bitcast.52), calls=%async_computation | async-start | bytes 524288 | tf_op jit(solution)/shard_map/all_to_all | solution.py:181
  50.4 61.9 %all-gather.5.cloned.1.call-start = ((), (), s32[]{:S(2)}) async-start(), calls=%async_computation.12 | async-start | bytes 2621440 | tf_op jit(solution)/shard_map/all_gather | solution.py:148
  102.3 1.6 copy-start.4
  106.2 23.7 %all-to-all-start.2 = ((bf16[64,32,128]{2,1,0:T(8,128)(2,1)}), bf16[64,32,128]{2,1,0:T(8,128)(2,1)}, u32[]{:S(2)}, u32[]{:S(2)}) async-start(bf16[64,32,128]{2,1,0:T(8,128)(2,1)} %copy-done.11), calls=%async_computation.2 | async-start | bytes 1048576 | tf_op jit(solution)/shard_map/all_to_all | solution.py:185
  112.3 173.0 %reduce-scatter.2.cloned.1.call-start = ((), (), s32[]{:S(2)}) async-start(), calls=%async_computation.13 | async-start | bytes 2621440 | tf_op jit(solution)/shard_map/reduce_scatter | solution.py:198
  131.5 21.1 %copy-start.5 = (bf16[4,4,256,256]{3,2,1,0:T(8,128)(2,1)S(1)}, bf16[4,4,256,256]{3,2,1,0:T(8,128)(2,1)}, u32[]{:S(2)}) copy-start(bf16[4,4,256,256]{3,2,1,0:T(8,128)(2,1)} %all-gather.3.cloned.1.call-done.seconds) | copy-start | bytes 6291460
  133.9 41.6 %copy-start.13 = (bf16[1024,128]{1,0:T(8,128)(2,1)}, bf16[1024,128]{1,0:T(8,128)(2,1)S(1)}, u32[]{:S(2)}) copy-start(bf16[1024,128]{1,0:T(8,128)(2,1)S(1)} %get-tuple-element.15.upstream) | copy-start | bytes 786436
  152.6 22.9 %copy-start.2 = (bf16[4,4,256,256]{3,2,1,0:T(8,128)(2,1)S(1)}, bf16[4,4,256,256]{3,2,1,0:T(8,128)(2,1)}, u32[]{:S(2)}) copy-start(bf16[4,4,256,256]{3,2,1,0:T(8,128)(2,1)} %all-gather.5.cloned.1.call-done.firsts) | copy-start | bytes 6291460
  176.7 41.5 %copy-start.15 = (bf16[1024,128]{1,0:T(8,128)(2,1)}, bf16[1024,128]{1,0:T(8,128)(2,1)S(1)}, u32[]{:S(2)}) copy-start(bf16[1024,128]{1,0:T(8,128)(2,1)S(1)} %get-tuple-element.17.upstream) | copy-start | bytes 786436
  219.4 18.7 %copy-start.17 = (bf16[1024,128]{1,0:T(8,128)(2,1)}, bf16[1024,128]{1,0:T(8,128)(2,1)S(1)}, u32[]{:S(2)}) copy-start(bf16[1024,128]{1,0:T(8,128)(2,1)S(1)} %get-tuple-element.19.upstream) | copy-start | bytes 786436
  241.2 1.6 copy-start.6
  242.8 22.9 %copy-start.3 = (bf16[4,4,256,256]{3,2,1,0:T(8,128)(2,1)S(1)}, bf16[4,4,256,256]{3,2,1,0:T(8,128)(2,1)}, u32[]{:S(2)}) copy-start(bf16[4,4,256,256]{3,2,1,0:T(8,128)(2,1)} %all-gather.5.cloned.1.call-done.firsts) | copy-start | bytes 6291460
  242.8 22.9 %copy-start.18 = (bf16[1024,128]{1,0:T(8,128)(2,1)S(1)}, bf16[1024,128]{1,0:T(8,128)(2,1)}, u32[]{:S(2)}) copy-start(bf16[1024,128]{1,0:T(8,128)(2,1)} %copy-done.17) | copy-start | bytes 786436
  (15 other events, 14.4 us)
Sparse Core Ops, SparseCore 0:
  9.8 37.1 all-gather.2
  53.1 45.5 all-gather.4
  241.3 25.7 reduce-scatter.1
where the time goes:
time: 295 us; the launch traced here: 294 us
  blocking collectives  179 us (61%)
  waiting for transfers between devices  37.6 us (13%)
  starting transfers between devices  29.6 us (10%)
  local copies, waits for them, and re-layouts  18.1 us (6%)
  between operations  14.1 us (5%)
  Pallas kernels  13.1 us (4%)
    all_to_all x3, blocking collectives, body(): received = lax.all_to_all(payload, 'seq', 0, 0, tiled=True)  67 us
    all_to_all x3, blocking collectives, body(): lax.all_to_all(sends.reshape(64, 16, 128), 'seq', 0, 0, tiled=True)  56 us
    all_to_all x1, blocking collectives, body(): lax.all_to_all(firsts_out.reshape(256, 16, 128), ('segment', 'seq'), 0, 0...  38.8 us
    all_to_all x1, waiting for transfers between devices, body(): received = lax.all_to_all(payload, 'seq', 0, 0, tiled=True)  17.6 us
    all_to_all x1, blocking collectives, body(): back = lax.all_to_all(jnp.stack(results), 'segment', 0, 0, tiled=True)  17.2 us
    unnamed x56, local copies, waits for them, and re-layouts  15.8 us
    all_to_all x1, starting transfers between devices, body(): lax.all_to_all(sends.reshape(64, 16, 128), 'seq', 0, 0, tiled=True)  14.3 us
    ppermute x3, waiting for transfers between devices, body(): vector = lax.ppermute(vector, 'segment', ring)  9.62 us
  transfers between devices with their start and end apart: 11, of which 4 were waited for; matrix products, arithmetic and copies ran while one was open for 1% of the time, Pallas kernels for 2%

commit v1 on v0

v1 whole, which is shorter than its diff:
```python
import functools

import jax
import jax.numpy as jnp
from jax import lax
from jax.experimental import pallas as pl
from jax.experimental.pallas import tpu as pltpu
from jax.sharding import PartitionSpec as P

BF = jnp.bfloat16
F32 = jnp.float32
VMEM_LIMIT = 6 * 1024 * 1024
LARGE_LIMIT = 58 * 1024 * 1024


def dot(a, b):
    return lax.dot_general(a, b, (((1,), (0,)), ((), ())), preferred_element_type=F32)


def dot_first(a, b):
    return lax.dot_general(a, b, (((0,), (0,)), ((), ())), preferred_element_type=F32)


def dot_last(a, b):
    return lax.dot_general(a, b, (((1,), (1,)), ((), ())), preferred_element_type=F32)


def spread(block, chunks, row):
    for col in range(4):
        chunks[pl.ds(row * 4 + col, 64, stride=16), :] = block[pl.ds(col, 64, stride=4), :]


def collect(chunks, block, row):
    for col in range(4):
        block[pl.ds(col, 64, stride=4), :] = chunks[pl.ds(row * 4 + col, 64, stride=16), :]


def first_kernel(firsts, inputs, scale, shift, tops, out, upstream, block, chunks, vectors, both, weights, held, sems):
    lanes = pl.ds(pl.multiple_of(lax.axis_index("segment") * 128, 128), 128)
    copies = []
    for row in range(4):
        copies.append(pltpu.make_async_copy(firsts.at[row], weights.at[row], sems.at[2 * row]))
        copies.append(pltpu.make_async_copy(inputs.at[row], held.at[row], sems.at[2 * row + 1]))
    copies.append(pltpu.make_async_copy(scale, both.at[0:1, :], sems.at[8]))
    copies.append(pltpu.make_async_copy(shift, both.at[1:2, :], sems.at[9]))
    copies.append(pltpu.make_async_copy(tops.at[:, lanes], upstream, sems.at[10]))
    for copy in copies:
        copy.start()
    for copy in copies:
        copy.wait()
    vectors[...] = jnp.zeros_like(vectors)
    for part in range(4):
        lanes = slice(part * 128, (part + 1) * 128)
        for row in range(4):
            out[part, row * 256:(row + 1) * 256, :] = held[row, :, lanes]
            block[...] = dot(weights[row], held[row, :, lanes])
            spread(block, chunks, row)
        out[part, 1024:2048, :] = chunks[...].astype(BF)
        for place in range(2):
            left = both[place:place + 1, lanes]
            for term in range(3):
                piece = left.astype(BF).astype(F32)
                vectors[place * 3 + term:place * 3 + term + 1, :] = piece
                left = left - piece
        out[part, 2048:, :] = vectors[...].astype(BF)


def gated(held, vectors, layer, rows):
    scale, shift = vectors[layer, 0:1, :], vectors[layer, 1:2, :]
    return jax.nn.sigmoid(held[layer, rows, :].astype(F32) * scale + shift), scale


def gate_kernel(upstream, held, out, vectors, block, chunks):
    for layer in range(4):
        terms = held[layer, 2048:, :].astype(F32)
        vectors[layer, 0:1, :] = terms[0:1, :] + (terms[1:2, :] + terms[2:3, :])
        vectors[layer, 1:2, :] = terms[3:4, :] + (terms[4:5, :] + terms[5:6, :])
    for row in range(4):
        rows = slice(row * 256, (row + 1) * 256)
        gate, _ = gated(held, vectors, 3, rows)
        block[...] = upstream[rows, :].astype(F32) * gate
        spread(block, chunks, row)
    out[:, 0] = chunks[...].astype(BF).reshape(64, 16, 128)
    for place, layer in ((1, 3), (2, 2), (3, 1)):
        out[:, place] = held[layer, 1024:2048, :].reshape(64, 16, 128)


def column_kernel(layer, seconds, received, out, wide, result):
    for place, owner in enumerate(MIXED[layer]):
        wide[...] = received[:, place].reshape(1024, 128).astype(F32)
        for col in range(4):
            rows = pl.ds(col, 256, stride=4)
            times = dot_first if place == 0 else dot
            result[rows, :] = times(seconds[owner, col], wide[rows, :].astype(BF))
        out[:, place] = result[...].astype(BF).reshape(64, 16, 128)


def second_kernel(zero, one, two, three, out, grads, firsts_out):
    firsts = ((zero, 1), (three, 3), (three, 2), (three, 1))
    for layer, received in enumerate((zero, one, two, three)):
        source, place = firsts[layer]
        grads[...] = received[:, 0].reshape(1024, 128).astype(F32)
        firsts_out[...] = source[:, place].reshape(1024, 128).astype(F32)
        for col in range(4):
            rows = pl.ds(col, 256, stride=4)
            out[layer, col] = dot_last(
                grads[rows, :].astype(BF), firsts_out[rows, :].astype(BF)
            ).astype(BF)


def row_kernel(layer, received, mixed, firsts, upstream, held, vectors, *rest):
    if layer == 0:
        out, chunks, mixed_chunks, block, mixed_block = rest
    else:
        out, next_out, chunks, mixed_chunks, block, mixed_block, next_chunks = rest
    place = (1, 3, 2, 1)[layer]
    chunks[...] = received[:, 0].reshape(1024, 128).astype(F32)
    mixed_chunks[...] = mixed[:, place].reshape(1024, 128).astype(F32)
    for row in range(4):
        rows = slice(row * 256, (row + 1) * 256)
        collect(chunks, block, row)
        collect(mixed_chunks, mixed_block, row)
        through = dot_first(firsts[layer, row], block[...].astype(BF))
        up = upstream[rows, :].astype(F32)
        gate, scale = gated(held, vectors, layer, rows)
        slope = (up * gate * (1.0 - gate)).astype(BF).astype(F32)
        gate_grad = (slope * mixed_block[...]).astype(BF).astype(F32)
        result = (up + through + gate_grad * scale).astype(BF)
        out[rows, :] = result
        if layer > 0:
            gate, _ = gated(held, vectors, layer - 1, rows)
            block[...] = result.astype(F32) * gate
            spread(block, next_chunks, row)
    if layer > 0:
        next_out[:, 0] = next_chunks[...].astype(BF).reshape(64, 16, 128)
        if layer == 1:
            next_out[:, 1] = held[0, 1024:2048, :].reshape(64, 16, 128)


def end_kernel(zero, one, two, three, *outs):
    index = lax.axis_index("segment")
    for step, out in enumerate(outs):
        for layer, value in enumerate((zero, one, two, three)):
            @pl.when((index + step) % 4 == layer)
            def _():
                out[...] = value[...]


def final_kernel(own, near, far, last, out):
    index = lax.axis_index("segment")
    for step, value in enumerate((own, near, far, last)):
        lanes = pl.ds(pl.multiple_of(((index + 4 - step) % 4) * 128, 128), 128)
        out[:, lanes] = value[...]


IN_VMEM = pl.BlockSpec(memory_space=pltpu.VMEM)


IN_HBM = pl.BlockSpec(memory_space=pltpu.HBM)


def call(kernel, count, out_shapes, scratch, flops, fetched=0, copies=0, grant=VMEM_LIMIT):
    outs = [jax.ShapeDtypeStruct(s, d) for s, d in out_shapes]
    single = len(outs) == 1
    return pl.pallas_call(
        kernel,
        in_specs=[IN_VMEM] * (count - fetched) + [IN_HBM] * fetched,
        out_shape=outs[0] if single else outs,
        out_specs=IN_VMEM if single else [IN_VMEM] * len(outs),
        scratch_shapes=[pltpu.VMEM(*s) if isinstance(s[0], tuple) else pltpu.VMEM(s, F32) for s in scratch]
        + ([pltpu.SemaphoreType.DMA((copies,))] if copies else []),
        compiler_params=pltpu.CompilerParams(vmem_limit_bytes=grant),
        cost_estimate=pl.CostEstimate(flops=flops, bytes_accessed=2 << 20, transcendentals=0),
    )


TALL = (1024, 128)
MIXED = {3: (3, 3, 2, 1), 2: (2,), 1: (1,), 0: (0, 0)}
BLOCK = (256, 128)
FLOPS = 2 * 4 * 256 * 256 * 128


def body(layer_inputs, first_blocks, second_blocks, gate_scale, gate_shift, top_grads):
    payload, upstream = call(
        first_kernel,
        5,
        [((4, 2064, 128), BF), (TALL, BF)],
        [BLOCK, TALL, (16, 128), (2, 512), ((4, 256, 256), BF), ((4, 256, 512), BF)],
        4 * FLOPS,
        fetched=5,
        copies=11,
        grant=LARGE_LIMIT,
    )(first_blocks[0], layer_inputs[0].reshape(4, 256, 512), gate_scale, gate_shift, top_grads)
    held = lax.all_to_all(payload, "segment", 0, 0, tiled=True)
    held, first_blocks, second_blocks = lax.optimization_barrier((held, first_blocks, second_blocks))
    seconds_all = lax.all_gather(second_blocks, "segment", tiled=True)
    firsts_all = lax.all_gather(first_blocks, "segment", tiled=True)
    sends, vectors = call(
        gate_kernel, 2, [((64, 4, 16, 128), BF), ((4, 2, 128), F32)], [BLOCK, TALL], 1 << 20
    )(upstream, held)

    results, columns = [None] * 4, [None] * 4
    for l in (3, 2, 1, 0):
        places = len(MIXED[l])
        columns[l] = lax.all_to_all(sends, "seq", 0, 0, tiled=True)
        payload = call(
            functools.partial(column_kernel, l),
            2,
            [((64, places, 16, 128), BF)],
            [TALL] * 2,
            places * FLOPS,
        )(seconds_all, columns[l])
        if l == 0:
            partials = call(
                second_kernel, 4, [((4, 4, 256, 256), BF)], [TALL, TALL], 4 * FLOPS
            )(*columns)
            payload, partials = lax.optimization_barrier((payload, partials))
        received = lax.all_to_all(payload, "seq", 0, 0, tiled=True)
        if places > 1:
            mixed = received
        outs, scratch = [(TALL, BF)], [TALL, TALL, BLOCK, BLOCK]
        if l > 0:
            outs, scratch = outs + [((64, len(MIXED[l - 1]), 16, 128), BF)], scratch + [TALL]
        made = call(functools.partial(row_kernel, l), 6, outs, scratch, FLOPS)(
            received, mixed, firsts_all, upstream, held, vectors
        )
        upstream, sends = (made, None) if l == 0 else made
        results[l] = upstream

    second = lax.psum_scatter(partials, "segment", scatter_dimension=0, tiled=True).astype(F32)
    back = list(call(end_kernel, 4, [(TALL, BF)] * 4, [], 1 << 20)(*results))
    for step in (1, 2, 3):
        back[step] = lax.ppermute(back[step], "segment", [(i, (i + step) % 4) for i in range(4)])
    back, second = lax.optimization_barrier((back, second))
    grads_out = call(final_kernel, 4, [((1024, 512), BF)], [], 1 << 20)(*back)
    return grads_out[None], second


def solution(mesh):
    placed = (
        P("segment", "seq", None),
        P("segment", "seq", None, None),
        P("segment", "seq", None, None),
        P("segment", None),
        P("segment", None),
        P("seq", None),
    )
    return jax.shard_map(
        body,
        mesh=mesh,
        in_specs=placed,
        out_specs=(P("segment", "seq", None), P("segment", "seq", None, None)),
        check_vma=False,
    )
```

time: 295 us -> 277 us (0.939)
  blocking collectives: 179 us -> 148 us
  waiting for transfers between devices: 37.6 us -> 65.6 us
  local copies, waits for them, and re-layouts: 18.1 us -> 8.7 us
  starting transfers between devices: 29.6 us -> 24.1 us
    all_to_all x5 -> x4, blocking collectives: 112 us -> 89.1 us  [the longest x3 59.6 us: body(): columns[l] = lax.all_to_all(sends, 'seq', 0, 0, tiled=True)]
    all_to_all x1, waiting for transfers between devices: 9.05 us -> 27.2 us  [body(): columns[l] = lax.all_to_all(sends, 'seq', 0, 0, tiled=True)]
    all_gather x1, waiting for transfers between devices: 0.02 us -> 17.9 us  [body(): firsts_all = lax.all_gather(first_blocks, 'segment', tiled=True)]
    all_to_all x3, blocking collectives: 67 us -> 58.7 us  [body(): received = lax.all_to_all(payload, 'seq', 0, 0, tiled=True)]
    all_to_all x1, waiting for transfers between devices: 17.6 us -> 10.1 us  [body(): received = lax.all_to_all(payload, 'seq', 0, 0, tiled=True)]
    unnamed x56 -> x34, local copies, waits for them, and re-layouts: 15.8 us -> 8.7 us
    ppermute x6 -> x3, starting transfers between devices: 9.15 us -> 2.97 us  [body(): lax.ppermute(back[step], 'segment', [(i, (i + step) % 4) for i in range(4)])]
    pallas_call x12 -> x13, Pallas kernels: 13.1 us -> 13.5 us  [the longest x4 4.51 us: body(): call(functools.partial(row_kernel, l), 6, outs, scratch, FLOPS)]
  transfers between devices with their start and end apart: 11 -> 8, of which waited for: 4 -> 6; matrix products, arithmetic and copies ran while one was open for 1% -> 1% of each run, Pallas kernels for 2% -> 1%
where the time goes in v1:
time: 277 us; the launch traced here: 276 us
  blocking collectives  148 us (53%)
  waiting for transfers between devices  65.6 us (24%)
  starting transfers between devices  24.1 us (9%)
  between operations  14 us (5%)
  Pallas kernels  13.5 us (5%)
  local copies, waits for them, and re-layouts  8.7 us (3%)
    all_to_all x3, blocking collectives, body(): columns[l] = lax.all_to_all(sends, 'seq', 0, 0, tiled=True)  59.6 us
    all_to_all x3, blocking collectives, body(): received = lax.all_to_all(payload, 'seq', 0, 0, tiled=True)  58.7 us
    all_to_all x1, blocking collectives, body(): held = lax.all_to_all(payload, 'segment', 0, 0, tiled=True)  29.5 us
    all_to_all x1, waiting for transfers between devices, body(): columns[l] = lax.all_to_all(sends, 'seq', 0, 0, tiled=True)  27.2 us
    all_gather x1, waiting for transfers between devices, body(): firsts_all = lax.all_gather(first_blocks, 'segment', tiled=True)  17.9 us
    all_to_all x1, starting transfers between devices, body(): columns[l] = lax.all_to_all(sends, 'seq', 0, 0, tiled=True)  14.6 us
    all_to_all x1, waiting for transfers between devices, body(): received = lax.all_to_all(payload, 'seq', 0, 0, tiled=True)  10.1 us
    ppermute x3, waiting for transfers between devices, body(): lax.ppermute(back[step], 'segment', [(i, (i + step) % 4) for i in range(4)])  9.7 us
  transfers between devices with their start and end apart: 8, of which 6 were waited for; matrix products, arithmetic and copies ran while one was open for 1% of the time, Pallas kernels for 1%

profile of v1, /device:TPU:1, one launch (start us, length us, event | category | flops | bytes accessed | tf_op | source)
XLA Modules:
  0.0 275.9 jit_solution(13799980375294006612)
XLA Ops:
  7.2 4.4 %shard_map.77 = (bf16[4,2064,128]{2,1,0:T(8,128)(2,1)}, bf16[1024,128]{1,0:T(8,128)(2,1)}) custom-call(bf16[4,256,256]{2,1,0:T(8,128)(2,1)} %bitcast.3, bf16[4,256,512]{2,1,0:T(8,128)(2,1)} %bitcast.4, f32[1,512]{1,0:T(1,128)} %scale.1, f32[1,512]{1,0:T(1,128)} %shift.1, bf16[1024,512]{1,0:T(8,128)(2,1)} %tops.1), custom_call_target="tpu_custom_call" | custom-call | flops 268435456 | bytes 2097152 | tf_op jit(solution)/shard_map/pallas_call | solution.py:184
  11.6 29.5 %all_to_all.45.held = bf16[4,2064,128]{2,1,0:T(8,128)(2,1)S(1)} all-to-all(bf16[4,2064,128]{2,1,0:T(8,128)(2,1)} %get-tuple-element.26), channel_id=1, replica_groups=mesh['segment'=4,'seq'=64] {'segment'}, dimensions={0} | all-to-all | bytes 4227072 | tf_op jit(solution)/shard_map/all_to_all | solution.py:194
  42.5 14.6 %all-to-all-start.1 = ((bf16[64,4,16,128]{3,2,1,0:T(8,128)(2,1)}), bf16[64,4,16,128]{3,2,1,0:T(8,128)(2,1)S(1)}, u32[]{:S(2)}, u32[]{:S(2)}) async-start(bf16[64,4,16,128]{3,2,1,0:T(8,128)(2,1)} %copy-done.10), calls=%async_computation.1 | async-start | bytes 2097152 | tf_op jit(solution)/shard_map/all_to_all | solution.py:205
  57.8 27.2 %all-to-all-done.1.received.three = bf16[64,4,16,128]{3,2,1,0:T(8,128)(2,1)S(1)} async-done(((bf16[64,4,16,128]{3,2,1,0:T(8,128)(2,1)}), bf16[64,4,16,128]{3,2,1,0:T(8,128)(2,1)S(1)}, u32[]{:S(2)}, u32[]{:S(2)}) %all-to-all-start.1) | async-done | bytes 1048608 | tf_op jit(solution)/shard_map/all_to_all | solution.py:205
  85.1 2.0 copy-done
  88.9 6.5 %all-to-all-start.2 = ((bf16[64,4,16,128]{3,2,1,0:T(8,128)(2,1)}), bf16[64,4,16,128]{3,2,1,0:T(8,128)(2,1)S(1)}, u32[]{:S(2)}, u32[]{:S(2)}) async-start(bf16[64,4,16,128]{3,2,1,0:T(8,128)(2,1)} %copy-done.8), calls=%async_computation.2 | async-start | bytes 2097152 | tf_op jit(solution)/shard_map/all_to_all | solution.py:218
  95.5 17.9 %all-gather.5.cloned.1.call-done.firsts = bf16[4,4,256,256]{3,2,1,0:T(8,128)(2,1)} async-done(((bf16[1,4,256,256]{3,2,1,0:T(8,128)(2,1)}), bf16[4,4,256,256]{3,2,1,0:T(8,128)(2,1)}) %all-gather.5.cloned.1.call-update) | async-done | bytes 2097168 | tf_op jit(solution)/shard_map/all_gather | solution.py:197
  113.3 10.1 %all-to-all-done.2.received.mixed = bf16[64,4,16,128]{3,2,1,0:T(8,128)(2,1)S(1)} async-done(((bf16[64,4,16,128]{3,2,1,0:T(8,128)(2,1)}), bf16[64,4,16,128]{3,2,1,0:T(8,128)(2,1)S(1)}, u32[]{:S(2)}, u32[]{:S(2)}) %all-to-all-start.2) | async-done | bytes 1048608 | tf_op jit(solution)/shard_map/all_to_all | solution.py:218
  123.4 1.6 copy-done.2
  125.0 1.2 shard_map.80
  126.2 19.6 %all_to_all.46.received.two = bf16[64,1,16,128]{3,2,1,0:T(8,128)(2,1)S(1)} all-to-all(bf16[64,1,16,128]{3,2,1,0:T(8,128)(2,1)S(1)} %get-tuple-element.33), channel_id=1, replica_groups=mesh['segment'=4,'seq'=64] {'seq'}, dimensions={0} | all-to-all | bytes 524288 | tf_op jit(solution)/shard_map/all_to_all | solution.py:205
  146.2 17.7 %all_to_all.47.received = bf16[64,1,16,128]{3,2,1,0:T(8,128)(2,1)S(1)} all-to-all(bf16[64,1,16,128]{3,2,1,0:T(8,128)(2,1)S(1)} %shard_map.81), channel_id=1, replica_groups=mesh['segment'=4,'seq'=64] {'seq'}, dimensions={0} | all-to-all | bytes 524288 | tf_op jit(solution)/shard_map/all_to_all | solution.py:218
  163.9 1.2 shard_map.82
  165.1 17.7 %all_to_all.48.received.one = bf16[64,1,16,128]{3,2,1,0:T(8,128)(2,1)S(1)} all-to-all(bf16[64,1,16,128]{3,2,1,0:T(8,128)(2,1)S(1)} %get-tuple-element.35), channel_id=1, replica_groups=mesh['segment'=4,'seq'=64] {'seq'}, dimensions={0} | all-to-all | bytes 524288 | tf_op jit(solution)/shard_map/all_to_all | solution.py:205
  183.2 17.7 %all_to_all.49.received = bf16[64,1,16,128]{3,2,1,0:T(8,128)(2,1)S(1)} all-to-all(bf16[64,1,16,128]{3,2,1,0:T(8,128)(2,1)S(1)} %shard_map.83), channel_id=1, replica_groups=mesh['segment'=4,'seq'=64] {'seq'}, dimensions={0} | all-to-all | bytes 524288 | tf_op jit(solution)/shard_map/all_to_all | solution.py:218
  200.9 1.2 shard_map.84
  202.2 22.4 %all_to_all.50.received.zero = bf16[64,2,16,128]{3,2,1,0:T(8,128)(2,1)S(1)} all-to-all(bf16[64,2,16,128]{3,2,1,0:T(8,128)(2,1)S(1)} %get-tuple-element.37), channel_id=1, replica_groups=mesh['segment'=4,'seq'=64] {'seq'}, dimensions={0} | all-to-all | bytes 1048576 | tf_op jit(solution)/shard_map/all_to_all | solution.py:205
  225.9 1.3 copy-done.7
  227.2 23.4 %all_to_all.51.received.mixed = bf16[64,2,16,128]{3,2,1,0:T(8,128)(2,1)S(1)} all-to-all(bf16[64,2,16,128]{3,2,1,0:T(8,128)(2,1)S(1)} %shard_map.85), channel_id=1, replica_groups=mesh['segment'=4,'seq'=64] {'seq'}, dimensions={0} | all-to-all | bytes 1048576 | tf_op jit(solution)/shard_map/all_to_all | solution.py:218
  250.6 1.6 copy-done.4
  253.7 1.8 collective-permute-start.1
  256.4 2.1 convert_element_type.3
  258.5 4.4 %collective-permute-done.near = bf16[1024,128]{1,0:T(8,128)(2,1)S(1)} collective-permute-done((bf16[1024,128]{1,0:T(8,128)(2,1)S(1)}, bf16[1024,128]{1,0:T(8,128)(2,1)S(1)}, u32[]{:S(2)}, u32[]{:S(2)}) %collective-permute-start) | collective-permute-done | bytes 262176 | tf_op jit(solution)/shard_map/ppermute | solution.py:233
  262.9 4.3 %collective-permute-done.1.far = bf16[1024,128]{1,0:T(8,128)(2,1)S(1)} collective-permute-done((bf16[1024,128]{1,0:T(8,128)(2,1)S(1)}, bf16[1024,128]{1,0:T(8,128)(2,1)S(1)}, u32[]{:S(2)}, u32[]{:S(2)}) %collective-permute-start.1) | collective-permute-done | bytes 262176 | tf_op jit(solution)/shard_map/ppermute | solution.py:233
  (50 shorter events, 10.7 us)
Async XLA Ops:
  7.2 77.9 %all-gather.3.cloned.1.call-start = ((), (), s32[]{:S(2)}) async-start(), calls=%async_computation.10 | async-start | bytes 2621440 | tf_op jit(solution)/shard_map/all_gather | solution.py:196
  11.6 29.6 %copy-start.9 = (bf16[1024,128]{1,0:T(8,128)(2,1)S(1)}, bf16[1024,128]{1,0:T(8,128)(2,1)}, u32[]{:S(2)}) copy-start(bf16[1024,128]{1,0:T(8,128)(2,1)} %get-tuple-element.28.upstream) | copy-start | bytes 786436
  41.5 1.0 copy-start.10
  42.5 42.5 %all-to-all-start.1 = ((bf16[64,4,16,128]{3,2,1,0:T(8,128)(2,1)}), bf16[64,4,16,128]{3,2,1,0:T(8,128)(2,1)S(1)}, u32[]{:S(2)}, u32[]{:S(2)}) async-start(bf16[64,4,16,128]{3,2,1,0:T(8,128)(2,1)} %copy-done.10), calls=%async_computation.1 | async-start | bytes 2097152 | tf_op jit(solution)/shard_map/all_to_all | solution.py:205
  57.1 56.2 %all-gather.5.cloned.1.call-start = ((), (), s32[]{:S(2)}) async-start(), calls=%async_computation.11 | async-start | bytes 2621440 | tf_op jit(solution)/shard_map/all_gather | solution.py:197
  85.1 2.9 %copy-start.5 = (bf16[64,4,16,128]{3,2,1,0:T(8,128)(2,1)}, bf16[64,4,16,128]{3,2,1,0:T(8,128)(2,1)S(1)}, u32[]{:S(2)}) copy-start(bf16[64,4,16,128]{3,2,1,0:T(8,128)(2,1)S(1)} %all-to-all-done.1.received.three) | copy-start | bytes 3145732
  85.1 2.0 copy-start
  88.0 1.0 copy-start.8
  88.9 34.5 %all-to-all-start.2 = ((bf16[64,4,16,128]{3,2,1,0:T(8,128)(2,1)}), bf16[64,4,16,128]{3,2,1,0:T(8,128)(2,1)S(1)}, u32[]{:S(2)}, u32[]{:S(2)}) async-start(bf16[64,4,16,128]{3,2,1,0:T(8,128)(2,1)} %copy-done.8), calls=%async_computation.2 | async-start | bytes 2097152 | tf_op jit(solution)/shard_map/all_to_all | solution.py:218
  95.4 161.0 %reduce-scatter.2.cloned.1.call-start = ((), (), s32[]{:S(2)}) async-start(), calls=%async_computation.12 | async-start | bytes 2621440 | tf_op jit(solution)/shard_map/reduce_scatter | solution.py:230
  123.4 1.6 copy-start.2
  125.0 20.8 %copy-start.1 = (bf16[4,4,256,256]{3,2,1,0:T(8,128)(2,1)S(1)}, bf16[4,4,256,256]{3,2,1,0:T(8,128)(2,1)}, u32[]{:S(2)}) copy-start(bf16[4,4,256,256]{3,2,1,0:T(8,128)(2,1)} %all-gather.3.cloned.1.call-done.seconds) | copy-start | bytes 6291460
  126.2 38.9 %copy-start.11 = (bf16[1024,128]{1,0:T(8,128)(2,1)}, bf16[1024,128]{1,0:T(8,128)(2,1)S(1)}, u32[]{:S(2)}) copy-start(bf16[1024,128]{1,0:T(8,128)(2,1)S(1)} %get-tuple-element.34.upstream.three) | copy-start | bytes 786436
  126.2 37.6 %copy-start.3 = (bf16[4,4,256,256]{3,2,1,0:T(8,128)(2,1)S(1)}, bf16[4,4,256,256]{3,2,1,0:T(8,128)(2,1)}, u32[]{:S(2)}) copy-start(bf16[4,4,256,256]{3,2,1,0:T(8,128)(2,1)} %all-gather.5.cloned.1.call-done.firsts) | copy-start | bytes 6291460
  165.1 37.0 %copy-start.13 = (bf16[1024,128]{1,0:T(8,128)(2,1)}, bf16[1024,128]{1,0:T(8,128)(2,1)S(1)}, u32[]{:S(2)}) copy-start(bf16[1024,128]{1,0:T(8,128)(2,1)S(1)} %get-tuple-element.36.upstream.two) | copy-start | bytes 786436
  202.1 22.9 %copy-start.15 = (bf16[1024,128]{1,0:T(8,128)(2,1)}, bf16[1024,128]{1,0:T(8,128)(2,1)S(1)}, u32[]{:S(2)}) copy-start(bf16[1024,128]{1,0:T(8,128)(2,1)S(1)} %get-tuple-element.39.upstream.one) | copy-start | bytes 786436
  202.2 22.9 %copy-start.6 = (bf16[64,4,16,128]{3,2,1,0:T(8,128)(2,1)S(1)}, bf16[64,4,16,128]{3,2,1,0:T(8,128)(2,1)}, u32[]{:S(2)}) copy-start(bf16[64,4,16,128]{3,2,1,0:T(8,128)(2,1)} %copy-done.5) | copy-start | bytes 3145732
  225.9 1.3 copy-start.7
  227.2 23.4 %copy-start.16 = (bf16[1024,128]{1,0:T(8,128)(2,1)S(1)}, bf16[1024,128]{1,0:T(8,128)(2,1)}, u32[]{:S(2)}) copy-start(bf16[1024,128]{1,0:T(8,128)(2,1)} %copy-done.15) | copy-start | bytes 786436
  250.6 1.6 copy-start.4
  252.2 1.0 copy-start.14
  253.4 9.5 %collective-permute-start = (bf16[1024,128]{1,0:T(8,128)(2,1)S(1)}, bf16[1024,128]{1,0:T(8,128)(2,1)S(1)}, u32[]{:S(2)}, u32[]{:S(2)}) collective-permute-start(bf16[1024,128]{1,0:T(8,128)(2,1)S(1)} %get-tuple-element.41), channel_id=1, source_target_pairs={{0,64},{64,128},{128,192},{192,0},{1,65},{65,129},{129,193},{193,1... | collective-permute-start | bytes 786440 | tf_op jit(solution)/shard_map/ppermute | solution.py:233
  253.7 13.4 %collective-permute-start.1 = (bf16[1024,128]{1,0:T(8,128)(2,1)S(1)}, bf16[1024,128]{1,0:T(8,128)(2,1)S(1)}, u32[]{:S(2)}, u32[]{:S(2)}) collective-permute-start(bf16[1024,128]{1,0:T(8,128)(2,1)S(1)} %get-tuple-element.42), channel_id=1, source_target_pairs={{0,128},{64,192},{128,0},{192,64},{1,129},{65,193},{129,1},{193,65... | collective-permute-start | bytes 786440 | tf_op jit(solution)/shard_map/ppermute | solution.py:233
  255.5 12.7 %collective-permute-start.2 = (bf16[1024,128]{1,0:T(8,128)(2,1)S(1)}, bf16[1024,128]{1,0:T(8,128)(2,1)S(1)}, u32[]{:S(2)}, u32[]{:S(2)}) collective-permute-start(bf16[1024,128]{1,0:T(8,128)(2,1)S(1)} %get-tuple-element.43), channel_id=1, source_target_pairs={{0,192},{64,0},{128,64},{192,128},{1,193},{65,1},{129,65},{193,129... | collective-permute-start | bytes 786440 | tf_op jit(solution)/shard_map/ppermute | solution.py:233
  (1 other events, 1.0 us)
Sparse Core Ops, SparseCore 0:
  41.3 36.6 all-gather.2
  79.8 33.4 all-gather.4
  227.3 26.7 reduce-scatter.1

commit v2 on v1

v2 whole, which is shorter than its diff:
```python
import functools

import jax
import jax.numpy as jnp
from jax import lax
from jax.experimental import pallas as pl
from jax.experimental.pallas import tpu as pltpu
from jax.sharding import PartitionSpec as P

BF = jnp.bfloat16
F32 = jnp.float32
VMEM_LIMIT = 8 * 1024 * 1024
LARGE_LIMIT = 58 * 1024 * 1024


def dot(a, b):
    return lax.dot_general(a, b, (((1,), (0,)), ((), ())), preferred_element_type=F32)


def dot_first(a, b):
    return lax.dot_general(a, b, (((0,), (0,)), ((), ())), preferred_element_type=F32)


def dot_last(a, b):
    return lax.dot_general(a, b, (((1,), (1,)), ((), ())), preferred_element_type=F32)


def spread(block, chunks, row):
    for col in range(4):
        chunks[pl.ds(row * 4 + col, 64, stride=16), :] = block[pl.ds(col, 64, stride=4), :]


def collect(chunks, block, row):
    for col in range(4):
        block[pl.ds(col, 64, stride=4), :] = chunks[pl.ds(row * 4 + col, 64, stride=16), :]


def moves(pairs, sems):
    copies = [pltpu.make_async_copy(source, to, sems.at[i]) for i, (source, to) in enumerate(pairs)]
    for copy in copies:
        copy.start()
    return copies


def choose(act, refs, offsets, layer, to, sem):
    index = lax.axis_index("segment")
    for ref, offset in zip(refs, offsets):
        @pl.when((index + offset) % 4 == layer)
        def _():
            getattr(pltpu.make_async_copy(ref, to, sem), act)()


def parts_kernel(inputs, scale, shift, tops, *refs):
    outs, upstream, both, vectors, sems = refs[:4], refs[4], refs[5], refs[6], refs[7]
    index = lax.axis_index("segment")
    lanes = [pl.ds(pl.multiple_of(((index + step) % 4) * 128, 128), 128) for step in range(4)]
    pairs = [(scale, both.at[0:1, :]), (shift, both.at[1:2, :]), (tops.at[:, lanes[0]], upstream)]
    pairs += [(inputs.at[:, lanes[step]], outs[step].at[:1024, :]) for step in range(4)]
    copies = moves(pairs, sems)
    copies[0].wait()
    copies[1].wait()
    vectors[...] = jnp.zeros_like(vectors)
    for step in range(4):
        for place in range(2):
            left = both[place:place + 1, lanes[step]]
            for term in range(3):
                piece = left.astype(BF).astype(F32)
                vectors[place * 3 + term:place * 3 + term + 1, :] = piece
                left = left - piece
        outs[step][1024:, :] = vectors[...].astype(BF)
    for copy in copies[2:]:
        copy.wait()


def first_kernel(firsts, inputs, out, block, chunks, weights, held, sems):
    copies = moves([(firsts, weights), (inputs, held)], sems)
    for copy in copies:
        copy.wait()
    for part in range(4):
        lanes = slice(part * 128, (part + 1) * 128)
        for row in range(4):
            block[...] = dot(weights[row], held[row * 256:(row + 1) * 256, lanes])
            spread(block, chunks, row)
        out[:, part] = chunks[...].astype(BF).reshape(64, 16, 128)


def gated(inputs, vector, place, rows):
    scale, shift = vector[place, 0:1, :], vector[place, 1:2, :]
    return jax.nn.sigmoid(inputs[place, rows, :].astype(F32) * scale + shift), scale


def gate_kernel(seconds, firsts_cols, upstream, own, near, far, last, out, held, vectors, *scratch):
    block, chunks, wide, mixed, weights, fcols, ups, terms, sems = scratch
    index = lax.axis_index("segment")
    pairs = [(seconds, weights), (firsts_cols, fcols), (upstream, ups)]
    for step, part in enumerate((own, near, far, last)):
        layer = (index + 4 - step) % 4
        pairs += [(part.at[:1024, :], held.at[layer]), (part.at[1024:, :], terms.at[layer])]
    for copy in moves(pairs, sems):
        copy.wait()
    for layer in range(4):
        values = terms[layer].astype(F32)
        vectors[layer, 0:1, :] = values[0:1, :] + (values[1:2, :] + values[2:3, :])
        vectors[layer, 1:2, :] = values[3:4, :] + (values[4:5, :] + values[5:6, :])
    for part in range(4):
        wide[...] = fcols[:, part].reshape(1024, 128).astype(F32)
        for col in range(4):
            rows = pl.ds(col, 256, stride=4)
            mixed[rows, :] = dot(weights[col], wide[rows, :].astype(BF))
        out[:, part] = mixed[...].astype(BF).reshape(64, 16, 128)
    for row in range(4):
        rows = slice(row * 256, (row + 1) * 256)
        gate, _ = gated(held, vectors, 3, rows)
        block[...] = ups[rows, :].astype(F32) * gate
        spread(block, chunks, row)
    out[:, 4] = chunks[...].astype(BF).reshape(64, 16, 128)


def column_kernel(layer, received, own, left, right, across, *rest):
    columns, rest = (rest[:3], rest[3:]) if layer == 0 else ((), rest)
    out, (grads, back, weights, got, sems) = rest[0], rest[-5:]
    picked = rest[1:-5]
    index = lax.axis_index("segment")
    factors = (own, left, right, across)
    choose("start", factors, RING, layer, weights, sems.at[5])
    pairs = [(received.at[:, 4] if layer == 3 else received, got)]
    if layer == 3:
        pairs += [(received.at[:, (index + step) % 4], part) for step, part in enumerate(picked)]
    copies = moves(pairs, sems)
    if layer == 0:
        for step, part in enumerate(picked):
            pick("start", (received,) + columns, step, part, sems.at[1 + step])
    copies[0].wait()
    grads[...] = got[...].reshape(1024, 128).astype(F32)
    choose("wait", factors, RING, layer, weights, sems.at[5])
    for col in range(4):
        rows = pl.ds(col, 256, stride=4)
        back[rows, :] = dot_first(weights[col], grads[rows, :].astype(BF))
    out[...] = back[...].astype(BF).reshape(64, 16, 128)
    for copy in copies[1:]:
        copy.wait()
    if layer == 0:
        for step, part in enumerate(picked):
            pick("wait", (received,) + columns, step, part, sems.at[1 + step])


def pick(act, values, step, to, sem):
    index = lax.axis_index("segment")
    for layer, value in enumerate(values):
        if value is not None:
            @pl.when((index + step) % 4 == layer)
            def _():
                getattr(pltpu.make_async_copy(value, to, sem), act)()


def second_kernel(firsts_cols, own, near, far, last, out, grads, firsts_out):
    index = lax.axis_index("segment")
    for step, received in enumerate((own, near, far, last)):
        grads[...] = received[...].reshape(1024, 128).astype(F32)
        firsts_out[...] = firsts_cols[:, (index + 4 - step) % 4].reshape(1024, 128).astype(F32)
        for col in range(4):
            rows = pl.ds(col, 256, stride=4)
            part = dot_last(grads[rows, :].astype(BF), firsts_out[rows, :].astype(BF))
            out[col] = part if step == 0 else out[col] + part


def row_kernel(layer, received, own, left, right, across, upstream, held, vectors, *rest):
    slots, rest = rest[:4], rest[4:]
    earlier, rest = ((None,) + rest[:3], rest[3:]) if layer == 0 else ((), rest)
    outs, rest = (rest[:4], rest[4:]) if layer == 0 else (rest[:2], rest[2:])
    chunks, mixed_chunks, block, mixed_block, next_chunks, vector, weights, inputs, ups, mixed, got, sems = rest
    index = lax.axis_index("segment")
    factors = (own, left, right, across)
    pairs = [(received, got), (upstream, ups), (vectors, vector), (held.at[layer], inputs.at[layer])]
    if layer > 0:
        pairs.append((held.at[layer - 1], inputs.at[layer - 1]))
    copies = moves(pairs, sems)
    choose("start", slots, (0, 3, 2, 1), layer, mixed, sems.at[5])
    choose("start", factors, RING, layer, weights, sems.at[6])
    if layer == 0:
        for step in range(4):
            pick("start", earlier, step, outs[step], sems.at[7 + step])
    copies[0].wait()
    chunks[...] = got[...].reshape(1024, 128).astype(F32)
    choose("wait", slots, (0, 3, 2, 1), layer, mixed, sems.at[5])
    mixed_chunks[...] = mixed[...].reshape(1024, 128).astype(F32)
    choose("wait", factors, RING, layer, weights, sems.at[6])
    for copy in copies[1:]:
        copy.wait()
    for row in range(4):
        rows = slice(row * 256, (row + 1) * 256)
        collect(chunks, block, row)
        collect(mixed_chunks, mixed_block, row)
        through = dot_first(weights[row], block[...].astype(BF))
        up = ups[rows, :].astype(F32)
        gate, scale = gated(inputs, vector, layer, rows)
        slope = (up * gate * (1.0 - gate)).astype(BF).astype(F32)
        gate_grad = (slope * mixed_block[...]).astype(BF).astype(F32)
        result = (up + through + gate_grad * scale).astype(BF)
        if layer == 0:
            for step in range(4):
                @pl.when((index + step) % 4 == 0)
                def _():
                    outs[step][rows, :] = result
        else:
            outs[0][rows, :] = result
            gate, _ = gated(inputs, vector, layer - 1, rows)
            block[...] = result.astype(F32) * gate
            spread(block, next_chunks, row)
    if layer > 0:
        outs[1][...] = next_chunks[...].astype(BF).reshape(64, 16, 128)
    else:
        for step in range(4):
            pick("wait", earlier, step, outs[step], sems.at[7 + step])


def final_kernel(own, near, far, last, out):
    index = lax.axis_index("segment")
    for step, value in enumerate((own, near, far, last)):
        lanes = pl.ds(pl.multiple_of(((index + 4 - step) % 4) * 128, 128), 128)
        out[:, lanes] = value[...]


IN_VMEM = pl.BlockSpec(memory_space=pltpu.VMEM)
ANYWHERE = pl.BlockSpec(memory_space=pl.ANY)


def call(kernel, count, out_shapes, scratch, flops, copies=0, grant=VMEM_LIMIT):
    outs = [jax.ShapeDtypeStruct(s, d) for s, d in out_shapes]
    single = len(outs) == 1
    return pl.pallas_call(
        kernel,
        in_specs=[ANYWHERE if copies else IN_VMEM] * count,
        out_shape=outs[0] if single else outs,
        out_specs=IN_VMEM if single else [IN_VMEM] * len(outs),
        scratch_shapes=[pltpu.VMEM(*s) if isinstance(s[0], tuple) else pltpu.VMEM(s, F32) for s in scratch]
        + ([pltpu.SemaphoreType.DMA((copies,))] if copies else []),
        compiler_params=pltpu.CompilerParams(vmem_limit_bytes=grant),
        cost_estimate=pl.CostEstimate(flops=flops, bytes_accessed=2 << 20, transcendentals=0),
    )


RING = (0, 3, 1, 2)
TALL = (1024, 128)
CHUNKS = (64, 16, 128)
BLOCK = (256, 128)
FLOPS = 2 * 4 * 256 * 256 * 128


FACTOR = ((4, 256, 256), BF)


def passed(value, step):
    return lax.ppermute(value, "segment", [(i, (i + step) % 4) for i in range(4)])


def exchanged(parts):
    return [parts[0]] + [passed(parts[step], step) for step in (1, 2, 3)]


def body(layer_inputs, first_blocks, second_blocks, gate_scale, gate_shift, top_grads):
    firsts, seconds = first_blocks[0], second_blocks[0]
    made = call(
        parts_kernel,
        4,
        [((1040, 128), BF)] * 4 + [(TALL, BF)],
        [(2, 512), (16, 128)],
        1 << 20,
        copies=7,
        grant=LARGE_LIMIT,
    )(layer_inputs[0], gate_scale, gate_shift, top_grads)
    parts, upstream = exchanged(made[:4]), made[4]
    firsts_out = call(
        first_kernel,
        2,
        [((64, 4, 16, 128), BF)],
        [BLOCK, TALL, FACTOR, ((1024, 512), BF)],
        4 * FLOPS,
        copies=2,
        grant=LARGE_LIMIT,
    )(firsts, layer_inputs[0])
    firsts_cols = lax.all_to_all(firsts_out, "seq", 0, 0, tiled=True)
    firsts_cols, parts, firsts, seconds = lax.optimization_barrier((firsts_cols, parts, firsts, seconds))
    payload, held, vectors = call(
        gate_kernel,
        7,
        [((64, 5, 16, 128), BF), ((4, 1024, 128), BF), ((4, 2, 128), F32)],
        [BLOCK, TALL, TALL, TALL, FACTOR, ((64, 4, 16, 128), BF), (TALL, BF), ((4, 16, 128), BF)],
        4 * FLOPS,
        copies=11,
        grant=LARGE_LIMIT,
    )(seconds, firsts_cols, upstream, *parts)
    columns = [None] * 4
    columns[3] = lax.all_to_all(payload, "seq", 0, 0, tiled=True)
    firsts_all = [firsts, passed(firsts, 1), passed(firsts, 3)]
    seconds_all = [seconds, passed(seconds, 1), passed(seconds, 3)]
    firsts_all.append(passed(firsts_all[2], 3))
    seconds_all.append(passed(seconds_all[1], 1))
    columns[3], firsts_all, seconds_all = lax.optimization_barrier((columns[3], firsts_all, seconds_all))

    results, mixed = [None] * 4, None
    for l in (3, 2, 1, 0):
        grant = LARGE_LIMIT if l in (3, 0) else VMEM_LIMIT
        if l < 3:
            columns[l] = lax.all_to_all(sends, "seq", 0, 0, tiled=True)
        operands = [columns[l], *seconds_all] + (columns[1:3] + [grads_three] if l == 0 else [])
        made = call(
            functools.partial(column_kernel, l),
            len(operands),
            [(CHUNKS, BF)] * (5 if l in (3, 0) else 1),
            [TALL, TALL, FACTOR, (CHUNKS, BF)],
            FLOPS,
            copies=6,
            grant=grant,
        )(*operands)
        back = made[0] if l in (3, 0) else made
        received = lax.all_to_all(back, "seq", 0, 0, tiled=True)
        if l == 3:
            mixed = exchanged(made[1:])
            grads_three = columns[3][:, 4]
        if l == 0:
            grads = exchanged(made[1:])
        operands = [received, *firsts_all, upstream, held, vectors, *mixed] + (results[1:] if l == 0 else [])
        made = call(
            functools.partial(row_kernel, l),
            len(operands),
            [(TALL, BF), (CHUNKS, BF)] if l > 0 else [(TALL, BF)] * 4,
            [TALL, TALL, BLOCK, BLOCK, TALL, (4, 2, 128)]
            + [FACTOR, ((4, 1024, 128), BF), (TALL, BF), (CHUNKS, BF), (CHUNKS, BF)],
            FLOPS,
            copies=11,
            grant=grant,
        )(*operands)
        if l > 0:
            upstream, sends = made
            results[l] = upstream

    second = call(second_kernel, 5, [((4, 256, 256), F32)], [TALL, TALL], 4 * FLOPS)(firsts_cols, *grads)
    grads_out = call(final_kernel, 4, [((1024, 512), BF)], [], 1 << 20)(*exchanged(made))
    return grads_out[None], second[None]


def solution(mesh):
    placed = (
        P("segment", "seq", None),
        P("segment", "seq", None, None),
        P("segment", "seq", None, None),
        P("segment", None),
        P("segment", None),
        P("seq", None),
    )
    return jax.shard_map(
        body,
        mesh=mesh,
        in_specs=placed,
        out_specs=(P("segment", "seq", None), P("segment", "seq", None, None)),
        check_vma=False,
    )
```

time: 277 us -> 279 us (level)
  blocking collectives: 148 us -> 77.9 us
  starting transfers between devices: 24.1 us -> 64.4 us
  waiting for transfers between devices: 65.6 us -> 93.5 us
  Pallas kernels: 13.5 us -> 30.4 us
  between operations: 14 us -> 1.08 us
    all_to_all x4 -> x2, blocking collectives: 88.3 us -> 35.5 us  [body(): received = lax.all_to_all(back, 'seq', 0, 0, tiled=True)]
    ppermute x3 -> x18, waiting for transfers between devices: 9.7 us -> 62.5 us  [passed(): lax.ppermute(value, 'segment', [(i, (i + step) % 4) for i in range(4)])]
    all_to_all x1 -> x4, starting transfers between devices: 6.46 us -> 36.3 us  [the longest x2 16.4 us: body(): received = lax.all_to_all(back, 'seq', 0, 0, tiled=True)]
    ppermute x3 -> x18, starting transfers between devices: 2.97 us -> 23.1 us  [passed(): lax.ppermute(value, 'segment', [(i, (i + step) % 4) for i in range(4)])]
    all_gather x2 -> x0, waiting for transfers between devices: 17.9 us -> none  [the longest x1 17.9 us: body(): firsts_all = lax.all_gather(first_blocks, 'segment', tiled=True)]
    all_to_all x3 -> x2, blocking collectives: 59.6 us -> 42.5 us  [body(): columns[l] = lax.all_to_all(sends, 'seq', 0, 0, tiled=True)]
    pallas_call x13, Pallas kernels: 13.5 us -> 30.4 us  [the longest x4 10.9 us: body(): call(functools.partial(row_kernel, l), len(operands), [(TALL, BF), (CHUNK...]
    all_to_all x1, waiting for transfers between devices: 27.2 us -> 11.5 us  [body(): columns[l] = lax.all_to_all(sends, 'seq', 0, 0, tiled=True)]
  transfers between devices with their start and end apart: 8 -> 23, of which waited for: 6 -> 14; matrix products, arithmetic and copies ran while one was open for 1% -> 1% of each run, Pallas kernels for 1% -> 3%
where the time goes in v2:
time: 279 us; the launch traced here: 278 us
  waiting for transfers between devices  93.5 us (34%)
  blocking collectives  77.9 us (28%)
  starting transfers between devices  64.4 us (23%)
  Pallas kernels  30.4 us (11%)
  local copies, waits for them, and re-layouts  10.2 us (4%)
    ppermute x18, waiting for transfers between devices, passed(): lax.ppermute(value, 'segment', [(i, (i + step) % 4) for i in range(4)])  62.5 us
    all_to_all x2, blocking collectives, body(): columns[l] = lax.all_to_all(sends, 'seq', 0, 0, tiled=True)  42.5 us
    all_to_all x2, blocking collectives, body(): received = lax.all_to_all(back, 'seq', 0, 0, tiled=True)  35.5 us
    ppermute x18, starting transfers between devices, passed(): lax.ppermute(value, 'segment', [(i, (i + step) % 4) for i in range(4)])  23.1 us
    all_to_all x2, starting transfers between devices, body(): received = lax.all_to_all(back, 'seq', 0, 0, tiled=True)  16.4 us
    all_to_all x1, starting transfers between devices, body(): firsts_cols = lax.all_to_all(firsts_out, 'seq', 0, 0, tiled=True)  13.2 us
    all_to_all x1, waiting for transfers between devices, body(): columns[l] = lax.all_to_all(sends, 'seq', 0, 0, tiled=True)  11.5 us
    pallas_call x4, Pallas kernels, body(): call(functools.partial(row_kernel, l), len(operands), [(TALL, BF), (CHUNK...  10.9 us
  transfers between devices with their start and end apart: 23, of which 14 were waited for; matrix products, arithmetic and copies ran while one was open for 1% of the time, Pallas kernels for 3%

profile of v2, /device:TPU:1, one launch (start us, length us, event | category | flops | bytes accessed | tf_op | source)
XLA Modules:
  0.0 277.6 jit_solution(1135856337248141696)
XLA Ops:
  0.6 3.6 %shard_map.77 = bf16[64,4,16,128]{3,2,1,0:T(8,128)(2,1)} custom-call(bf16[4,256,256]{2,1,0:T(8,128)(2,1)} %bitcast.14, bf16[1024,512]{1,0:T(8,128)(2,1)} %bitcast.21), custom_call_target="tpu_custom_call" | custom-call | flops 268435456 | bytes 2097152 | tf_op jit(solution)/shard_map/pallas_call | solution.py:273
  4.3 13.2 %all-to-all-start = ((bf16[64,4,16,128]{3,2,1,0:T(8,128)(2,1)}), bf16[64,4,16,128]{3,2,1,0:T(8,128)(2,1)S(1)}, u32[]{:S(2)}, u32[]{:S(2)}) async-start(bf16[64,4,16,128]{3,2,1,0:T(8,128)(2,1)} %shard_map.77), calls=%async_computation | async-start | bytes 2097152 | tf_op jit(solution)/shard_map/all_to_all | solution.py:282
  24.8 4.1 %collective-permute-done.near = bf16[1040,128]{1,0:T(8,128)(2,1)S(1)} collective-permute-done((bf16[1040,128]{1,0:T(8,128)(2,1)}, bf16[1040,128]{1,0:T(8,128)(2,1)S(1)}, u32[]{:S(2)}, u32[]{:S(2)}) %collective-permute-start) | collective-permute-done | bytes 266272 | tf_op jit(solution)/shard_map/ppermute | solution.py:254
  28.9 6.7 %collective-permute-done.1.far = bf16[1040,128]{1,0:T(8,128)(2,1)S(1)} collective-permute-done((bf16[1040,128]{1,0:T(8,128)(2,1)}, bf16[1040,128]{1,0:T(8,128)(2,1)S(1)}, u32[]{:S(2)}, u32[]{:S(2)}) %collective-permute-start.1) | collective-permute-done | bytes 266272 | tf_op jit(solution)/shard_map/ppermute | solution.py:254
  35.6 9.8 %all-to-all-done.firsts_cols = bf16[64,4,16,128]{3,2,1,0:T(8,128)(2,1)S(1)} async-done(((bf16[64,4,16,128]{3,2,1,0:T(8,128)(2,1)}), bf16[64,4,16,128]{3,2,1,0:T(8,128)(2,1)S(1)}, u32[]{:S(2)}, u32[]{:S(2)}) %all-to-all-start) | async-done | bytes 1048608 | tf_op jit(solution)/shard_map/all_to_all | solution.py:282
  46.4 4.0 %shard_map.79 = (bf16[64,5,16,128]{3,2,1,0:T(8,128)(2,1)}, bf16[4,1024,128]{2,1,0:T(8,128)(2,1)}, f32[4,2,128]{2,1,0:T(2,128)}) custom-call(bf16[4,256,256]{2,1,0:T(8,128)(2,1)} %bitcast.7, bf16[64,4,16,128]{3,2,1,0:T(8,128)(2,1)} %copy-done.5, bf16[1024,128]{1,0:T(8,128)(2,1)} %get-tuple-element.52.upstream, bf16[1040,128]{1,0:T(8,128)(2,1)} %get-tuple-element.53.own, ...), custom_call_target="tpu_custom_call" | custom-call | flops 268435456 | bytes 2097152 | tf_op jit(solution)/shard_map/pallas_call | solution.py:284
  50.4 6.8 %all-to-all-start.1 = ((bf16[64,5,16,128]{3,2,1,0:T(8,128)(2,1)}), bf16[64,5,16,128]{3,2,1,0:T(8,128)(2,1)}, u32[]{:S(2)}, u32[]{:S(2)}) async-start(bf16[64,5,16,128]{3,2,1,0:T(8,128)(2,1)} %get-tuple-element.57), calls=%async_computation.1 | async-start | bytes 2621440 | tf_op jit(solution)/shard_map/all_to_all | solution.py:294
  62.5 8.1 %collective-permute-done.4.right = bf16[4,256,256]{2,1,0:T(8,128)(2,1)S(1)} collective-permute-done((bf16[4,256,256]{2,1,0:T(8,128)(2,1)S(1)}, bf16[4,256,256]{2,1,0:T(8,128)(2,1)S(1)}, u32[]{:S(2)}, u32[]{:S(2)}) %collective-permute-start.4) | collective-permute-done | bytes 524320 | tf_op jit(solution)/shard_map/ppermute | solution.py:254
  74.1 10.9 %collective-permute-done.3.left = bf16[4,256,256]{2,1,0:T(8,128)(2,1)S(1)} collective-permute-done((bf16[4,256,256]{2,1,0:T(8,128)(2,1)S(1)}, bf16[4,256,256]{2,1,0:T(8,128)(2,1)S(1)}, u32[]{:S(2)}, u32[]{:S(2)}) %collective-permute-start.3) | collective-permute-done | bytes 524320 | tf_op jit(solution)/shard_map/ppermute | solution.py:254
  85.0 8.0 %collective-permute-done.5.across = bf16[4,256,256]{2,1,0:T(8,128)(2,1)S(1)} collective-permute-done((bf16[4,256,256]{2,1,0:T(8,128)(2,1)S(1)}, bf16[4,256,256]{2,1,0:T(8,128)(2,1)S(1)}, u32[]{:S(2)}, u32[]{:S(2)}) %collective-permute-start.5) | collective-permute-done | bytes 524320 | tf_op jit(solution)/shard_map/ppermute | solution.py:254
  99.6 11.6 %all-to-all-start.2 = ((bf16[64,16,128]{2,1,0:T(8,128)(2,1)}), bf16[64,16,128]{2,1,0:T(8,128)(2,1)S(1)}, u32[]{:S(2)}, u32[]{:S(2)}) async-start(bf16[64,16,128]{2,1,0:T(8,128)(2,1)} %get-tuple-element.64), calls=%async_computation.2 | async-start | bytes 524288 | tf_op jit(solution)/shard_map/all_to_all | solution.py:317
  114.0 6.9 %collective-permute-done.9.rest_1_ = bf16[64,16,128]{2,1,0:T(8,128)(2,1)S(1)} collective-permute-done((bf16[64,16,128]{2,1,0:T(8,128)(2,1)}, bf16[64,16,128]{2,1,0:T(8,128)(2,1)S(1)}, u32[]{:S(2)}, u32[]{:S(2)}) %collective-permute-start.9) | collective-permute-done | bytes 262176 | tf_op jit(solution)/shard_map/ppermute | solution.py:254
  120.9 4.3 %collective-permute-done.10.rest_2_ = bf16[64,16,128]{2,1,0:T(8,128)(2,1)S(1)} collective-permute-done((bf16[64,16,128]{2,1,0:T(8,128)(2,1)}, bf16[64,16,128]{2,1,0:T(8,128)(2,1)S(1)}, u32[]{:S(2)}, u32[]{:S(2)}) %collective-permute-start.10) | collective-permute-done | bytes 262176 | tf_op jit(solution)/shard_map/ppermute | solution.py:254
  130.6 24.8 %all_to_all.45.received.rest_1_ = bf16[64,16,128]{2,1,0:T(8,128)(2,1)S(1)} all-to-all(bf16[64,16,128]{2,1,0:T(8,128)(2,1)} %get-tuple-element.75), channel_id=1, replica_groups=mesh['segment'=4,'seq'=64] {'seq'}, dimensions={0} | all-to-all | bytes 524288 | tf_op jit(solution)/shard_map/all_to_all | solution.py:305
  156.1 17.8 %all_to_all.46.received = bf16[64,16,128]{2,1,0:T(8,128)(2,1)S(1)} all-to-all(bf16[64,16,128]{2,1,0:T(8,128)(2,1)S(1)} %shard_map.82), channel_id=1, replica_groups=mesh['segment'=4,'seq'=64] {'seq'}, dimensions={0} | all-to-all | bytes 524288 | tf_op jit(solution)/shard_map/all_to_all | solution.py:317
  178.3 17.7 %all_to_all.47.received.rest_0_ = bf16[64,16,128]{2,1,0:T(8,128)(2,1)S(1)} all-to-all(bf16[64,16,128]{2,1,0:T(8,128)(2,1)S(1)} %get-tuple-element.77), channel_id=1, replica_groups=mesh['segment'=4,'seq'=64] {'seq'}, dimensions={0} | all-to-all | bytes 524288 | tf_op jit(solution)/shard_map/all_to_all | solution.py:305
  196.7 17.7 %all_to_all.48.received = bf16[64,16,128]{2,1,0:T(8,128)(2,1)S(1)} all-to-all(bf16[64,16,128]{2,1,0:T(8,128)(2,1)S(1)} %shard_map.84), channel_id=1, replica_groups=mesh['segment'=4,'seq'=64] {'seq'}, dimensions={0} | all-to-all | bytes 524288 | tf_op jit(solution)/shard_map/all_to_all | solution.py:317
  217.3 4.9 %all-to-all-start.7 = ((bf16[64,16,128]{2,1,0:T(8,128)(2,1)}), bf16[64,16,128]{2,1,0:T(8,128)(2,1)S(1)}, u32[]{:S(2)}, u32[]{:S(2)}) async-start(bf16[64,16,128]{2,1,0:T(8,128)(2,1)} %get-tuple-element.79), calls=%async_computation.7 | async-start | bytes 524288 | tf_op jit(solution)/shard_map/all_to_all | solution.py:305
  223.9 11.5 %all-to-all-done.7.received = bf16[64,16,128]{2,1,0:T(8,128)(2,1)S(1)} async-done(((bf16[64,16,128]{2,1,0:T(8,128)(2,1)}), bf16[64,16,128]{2,1,0:T(8,128)(2,1)S(1)}, u32[]{:S(2)}, u32[]{:S(2)}) %all-to-all-start.7) | async-done | bytes 262176 | tf_op jit(solution)/shard_map/all_to_all | solution.py:305
  238.8 4.7 %all-to-all-start.8 = ((bf16[64,16,128]{2,1,0:T(8,128)(2,1)}), bf16[64,16,128]{2,1,0:T(8,128)(2,1)S(1)}, u32[]{:S(2)}, u32[]{:S(2)}) async-start(bf16[64,16,128]{2,1,0:T(8,128)(2,1)} %get-tuple-element.80), calls=%async_computation.8 | async-start | bytes 524288 | tf_op jit(solution)/shard_map/all_to_all | solution.py:317
  246.9 9.8 %all-to-all-done.8.received = bf16[64,16,128]{2,1,0:T(8,128)(2,1)S(1)} async-done(((bf16[64,16,128]{2,1,0:T(8,128)(2,1)}), bf16[64,16,128]{2,1,0:T(8,128)(2,1)S(1)}, u32[]{:S(2)}, u32[]{:S(2)}) %all-to-all-start.8) | async-done | bytes 262176 | tf_op jit(solution)/shard_map/all_to_all | solution.py:317
  257.4 3.6 %shard_map.87 = (bf16[1024,128]{1,0:T(8,128)(2,1)}, bf16[1024,128]{1,0:T(8,128)(2,1)}, bf16[1024,128]{1,0:T(8,128)(2,1)}, bf16[1024,128]{1,0:T(8,128)(2,1)}) custom-call(bf16[64,16,128]{2,1,0:T(8,128)(2,1)} %copy-done.36, bf16[4,256,256]{2,1,0:T(8,128)(2,1)} %bitcast.16, bf16[4,256,256]{2,1,0:T(8,128)(2,1)} %copy-done.15, bf16[4,256,256]{2,1,0:T(8,128)(2,1)} %copy-done.13, ...), custom_call_target="tpu_custom_call" | custom-call | flops 67108864 | bytes 2097152 | tf_op jit(solution)/shard_map/pallas_call | solution.py:324
  266.2 4.0 %collective-permute-done.12.near = bf16[1024,128]{1,0:T(8,128)(2,1)S(1)} collective-permute-done((bf16[1024,128]{1,0:T(8,128)(2,1)}, bf16[1024,128]{1,0:T(8,128)(2,1)S(1)}, u32[]{:S(2)}, u32[]{:S(2)}) %collective-permute-start.12) | collective-permute-done | bytes 262176 | tf_op jit(solution)/shard_map/ppermute | solution.py:254
  270.2 6.2 %collective-permute-done.13.far = bf16[1024,128]{1,0:T(8,128)(2,1)S(1)} collective-permute-done((bf16[1024,128]{1,0:T(8,128)(2,1)}, bf16[1024,128]{1,0:T(8,128)(2,1)S(1)}, u32[]{:S(2)}, u32[]{:S(2)}) %collective-permute-start.13) | collective-permute-done | bytes 262176 | tf_op jit(solution)/shard_map/ppermute | solution.py:254
  (124 shorter events, 55.8 us)
Async XLA Ops:
  4.3 41.2 %all-to-all-start = ((bf16[64,4,16,128]{3,2,1,0:T(8,128)(2,1)}), bf16[64,4,16,128]{3,2,1,0:T(8,128)(2,1)S(1)}, u32[]{:S(2)}, u32[]{:S(2)}) async-start(bf16[64,4,16,128]{3,2,1,0:T(8,128)(2,1)} %shard_map.77), calls=%async_computation | async-start | bytes 2097152 | tf_op jit(solution)/shard_map/all_to_all | solution.py:282
  19.9 9.0 %collective-permute-start = (bf16[1040,128]{1,0:T(8,128)(2,1)}, bf16[1040,128]{1,0:T(8,128)(2,1)S(1)}, u32[]{:S(2)}, u32[]{:S(2)}) collective-permute-start(bf16[1040,128]{1,0:T(8,128)(2,1)} %get-tuple-element.47), channel_id=1, source_target_pairs={{0,64},{64,128},{128,192},{192,0},{1,65},{65,129},{129,193},{193,1... | collective-permute-start | bytes 798728 | tf_op jit(solution)/shard_map/ppermute | solution.py:254
  21.2 14.4 %collective-permute-start.1 = (bf16[1040,128]{1,0:T(8,128)(2,1)}, bf16[1040,128]{1,0:T(8,128)(2,1)S(1)}, u32[]{:S(2)}, u32[]{:S(2)}) collective-permute-start(bf16[1040,128]{1,0:T(8,128)(2,1)} %get-tuple-element.48), channel_id=1, source_target_pairs={{0,128},{64,192},{128,0},{192,64},{1,129},{65,193},{129,1},{193,65... | collective-permute-start | bytes 798728 | tf_op jit(solution)/shard_map/ppermute | solution.py:254
  23.6 12.0 %collective-permute-start.2 = (bf16[1040,128]{1,0:T(8,128)(2,1)}, bf16[1040,128]{1,0:T(8,128)(2,1)S(1)}, u32[]{:S(2)}, u32[]{:S(2)}) collective-permute-start(bf16[1040,128]{1,0:T(8,128)(2,1)} %get-tuple-element.49), channel_id=1, source_target_pairs={{0,192},{64,0},{128,64},{192,128},{1,193},{65,1},{129,65},{193,129... | collective-permute-start | bytes 798728 | tf_op jit(solution)/shard_map/ppermute | solution.py:254
  50.4 45.7 %all-to-all-start.1 = ((bf16[64,5,16,128]{3,2,1,0:T(8,128)(2,1)}), bf16[64,5,16,128]{3,2,1,0:T(8,128)(2,1)}, u32[]{:S(2)}, u32[]{:S(2)}) async-start(bf16[64,5,16,128]{3,2,1,0:T(8,128)(2,1)} %get-tuple-element.57), calls=%async_computation.1 | async-start | bytes 2621440 | tf_op jit(solution)/shard_map/all_to_all | solution.py:294
  57.2 13.3 %collective-permute-start.4 = (bf16[4,256,256]{2,1,0:T(8,128)(2,1)S(1)}, bf16[4,256,256]{2,1,0:T(8,128)(2,1)S(1)}, u32[]{:S(2)}, u32[]{:S(2)}) collective-permute-start(bf16[4,256,256]{2,1,0:T(8,128)(2,1)S(1)} %bitcast.17), channel_id=1, source_target_pairs={{0,192},{64,0},{128,64},{192,128},{1,193},{65,1},{129,65},{193,129... | collective-permute-start | bytes 1572872 | tf_op jit(solution)/shard_map/ppermute | solution.py:254
  59.8 14.3 %collective-permute-start.6 = (bf16[4,256,256]{2,1,0:T(8,128)(2,1)S(1)}, bf16[4,256,256]{2,1,0:T(8,128)(2,1)S(1)}, u32[]{:S(2)}, u32[]{:S(2)}) collective-permute-start(bf16[4,256,256]{2,1,0:T(8,128)(2,1)S(1)} %bitcast.10), channel_id=1, source_target_pairs={{0,64},{64,128},{128,192},{192,0},{1,65},{65,129},{129,193},{193,1... | collective-permute-start | bytes 1572872 | tf_op jit(solution)/shard_map/ppermute | solution.py:254
  59.8 25.2 %collective-permute-start.3 = (bf16[4,256,256]{2,1,0:T(8,128)(2,1)S(1)}, bf16[4,256,256]{2,1,0:T(8,128)(2,1)S(1)}, u32[]{:S(2)}, u32[]{:S(2)}) collective-permute-start(bf16[4,256,256]{2,1,0:T(8,128)(2,1)S(1)} %bitcast.18), channel_id=1, source_target_pairs={{0,64},{64,128},{128,192},{192,0},{1,65},{65,129},{129,193},{193,1... | collective-permute-start | bytes 1572872 | tf_op jit(solution)/shard_map/ppermute | solution.py:254
  60.0 25.0 %collective-permute-start.7 = (bf16[4,256,256]{2,1,0:T(8,128)(2,1)S(1)}, bf16[4,256,256]{2,1,0:T(8,128)(2,1)S(1)}, u32[]{:S(2)}, u32[]{:S(2)}) collective-permute-start(bf16[4,256,256]{2,1,0:T(8,128)(2,1)S(1)} %bitcast.11), channel_id=1, source_target_pairs={{0,192},{64,0},{128,64},{192,128},{1,193},{65,1},{129,65},{193,129... | collective-permute-start | bytes 1572872 | tf_op jit(solution)/shard_map/ppermute | solution.py:254
  70.5 55.6 %copy-start.13 = (bf16[4,256,256]{2,1,0:T(8,128)(2,1)}, bf16[4,256,256]{2,1,0:T(8,128)(2,1)S(1)}, u32[]{:S(2)}) copy-start(bf16[4,256,256]{2,1,0:T(8,128)(2,1)S(1)} %collective-permute-done.4.right) | copy-start | bytes 1572868
  70.5 22.5 %collective-permute-start.5 = (bf16[4,256,256]{2,1,0:T(8,128)(2,1)S(1)}, bf16[4,256,256]{2,1,0:T(8,128)(2,1)S(1)}, u32[]{:S(2)}, u32[]{:S(2)}) collective-permute-start(bf16[4,256,256]{2,1,0:T(8,128)(2,1)S(1)} %collective-permute-done.4.right), channel_id=1, source_target_pairs={{0,192},{64,0},{128,64},{192,128},{1,193},{65,1},{129,65},{193,129... | collective-permute-start | bytes 1572872 | tf_op jit(solution)/shard_map/ppermute | solution.py:254
  74.1 22.0 %collective-permute-start.8 = (bf16[4,256,256]{2,1,0:T(8,128)(2,1)S(1)}, bf16[4,256,256]{2,1,0:T(8,128)(2,1)S(1)}, u32[]{:S(2)}, u32[]{:S(2)}) collective-permute-start(bf16[4,256,256]{2,1,0:T(8,128)(2,1)S(1)} %collective-permute-done.6.left), channel_id=1, source_target_pairs={{0,64},{64,128},{128,192},{192,0},{1,65},{65,129},{129,193},{193,1... | collective-permute-start | bytes 1572872 | tf_op jit(solution)/shard_map/ppermute | solution.py:254
  99.6 26.5 %all-to-all-start.2 = ((bf16[64,16,128]{2,1,0:T(8,128)(2,1)}), bf16[64,16,128]{2,1,0:T(8,128)(2,1)S(1)}, u32[]{:S(2)}, u32[]{:S(2)}) async-start(bf16[64,16,128]{2,1,0:T(8,128)(2,1)} %get-tuple-element.64), calls=%async_computation.2 | async-start | bytes 524288 | tf_op jit(solution)/shard_map/all_to_all | solution.py:317
  111.2 9.6 %collective-permute-start.9 = (bf16[64,16,128]{2,1,0:T(8,128)(2,1)}, bf16[64,16,128]{2,1,0:T(8,128)(2,1)S(1)}, u32[]{:S(2)}, u32[]{:S(2)}) collective-permute-start(bf16[64,16,128]{2,1,0:T(8,128)(2,1)} %get-tuple-element.72), channel_id=1, source_target_pairs={{0,64},{64,128},{128,192},{192,0},{1,65},{65,129},{129,193},{193,1... | collective-permute-start | bytes 786440 | tf_op jit(solution)/shard_map/ppermute | solution.py:254
  111.3 13.8 %collective-permute-start.10 = (bf16[64,16,128]{2,1,0:T(8,128)(2,1)}, bf16[64,16,128]{2,1,0:T(8,128)(2,1)S(1)}, u32[]{:S(2)}, u32[]{:S(2)}) collective-permute-start(bf16[64,16,128]{2,1,0:T(8,128)(2,1)} %get-tuple-element.73), channel_id=1, source_target_pairs={{0,128},{64,192},{128,0},{192,64},{1,129},{65,193},{129,1},{193,65... | collective-permute-start | bytes 786440 | tf_op jit(solution)/shard_map/ppermute | solution.py:254
  113.3 12.8 %collective-permute-start.11 = (bf16[64,16,128]{2,1,0:T(8,128)(2,1)}, bf16[64,16,128]{2,1,0:T(8,128)(2,1)S(1)}, u32[]{:S(2)}, u32[]{:S(2)}) collective-permute-start(bf16[64,16,128]{2,1,0:T(8,128)(2,1)} %get-tuple-element.74), channel_id=1, source_target_pairs={{0,192},{64,0},{128,64},{192,128},{1,193},{65,1},{129,65},{193,129... | collective-permute-start | bytes 786440 | tf_op jit(solution)/shard_map/ppermute | solution.py:254
  217.3 18.1 %all-to-all-start.7 = ((bf16[64,16,128]{2,1,0:T(8,128)(2,1)}), bf16[64,16,128]{2,1,0:T(8,128)(2,1)S(1)}, u32[]{:S(2)}, u32[]{:S(2)}) async-start(bf16[64,16,128]{2,1,0:T(8,128)(2,1)} %get-tuple-element.79), calls=%async_computation.7 | async-start | bytes 524288 | tf_op jit(solution)/shard_map/all_to_all | solution.py:305
  238.8 17.9 %all-to-all-start.8 = ((bf16[64,16,128]{2,1,0:T(8,128)(2,1)}), bf16[64,16,128]{2,1,0:T(8,128)(2,1)S(1)}, u32[]{:S(2)}, u32[]{:S(2)}) async-start(bf16[64,16,128]{2,1,0:T(8,128)(2,1)} %get-tuple-element.80), calls=%async_computation.8 | async-start | bytes 524288 | tf_op jit(solution)/shard_map/all_to_all | solution.py:317
  243.5 20.9 %collective-permute-start.15 = (bf16[64,16,128]{2,1,0:T(8,128)(2,1)}, bf16[64,16,128]{2,1,0:T(8,128)(2,1)S(1)}, u32[]{:S(2)}, u32[]{:S(2)}) collective-permute-start(bf16[64,16,128]{2,1,0:T(8,128)(2,1)} %get-tuple-element.87), channel_id=1, source_target_pairs={{0,64},{64,128},{128,192},{192,0},{1,65},{65,129},{129,193},{193,1... | collective-permute-start | bytes 786440 | tf_op jit(solution)/shard_map/ppermute | solution.py:254
  243.6 20.8 %collective-permute-start.16 = (bf16[64,16,128]{2,1,0:T(8,128)(2,1)}, bf16[64,16,128]{2,1,0:T(8,128)(2,1)S(1)}, u32[]{:S(2)}, u32[]{:S(2)}) collective-permute-start(bf16[64,16,128]{2,1,0:T(8,128)(2,1)} %get-tuple-element.88), channel_id=1, source_target_pairs={{0,128},{64,192},{128,0},{192,64},{1,129},{65,193},{129,1},{193,65... | collective-permute-start | bytes 786440 | tf_op jit(solution)/shard_map/ppermute | solution.py:254
  246.9 17.5 %collective-permute-start.17 = (bf16[64,16,128]{2,1,0:T(8,128)(2,1)}, bf16[64,16,128]{2,1,0:T(8,128)(2,1)S(1)}, u32[]{:S(2)}, u32[]{:S(2)}) collective-permute-start(bf16[64,16,128]{2,1,0:T(8,128)(2,1)} %get-tuple-element.89), channel_id=1, source_target_pairs={{0,192},{64,0},{128,64},{192,128},{1,193},{65,1},{129,65},{193,129... | collective-permute-start | bytes 786440 | tf_op jit(solution)/shard_map/ppermute | solution.py:254
  261.0 9.2 %collective-permute-start.12 = (bf16[1024,128]{1,0:T(8,128)(2,1)}, bf16[1024,128]{1,0:T(8,128)(2,1)S(1)}, u32[]{:S(2)}, u32[]{:S(2)}) collective-permute-start(bf16[1024,128]{1,0:T(8,128)(2,1)} %get-tuple-element.83), channel_id=1, source_target_pairs={{0,64},{64,128},{128,192},{192,0},{1,65},{65,129},{129,193},{193,1... | collective-permute-start | bytes 786440 | tf_op jit(solution)/shard_map/ppermute | solution.py:254
  261.1 15.3 %collective-permute-start.13 = (bf16[1024,128]{1,0:T(8,128)(2,1)}, bf16[1024,128]{1,0:T(8,128)(2,1)S(1)}, u32[]{:S(2)}, u32[]{:S(2)}) collective-permute-start(bf16[1024,128]{1,0:T(8,128)(2,1)} %get-tuple-element.84), channel_id=1, source_target_pairs={{0,128},{64,192},{128,0},{192,64},{1,129},{65,193},{129,1},{193,65... | collective-permute-start | bytes 786440 | tf_op jit(solution)/shard_map/ppermute | solution.py:254
  264.4 12.0 %collective-permute-start.14 = (bf16[1024,128]{1,0:T(8,128)(2,1)}, bf16[1024,128]{1,0:T(8,128)(2,1)S(1)}, u32[]{:S(2)}, u32[]{:S(2)}) collective-permute-start(bf16[1024,128]{1,0:T(8,128)(2,1)} %get-tuple-element.85), channel_id=1, source_target_pairs={{0,192},{64,0},{128,64},{192,128},{1,193},{65,1},{129,65},{193,129... | collective-permute-start | bytes 786440 | tf_op jit(solution)/shard_map/ppermute | solution.py:254
  (41 other events, 548.9 us)

commit v3 on v2

--- a/solution.py
+++ b/solution.py
@@ -73,19 +73,23 @@
 
 
 def first_kernel(firsts, inputs, out, block, chunks, weights, held, sems):
-    copies = moves([(firsts, weights), (inputs, held)], sems)
+    copies = moves(
+        [(firsts.at[row], weights.at[row]) for row in range(4)]
+        + [(inputs.at[row], held.at[row]) for row in range(4)],
+        sems,
+    )
     for copy in copies:
         copy.wait()
     for part in range(4):
         lanes = slice(part * 128, (part + 1) * 128)
         for row in range(4):
-            block[...] = dot(weights[row], held[row * 256:(row + 1) * 256, lanes])
+            block[...] = dot(weights[row], held[row, :, lanes])
             spread(block, chunks, row)
         out[:, part] = chunks[...].astype(BF).reshape(64, 16, 128)
 
 
-def gated(inputs, vector, place, rows):
-    scale, shift = vector[place, 0:1, :], vector[place, 1:2, :]
+def gated(inputs, place, vectors, layer, rows):
+    scale, shift = vectors[layer, 0:1, :], vectors[layer, 1:2, :]
     return jax.nn.sigmoid(inputs[place, rows, :].astype(F32) * scale + shift), scale
 
 
@@ -96,21 +100,24 @@
     for step, part in enumerate((own, near, far, last)):
         layer = (index + 4 - step) % 4
         pairs += [(part.at[:1024, :], held.at[layer]), (part.at[1024:, :], terms.at[layer])]
-    for copy in moves(pairs, sems):
-        copy.wait()
-    for layer in range(4):
-        values = terms[layer].astype(F32)
-        vectors[layer, 0:1, :] = values[0:1, :] + (values[1:2, :] + values[2:3, :])
-        vectors[layer, 1:2, :] = values[3:4, :] + (values[4:5, :] + values[5:6, :])
+    copies = moves(pairs, sems)
+    copies[0].wait()
+    copies[1].wait()
     for part in range(4):
         wide[...] = fcols[:, part].reshape(1024, 128).astype(F32)
         for col in range(4):
             rows = pl.ds(col, 256, stride=4)
             mixed[rows, :] = dot(weights[col], wide[rows, :].astype(BF))
         out[:, part] = mixed[...].astype(BF).reshape(64, 16, 128)
+    for copy in copies[2:]:
+        copy.wait()
+    for layer in range(4):
+        values = terms[layer].astype(F32)
+        vectors[layer, 0:1, :] = values[0:1, :] + (values[1:2, :] + values[2:3, :])
+        vectors[layer, 1:2, :] = values[3:4, :] + (values[4:5, :] + values[5:6, :])
     for row in range(4):
         rows = slice(row * 256, (row + 1) * 256)
-        gate, _ = gated(held, vectors, 3, rows)
+        gate, _ = gated(held, 3, vectors, 3, rows)
         block[...] = ups[rows, :].astype(F32) * gate
         spread(block, chunks, row)
     out[:, 4] = chunks[...].astype(BF).reshape(64, 16, 128)
@@ -118,6 +125,8 @@
 
 def column_kernel(layer, received, own, left, right, across, *rest):
     columns, rest = (rest[:3], rest[3:]) if layer == 0 else ((), rest)
+    if layer == 0:
+        columns = columns[:2] + (columns[2].at[:, 4],)
     out, (grads, back, weights, got, sems) = rest[0], rest[-5:]
     picked = rest[1:-5]
     index = lax.axis_index("segment")
@@ -164,36 +173,49 @@
             out[col] = part if step == 0 else out[col] + part
 
 
-def row_kernel(layer, received, own, left, right, across, upstream, held, vectors, *rest):
-    slots, rest = rest[:4], rest[4:]
+def row_kernel(layer, received, upstream, held, vectors, own, left, right, across, *rest):
+    slots, rest = (rest[:4], rest[4:]) if layer == 3 else (rest[0], rest[1:])
     earlier, rest = ((None,) + rest[:3], rest[3:]) if layer == 0 else ((), rest)
     outs, rest = (rest[:4], rest[4:]) if layer == 0 else (rest[:2], rest[2:])
-    chunks, mixed_chunks, block, mixed_block, next_chunks, vector, weights, inputs, ups, mixed, got, sems = rest
+    kept, rest = (rest[:3], rest[3:]) if layer == 3 else ((), rest)
+    chunks, mixed_chunks, block, mixed_block, next_chunks, weights = rest[:6]
+    sems = rest[-1]
     index = lax.axis_index("segment")
     factors = (own, left, right, across)
-    pairs = [(received, got), (upstream, ups), (vectors, vector), (held.at[layer], inputs.at[layer])]
-    if layer > 0:
-        pairs.append((held.at[layer - 1], inputs.at[layer - 1]))
-    copies = moves(pairs, sems)
-    choose("start", slots, (0, 3, 2, 1), layer, mixed, sems.at[5])
-    choose("start", factors, RING, layer, weights, sems.at[6])
-    if layer == 0:
-        for step in range(4):
-            pick("start", earlier, step, outs[step], sems.at[7 + step])
-    copies[0].wait()
-    chunks[...] = got[...].reshape(1024, 128).astype(F32)
-    choose("wait", slots, (0, 3, 2, 1), layer, mixed, sems.at[5])
-    mixed_chunks[...] = mixed[...].reshape(1024, 128).astype(F32)
-    choose("wait", factors, RING, layer, weights, sems.at[6])
-    for copy in copies[1:]:
-        copy.wait()
+    choose("start", factors, RING, layer, weights, sems.at[0])
+    place = layer
+    if layer in (3, 0):
+        got, ups = rest[6:8]
+        pairs = [(received, got), (upstream, ups)]
+        if layer == 3:
+            mixed, inputs, vector = kept
+            for step, part in enumerate(slots):
+                pairs.append((part, mixed.at[(index + 4 - step) % 4]))
+            pairs += [(held, inputs), (vectors, vector)]
+        else:
+            place = 0
+            mixed, inputs, vector = rest[8:11]
+            pairs += [(slots.at[0:1], mixed), (held.at[0:1], inputs), (vectors, vector)]
+        copies = moves(pairs, sems.at[5:])
+        for step in range(len(earlier)):
+            pick("start", earlier, step, outs[step], sems.at[1 + step])
+        copies[0].wait()
+        received, upstream, held, vectors = got, ups, inputs, vector
+    else:
+        mixed = slots
+    chunks[...] = received[...].reshape(1024, 128).astype(F32)
+    if layer in (3, 0):
+        for copy in copies[1:]:
+            copy.wait()
+    mixed_chunks[...] = mixed[place].reshape(1024, 128).astype(F32)
+    choose("wait", factors, RING, layer, weights, sems.at[0])
     for row in range(4):
         rows = slice(row * 256, (row + 1) * 256)
         collect(chunks, block, row)
         collect(mixed_chunks, mixed_block, row)
         through = dot_first(weights[row], block[...].astype(BF))
-        up = ups[rows, :].astype(F32)
-        gate, scale = gated(inputs, vector, layer, rows)
+        up = upstream[rows, :].astype(F32)
+        gate, scale = gated(held, place, vectors, layer, rows)
         slope = (up * gate * (1.0 - gate)).astype(BF).astype(F32)
         gate_grad = (slope * mixed_block[...]).astype(BF).astype(F32)
         result = (up + through + gate_grad * scale).astype(BF)
@@ -204,14 +226,18 @@
                     outs[step][rows, :] = result
         else:
             outs[0][rows, :] = result
-            gate, _ = gated(inputs, vector, layer - 1, rows)
+            gate, _ = gated(held, place - 1, vectors, layer - 1, rows)
             block[...] = result.astype(F32) * gate
             spread(block, next_chunks, row)
     if layer > 0:
         outs[1][...] = next_chunks[...].astype(BF).reshape(64, 16, 128)
     else:
         for step in range(4):
-            pick("wait", earlier, step, outs[step], sems.at[7 + step])
+            pick("wait", earlier, step, outs[step], sems.at[1 + step])
+
+
+def middle_kernel(layer, received, upstream, held, vectors, mixed, own, left, right, across, *rest):
+    row_kernel(layer, received, upstream, held, vectors, own, left, right, across, mixed, *rest)
 
 
 def final_kernel(own, near, far, last, out):
@@ -225,12 +251,12 @@
 ANYWHERE = pl.BlockSpec(memory_space=pl.ANY)
 
 
-def call(kernel, count, out_shapes, scratch, flops, copies=0, grant=VMEM_LIMIT):
+def call(kernel, count, out_shapes, scratch, flops, anywhere=0, copies=0, grant=VMEM_LIMIT):
     outs = [jax.ShapeDtypeStruct(s, d) for s, d in out_shapes]
     single = len(outs) == 1
     return pl.pallas_call(
         kernel,
-        in_specs=[ANYWHERE if copies else IN_VMEM] * count,
+        in_specs=[IN_VMEM] * (count - anywhere) + [ANYWHERE] * anywhere,
         out_shape=outs[0] if single else outs,
         out_specs=IN_VMEM if single else [IN_VMEM] * len(outs),
         scratch_shapes=[pltpu.VMEM(*s) if isinstance(s[0], tuple) else pltpu.VMEM(s, F32) for s in scratch]
@@ -266,6 +292,7 @@
         [((1040, 128), BF)] * 4 + [(TALL, BF)],
         [(2, 512), (16, 128)],
         1 << 20,
+        anywhere=4,
         copies=7,
         grant=LARGE_LIMIT,
     )(layer_inputs[0], gate_scale, gate_shift, top_grads)
@@ -274,26 +301,30 @@
         first_kernel,
         2,
         [((64, 4, 16, 128), BF)],
-        [BLOCK, TALL, FACTOR, ((1024, 512), BF)],
+        [BLOCK, TALL, FACTOR, ((4, 256, 512), BF)],
         4 * FLOPS,
-        copies=2,
+        anywhere=2,
+        copies=8,
         grant=LARGE_LIMIT,
-    )(firsts, layer_inputs[0])
+    )(firsts, layer_inputs[0].reshape(4, 256, 512))
     firsts_cols = lax.all_to_all(firsts_out, "seq", 0, 0, tiled=True)
-    firsts_cols, parts, firsts, seconds = lax.optimization_barrier((firsts_cols, parts, firsts, seconds))
+    seconds_all = [seconds, passed(seconds, 1), passed(seconds, 3)]
+    firsts_cols, parts, firsts, seconds_all = lax.optimization_barrier(
+        (firsts_cols, parts, firsts, seconds_all)
+    )
     payload, held, vectors = call(
         gate_kernel,
         7,
         [((64, 5, 16, 128), BF), ((4, 1024, 128), BF), ((4, 2, 128), F32)],
         [BLOCK, TALL, TALL, TALL, FACTOR, ((64, 4, 16, 128), BF), (TALL, BF), ((4, 16, 128), BF)],
         4 * FLOPS,
+        anywhere=7,
         copies=11,
         grant=LARGE_LIMIT,
-    )(seconds, firsts_cols, upstream, *parts)
+    )(seconds_all[0], firsts_cols, upstream, *parts)
     columns = [None] * 4
     columns[3] = lax.all_to_all(payload, "seq", 0, 0, tiled=True)
     firsts_all = [firsts, passed(firsts, 1), passed(firsts, 3)]
-    seconds_all = [seconds, passed(seconds, 1), passed(seconds, 3)]
     firsts_all.append(passed(firsts_all[2], 3))
     seconds_all.append(passed(seconds_all[1], 1))
     columns[3], firsts_all, seconds_all = lax.optimization_barrier((columns[3], firsts_all, seconds_all))
@@ -303,34 +334,47 @@
         grant = LARGE_LIMIT if l in (3, 0) else VMEM_LIMIT
         if l < 3:
             columns[l] = lax.all_to_all(sends, "seq", 0, 0, tiled=True)
-        operands = [columns[l], *seconds_all] + (columns[1:3] + [grads_three] if l == 0 else [])
+        operands = [columns[l], *seconds_all] + (columns[1:] if l == 0 else [])
         made = call(
             functools.partial(column_kernel, l),
             len(operands),
             [(CHUNKS, BF)] * (5 if l in (3, 0) else 1),
             [TALL, TALL, FACTOR, (CHUNKS, BF)],
             FLOPS,
+            anywhere=len(operands),
             copies=6,
-            grant=grant,
+            grant=LARGE_LIMIT if l == 3 else VMEM_LIMIT,
         )(*operands)
         back = made[0] if l in (3, 0) else made
         received = lax.all_to_all(back, "seq", 0, 0, tiled=True)
         if l == 3:
             mixed = exchanged(made[1:])
-            grads_three = columns[3][:, 4]
         if l == 0:
             grads = exchanged(made[1:])
-        operands = [received, *firsts_all, upstream, held, vectors, *mixed] + (results[1:] if l == 0 else [])
+        operands = [received, upstream, held, vectors, *firsts_all]
+        operands += (mixed if l == 3 else [mixed]) + (results[1:] if l == 0 else [])
+        outs = [(TALL, BF), (CHUNKS, BF)] if l > 0 else [(TALL, BF)] * 4
+        scratch = [TALL, TALL, BLOCK, BLOCK, TALL, FACTOR]
+        if l in (3, 0):
+            scratch += [(CHUNKS, BF), (TALL, BF)]
+        if l == 3:
+            outs += [((4,) + CHUNKS, BF), ((4, 1024, 128), BF), ((4, 2, 128), F32)]
+        if l == 0:
+            scratch += [((1,) + CHUNKS, BF), ((1, 1024, 128), BF), (4, 2, 128)]
+        order = [0, 1, 2, 3] + [8] * (l in (2, 1)) + [4, 5, 6, 7] + list(range(8 + (l in (2, 1)), len(operands)))
         made = call(
-            functools.partial(row_kernel, l),
+            functools.partial(row_kernel, l) if l in (3, 0) else functools.partial(middle_kernel, l),
             len(operands),
-            [(TALL, BF), (CHUNKS, BF)] if l > 0 else [(TALL, BF)] * 4,
-            [TALL, TALL, BLOCK, BLOCK, TALL, (4, 2, 128)]
-            + [FACTOR, ((4, 1024, 128), BF), (TALL, BF), (CHUNKS, BF), (CHUNKS, BF)],
+            outs,
+            scratch,
             FLOPS,
-            copies=11,
+            anywhere=len(operands) if l in (3, 0) else 4,
+            copies=14,
             grant=grant,
-        )(*operands)
+        )(*[operands[i] for i in order])
+        if l == 3:
+            mixed, held, vectors = made[2:]
+            made = made[:2]
         if l > 0:
             upstream, sends = made
             results[l] = upstream

time: 279 us -> 269 us (0.964)
  blocking collectives: 77.9 us -> 95.6 us
  waiting for transfers between devices: 93.5 us -> 80.9 us
  starting transfers between devices: 64.4 us -> 55.2 us
  local copies, waits for them, and re-layouts: 10.2 us -> 5.49 us
    all_to_all x2 -> x3, blocking collectives: 42.5 us -> 60.2 us  [body(): columns[l] = lax.all_to_all(sends, 'seq', 0, 0, tiled=True)]
    all_to_all x1 -> x0, waiting for transfers between devices: 11.5 us -> none  [body(): columns[l] = lax.all_to_all(sends, 'seq', 0, 0, tiled=True)]
    all_to_all x1, waiting for transfers between devices: 9.81 us -> 0.93 us  [body(): firsts_cols = lax.all_to_all(firsts_out, 'seq', 0, 0, tiled=True)]
    all_to_all x1, waiting for transfers between devices: 0.01 us -> 7.1 us  [body(): columns[3] = lax.all_to_all(payload, 'seq', 0, 0, tiled=True)]
    all_to_all x2, starting transfers between devices: 16.4 us -> 11.1 us  [body(): received = lax.all_to_all(back, 'seq', 0, 0, tiled=True)]
    all_to_all x1, starting transfers between devices: 6.77 us -> 11.9 us  [body(): columns[3] = lax.all_to_all(payload, 'seq', 0, 0, tiled=True)]
    all_to_all x1 -> x0, starting transfers between devices: 4.93 us -> none  [body(): columns[l] = lax.all_to_all(sends, 'seq', 0, 0, tiled=True)]
    ppermute x18, starting transfers between devices: 23.1 us -> 19 us  [passed(): lax.ppermute(value, 'segment', [(i, (i + step) % 4) for i in range(4)])]
  transfers between devices with their start and end apart: 23 -> 22, of which waited for: 14 -> 11; matrix products, arithmetic and copies ran while one was open for 1% -> 0% of each run, Pallas kernels for 3% -> 3%
where the time goes in v3:
time: 269 us; the launch traced here: 268 us
  blocking collectives  95.6 us (36%)
  waiting for transfers between devices  80.9 us (30%)
  starting transfers between devices  55.2 us (21%)
  Pallas kernels  29.9 us (11%)
  local copies, waits for them, and re-layouts  5.49 us (2%)
    ppermute x18, waiting for transfers between devices, passed(): lax.ppermute(value, 'segment', [(i, (i + step) % 4) for i in range(4)])  63.1 us
    all_to_all x3, blocking collectives, body(): columns[l] = lax.all_to_all(sends, 'seq', 0, 0, tiled=True)  60.2 us
    all_to_all x2, blocking collectives, body(): received = lax.all_to_all(back, 'seq', 0, 0, tiled=True)  35.5 us
    ppermute x18, starting transfers between devices, passed(): lax.ppermute(value, 'segment', [(i, (i + step) % 4) for i in range(4)])  19 us
    all_to_all x1, starting transfers between devices, body(): firsts_cols = lax.all_to_all(firsts_out, 'seq', 0, 0, tiled=True)  13.3 us
    all_to_all x1, starting transfers between devices, body(): columns[3] = lax.all_to_all(payload, 'seq', 0, 0, tiled=True)  11.9 us
    pallas_call x4, Pallas kernels, body(): call(functools.partial(row_kernel, l) if l in (3, 0) else functools.parti...  11.8 us
    all_to_all x2, starting transfers between devices, body(): received = lax.all_to_all(back, 'seq', 0, 0, tiled=True)  11.1 us
  transfers between devices with their start and end apart: 22, of which 11 were waited for; matrix products, arithmetic and copies ran while one was open for 0% of the time, Pallas kernels for 3%

profile of v3, /device:TPU:1, one launch (start us, length us, event | category | flops | bytes accessed | tf_op | source)
XLA Modules:
  0.0 268.2 jit_solution(5485226074077702326)
XLA Ops:
  0.6 3.7 %shard_map.77 = bf16[64,4,16,128]{3,2,1,0:T(8,128)(2,1)} custom-call(bf16[4,256,256]{2,1,0:T(8,128)(2,1)} %bitcast.13, bf16[4,256,512]{2,1,0:T(8,128)(2,1)} %bitcast.20), custom_call_target="tpu_custom_call" | custom-call | flops 268435456 | bytes 2097152 | tf_op jit(solution)/shard_map/pallas_call | solution.py:300
  4.4 13.3 %all-to-all-start = ((bf16[64,4,16,128]{3,2,1,0:T(8,128)(2,1)}), bf16[64,4,16,128]{3,2,1,0:T(8,128)(2,1)S(1)}, u32[]{:S(2)}, u32[]{:S(2)}) async-start(bf16[64,4,16,128]{3,2,1,0:T(8,128)(2,1)} %shard_map.77), calls=%async_computation | async-start | bytes 2097152 | tf_op jit(solution)/shard_map/all_to_all | solution.py:310
  23.0 3.7 %collective-permute-start.1 = (bf16[1040,128]{1,0:T(8,128)(2,1)}, bf16[1040,128]{1,0:T(8,128)(2,1)S(1)}, u32[]{:S(2)}, u32[]{:S(2)}) collective-permute-start(bf16[1040,128]{1,0:T(8,128)(2,1)} %get-tuple-element.53), channel_id=1, source_target_pairs={{0,128},{64,192},{128,0},{192,64},{1,129},{65,193},{129,1},{193,65... | collective-permute-start | bytes 798728 | tf_op jit(solution)/shard_map/ppermute | solution.py:280
  26.7 14.2 %collective-permute-done.near = bf16[1040,128]{1,0:T(8,128)(2,1)S(1)} collective-permute-done((bf16[1040,128]{1,0:T(8,128)(2,1)}, bf16[1040,128]{1,0:T(8,128)(2,1)S(1)}, u32[]{:S(2)}, u32[]{:S(2)}) %collective-permute-start) | collective-permute-done | bytes 266272 | tf_op jit(solution)/shard_map/ppermute | solution.py:280
  40.8 3.9 %collective-permute-done.1.far = bf16[1040,128]{1,0:T(8,128)(2,1)S(1)} collective-permute-done((bf16[1040,128]{1,0:T(8,128)(2,1)}, bf16[1040,128]{1,0:T(8,128)(2,1)S(1)}, u32[]{:S(2)}, u32[]{:S(2)}) %collective-permute-start.1) | collective-permute-done | bytes 266272 | tf_op jit(solution)/shard_map/ppermute | solution.py:280
  46.7 3.8 %shard_map.79 = (bf16[64,5,16,128]{3,2,1,0:T(8,128)(2,1)}, bf16[4,1024,128]{2,1,0:T(8,128)(2,1)}, f32[4,2,128]{2,1,0:T(2,128)}) custom-call(bf16[4,256,256]{2,1,0:T(8,128)(2,1)} %bitcast.6, bf16[64,4,16,128]{3,2,1,0:T(8,128)(2,1)} %copy-done.6, bf16[1024,128]{1,0:T(8,128)(2,1)} %get-tuple-element.57.upstream, bf16[1040,128]{1,0:T(8,128)(2,1)} %get-tuple-element.58.own, ...), custom_call_target="tpu_custom_call" | custom-call | flops 268435456 | bytes 2097152 | tf_op jit(solution)/shard_map/pallas_call | solution.py:315
  50.5 11.9 %all-to-all-start.1 = ((bf16[64,5,16,128]{3,2,1,0:T(8,128)(2,1)}), bf16[64,5,16,128]{3,2,1,0:T(8,128)(2,1)S(1)}, u32[]{:S(2)}, u32[]{:S(2)}) async-start(bf16[64,5,16,128]{3,2,1,0:T(8,128)(2,1)} %get-tuple-element.62), calls=%async_computation.1 | async-start | bytes 2621440 | tf_op jit(solution)/shard_map/all_to_all | solution.py:326
  64.0 11.5 %collective-permute-done.6.right = bf16[4,256,256]{2,1,0:T(8,128)(2,1)S(1)} collective-permute-done((bf16[4,256,256]{2,1,0:T(8,128)(2,1)S(1)}, bf16[4,256,256]{2,1,0:T(8,128)(2,1)S(1)}, u32[]{:S(2)}, u32[]{:S(2)}) %collective-permute-start.6) | collective-permute-done | bytes 524320 | tf_op jit(solution)/shard_map/ppermute | solution.py:280
  76.9 11.1 %collective-permute-done.8.across = bf16[4,256,256]{2,1,0:T(8,128)(2,1)S(1)} collective-permute-done((bf16[4,256,256]{2,1,0:T(8,128)(2,1)S(1)}, bf16[4,256,256]{2,1,0:T(8,128)(2,1)S(1)}, u32[]{:S(2)}, u32[]{:S(2)}) %collective-permute-start.8) | collective-permute-done | bytes 524320 | tf_op jit(solution)/shard_map/ppermute | solution.py:280
  88.9 7.1 %all-to-all-done.1.received.rest_2_ = bf16[64,5,16,128]{3,2,1,0:T(8,128)(2,1)S(1)} async-done(((bf16[64,5,16,128]{3,2,1,0:T(8,128)(2,1)}), bf16[64,5,16,128]{3,2,1,0:T(8,128)(2,1)S(1)}, u32[]{:S(2)}, u32[]{:S(2)}) %all-to-all-start.1) | async-done | bytes 1310752 | tf_op jit(solution)/shard_map/all_to_all | solution.py:326
  99.8 6.3 %all-to-all-start.2 = ((bf16[64,16,128]{2,1,0:T(8,128)(2,1)}), bf16[64,16,128]{2,1,0:T(8,128)(2,1)S(1)}, u32[]{:S(2)}, u32[]{:S(2)}) async-start(bf16[64,16,128]{2,1,0:T(8,128)(2,1)} %get-tuple-element.71), calls=%async_computation.2 | async-start | bytes 524288 | tf_op jit(solution)/shard_map/all_to_all | solution.py:349
  108.9 11.8 %collective-permute-done.9.rest_1_ = bf16[64,16,128]{2,1,0:T(8,128)(2,1)S(1)} collective-permute-done((bf16[64,16,128]{2,1,0:T(8,128)(2,1)}, bf16[64,16,128]{2,1,0:T(8,128)(2,1)S(1)}, u32[]{:S(2)}, u32[]{:S(2)}) %collective-permute-start.9) | collective-permute-done | bytes 262176 | tf_op jit(solution)/shard_map/ppermute | solution.py:280
  121.9 4.4 %shard_map.81 = (bf16[1024,128]{1,0:T(8,128)(2,1)}, bf16[64,16,128]{2,1,0:T(8,128)(2,1)}, bf16[4,64,16,128]{3,2,1,0:T(8,128)(2,1)}, bf16[4,1024,128]{2,1,0:T(8,128)(2,1)}, f32[4,2,128]{2,1,0:T(2,128)}) custom-call(bf16[64,16,128]{2,1,0:T(8,128)(2,1)} %copy-done.26, bf16[1024,128]{1,0:T(8,128)(2,1)} %get-tuple-element.57.upstream, ...), custom_call_target="tpu_custom_call" | custom-call | flops 67108864 | bytes 2097152 | tf_op jit(solution)/shard_map/pallas_call | solution.py:365
  126.3 24.8 %all_to_all.45.received.rest_1_ = bf16[64,16,128]{2,1,0:T(8,128)(2,1)S(1)} all-to-all(bf16[64,16,128]{2,1,0:T(8,128)(2,1)} %get-tuple-element.82), channel_id=1, replica_groups=mesh['segment'=4,'seq'=64] {'seq'}, dimensions={0} | all-to-all | bytes 524288 | tf_op jit(solution)/shard_map/all_to_all | solution.py:336
  151.8 17.8 %all_to_all.46.received = bf16[64,16,128]{2,1,0:T(8,128)(2,1)S(1)} all-to-all(bf16[64,16,128]{2,1,0:T(8,128)(2,1)S(1)} %shard_map.82), channel_id=1, replica_groups=mesh['segment'=4,'seq'=64] {'seq'}, dimensions={0} | all-to-all | bytes 524288 | tf_op jit(solution)/shard_map/all_to_all | solution.py:349
  172.9 17.7 %all_to_all.47.received.rest_0_ = bf16[64,16,128]{2,1,0:T(8,128)(2,1)S(1)} all-to-all(bf16[64,16,128]{2,1,0:T(8,128)(2,1)S(1)} %get-tuple-element.87), channel_id=1, replica_groups=mesh['segment'=4,'seq'=64] {'seq'}, dimensions={0} | all-to-all | bytes 524288 | tf_op jit(solution)/shard_map/all_to_all | solution.py:336
  191.1 17.7 %all_to_all.48.received = bf16[64,16,128]{2,1,0:T(8,128)(2,1)S(1)} all-to-all(bf16[64,16,128]{2,1,0:T(8,128)(2,1)S(1)} %shard_map.84), channel_id=1, replica_groups=mesh['segment'=4,'seq'=64] {'seq'}, dimensions={0} | all-to-all | bytes 524288 | tf_op jit(solution)/shard_map/all_to_all | solution.py:349
  210.2 17.7 %all_to_all.49.received = bf16[64,16,128]{2,1,0:T(8,128)(2,1)S(1)} all-to-all(bf16[64,16,128]{2,1,0:T(8,128)(2,1)S(1)} %get-tuple-element.89), channel_id=1, replica_groups=mesh['segment'=4,'seq'=64] {'seq'}, dimensions={0} | all-to-all | bytes 524288 | tf_op jit(solution)/shard_map/all_to_all | solution.py:336
  229.3 4.7 %all-to-all-start.8 = ((bf16[64,16,128]{2,1,0:T(8,128)(2,1)}), bf16[64,16,128]{2,1,0:T(8,128)(2,1)S(1)}, u32[]{:S(2)}, u32[]{:S(2)}) async-start(bf16[64,16,128]{2,1,0:T(8,128)(2,1)} %get-tuple-element.90), calls=%async_computation.8 | async-start | bytes 524288 | tf_op jit(solution)/shard_map/all_to_all | solution.py:349
  237.4 9.8 %all-to-all-done.8.received = bf16[64,16,128]{2,1,0:T(8,128)(2,1)S(1)} async-done(((bf16[64,16,128]{2,1,0:T(8,128)(2,1)}), bf16[64,16,128]{2,1,0:T(8,128)(2,1)S(1)}, u32[]{:S(2)}, u32[]{:S(2)}) %all-to-all-start.8) | async-done | bytes 262176 | tf_op jit(solution)/shard_map/all_to_all | solution.py:349
  247.9 3.7 %shard_map.87 = (bf16[1024,128]{1,0:T(8,128)(2,1)}, bf16[1024,128]{1,0:T(8,128)(2,1)}, bf16[1024,128]{1,0:T(8,128)(2,1)}, bf16[1024,128]{1,0:T(8,128)(2,1)}) custom-call(bf16[64,16,128]{2,1,0:T(8,128)(2,1)} %copy-done.25, bf16[1024,128]{1,0:T(8,128)(2,1)} %copy-done.20, bf16[4,1024,128]{2,1,0:T(8,128)(2,1)} %get-tuple-element.84.held, ...), custom_call_target="tpu_custom_call" | custom-call | flops 67108864 | bytes 2097152 | tf_op jit(solution)/shard_map/pallas_call | solution.py:365
  251.7 3.3 %collective-permute-start.13 = (bf16[1024,128]{1,0:T(8,128)(2,1)}, bf16[1024,128]{1,0:T(8,128)(2,1)S(1)}, u32[]{:S(2)}, u32[]{:S(2)}) collective-permute-start(bf16[1024,128]{1,0:T(8,128)(2,1)} %get-tuple-element.94), channel_id=1, source_target_pairs={{0,128},{64,192},{128,0},{192,64},{1,129},{65,193},{129,1},{193,65... | collective-permute-start | bytes 786440 | tf_op jit(solution)/shard_map/ppermute | solution.py:280
  256.7 4.0 %collective-permute-done.12.near = bf16[1024,128]{1,0:T(8,128)(2,1)S(1)} collective-permute-done((bf16[1024,128]{1,0:T(8,128)(2,1)}, bf16[1024,128]{1,0:T(8,128)(2,1)S(1)}, u32[]{:S(2)}, u32[]{:S(2)}) %collective-permute-start.12) | collective-permute-done | bytes 262176 | tf_op jit(solution)/shard_map/ppermute | solution.py:280
  260.7 6.3 %collective-permute-done.13.far = bf16[1024,128]{1,0:T(8,128)(2,1)S(1)} collective-permute-done((bf16[1024,128]{1,0:T(8,128)(2,1)}, bf16[1024,128]{1,0:T(8,128)(2,1)S(1)}, u32[]{:S(2)}, u32[]{:S(2)}) %collective-permute-start.13) | collective-permute-done | bytes 262176 | tf_op jit(solution)/shard_map/ppermute | solution.py:280
  (104 shorter events, 33.0 us)
Async XLA Ops:
  4.4 41.3 %all-to-all-start = ((bf16[64,4,16,128]{3,2,1,0:T(8,128)(2,1)}), bf16[64,4,16,128]{3,2,1,0:T(8,128)(2,1)S(1)}, u32[]{:S(2)}, u32[]{:S(2)}) async-start(bf16[64,4,16,128]{3,2,1,0:T(8,128)(2,1)} %shard_map.77), calls=%async_computation | async-start | bytes 2097152 | tf_op jit(solution)/shard_map/all_to_all | solution.py:310
  17.7 27.0 %collective-permute-start.4 = (bf16[4,256,256]{2,1,0:T(8,128)(2,1)S(1)}, bf16[4,256,256]{2,1,0:T(8,128)(2,1)S(1)}, u32[]{:S(2)}, u32[]{:S(2)}) collective-permute-start(bf16[4,256,256]{2,1,0:T(8,128)(2,1)S(1)} %bitcast.8), channel_id=1, source_target_pairs={{0,192},{64,0},{128,64},{192,128},{1,193},{65,1},{129,65},{193,129... | collective-permute-start | bytes 1572872 | tf_op jit(solution)/shard_map/ppermute | solution.py:280
  20.3 24.5 %collective-permute-start.3 = (bf16[4,256,256]{2,1,0:T(8,128)(2,1)S(1)}, bf16[4,256,256]{2,1,0:T(8,128)(2,1)S(1)}, u32[]{:S(2)}, u32[]{:S(2)}) collective-permute-start(bf16[4,256,256]{2,1,0:T(8,128)(2,1)S(1)} %bitcast.9), channel_id=1, source_target_pairs={{0,64},{64,128},{128,192},{192,0},{1,65},{65,129},{129,193},{193,1... | collective-permute-start | bytes 1572872 | tf_op jit(solution)/shard_map/ppermute | solution.py:280
  22.7 18.1 %collective-permute-start = (bf16[1040,128]{1,0:T(8,128)(2,1)}, bf16[1040,128]{1,0:T(8,128)(2,1)S(1)}, u32[]{:S(2)}, u32[]{:S(2)}) collective-permute-start(bf16[1040,128]{1,0:T(8,128)(2,1)} %get-tuple-element.52), channel_id=1, source_target_pairs={{0,64},{64,128},{128,192},{192,0},{1,65},{65,129},{129,193},{193,1... | collective-permute-start | bytes 798728 | tf_op jit(solution)/shard_map/ppermute | solution.py:280
  23.0 21.7 %collective-permute-start.1 = (bf16[1040,128]{1,0:T(8,128)(2,1)}, bf16[1040,128]{1,0:T(8,128)(2,1)S(1)}, u32[]{:S(2)}, u32[]{:S(2)}) collective-permute-start(bf16[1040,128]{1,0:T(8,128)(2,1)} %get-tuple-element.53), channel_id=1, source_target_pairs={{0,128},{64,192},{128,0},{192,64},{1,129},{65,193},{129,1},{193,65... | collective-permute-start | bytes 798728 | tf_op jit(solution)/shard_map/ppermute | solution.py:280
  26.7 18.1 %collective-permute-start.2 = (bf16[1040,128]{1,0:T(8,128)(2,1)}, bf16[1040,128]{1,0:T(8,128)(2,1)S(1)}, u32[]{:S(2)}, u32[]{:S(2)}) collective-permute-start(bf16[1040,128]{1,0:T(8,128)(2,1)} %get-tuple-element.54), channel_id=1, source_target_pairs={{0,192},{64,0},{128,64},{192,128},{1,193},{65,1},{129,65},{193,129... | collective-permute-start | bytes 798728 | tf_op jit(solution)/shard_map/ppermute | solution.py:280
  44.7 51.2 %copy-start.10 = (bf16[4,256,256]{2,1,0:T(8,128)(2,1)}, bf16[4,256,256]{2,1,0:T(8,128)(2,1)S(1)}, u32[]{:S(2)}) copy-start(bf16[4,256,256]{2,1,0:T(8,128)(2,1)S(1)} %collective-permute-done.4.right) | copy-start | bytes 1572868
  44.7 51.2 %copy-start.12 = (bf16[4,256,256]{2,1,0:T(8,128)(2,1)}, bf16[4,256,256]{2,1,0:T(8,128)(2,1)S(1)}, u32[]{:S(2)}) copy-start(bf16[4,256,256]{2,1,0:T(8,128)(2,1)S(1)} %collective-permute-done.3.left) | copy-start | bytes 1572868
  50.5 45.5 %all-to-all-start.1 = ((bf16[64,5,16,128]{3,2,1,0:T(8,128)(2,1)}), bf16[64,5,16,128]{3,2,1,0:T(8,128)(2,1)S(1)}, u32[]{:S(2)}, u32[]{:S(2)}) async-start(bf16[64,5,16,128]{3,2,1,0:T(8,128)(2,1)} %get-tuple-element.62), calls=%async_computation.1 | async-start | bytes 2621440 | tf_op jit(solution)/shard_map/all_to_all | solution.py:326
  62.4 13.1 %collective-permute-start.6 = (bf16[4,256,256]{2,1,0:T(8,128)(2,1)S(1)}, bf16[4,256,256]{2,1,0:T(8,128)(2,1)S(1)}, u32[]{:S(2)}, u32[]{:S(2)}) collective-permute-start(bf16[4,256,256]{2,1,0:T(8,128)(2,1)S(1)} %bitcast.16), channel_id=1, source_target_pairs={{0,192},{64,0},{128,64},{192,128},{1,193},{65,1},{129,65},{193,129... | collective-permute-start | bytes 1572872 | tf_op jit(solution)/shard_map/ppermute | solution.py:280
  62.5 25.5 %collective-permute-start.5 = (bf16[4,256,256]{2,1,0:T(8,128)(2,1)S(1)}, bf16[4,256,256]{2,1,0:T(8,128)(2,1)S(1)}, u32[]{:S(2)}, u32[]{:S(2)}) collective-permute-start(bf16[4,256,256]{2,1,0:T(8,128)(2,1)S(1)} %bitcast.17), channel_id=1, source_target_pairs={{0,64},{64,128},{128,192},{192,0},{1,65},{65,129},{129,193},{193,1... | collective-permute-start | bytes 1572872 | tf_op jit(solution)/shard_map/ppermute | solution.py:280
  63.9 24.1 %collective-permute-start.8 = (bf16[4,256,256]{2,1,0:T(8,128)(2,1)S(1)}, bf16[4,256,256]{2,1,0:T(8,128)(2,1)S(1)}, u32[]{:S(2)}, u32[]{:S(2)}) collective-permute-start(bf16[4,256,256]{2,1,0:T(8,128)(2,1)S(1)} %collective-permute-done.3.left), channel_id=1, source_target_pairs={{0,64},{64,128},{128,192},{192,0},{1,65},{65,129},{129,193},{193,1... | collective-permute-start | bytes 1572872 | tf_op jit(solution)/shard_map/ppermute | solution.py:280
  75.5 13.4 %collective-permute-start.7 = (bf16[4,256,256]{2,1,0:T(8,128)(2,1)S(1)}, bf16[4,256,256]{2,1,0:T(8,128)(2,1)}, u32[]{:S(2)}, u32[]{:S(2)}) collective-permute-start(bf16[4,256,256]{2,1,0:T(8,128)(2,1)S(1)} %collective-permute-done.6.right), channel_id=1, source_target_pairs={{0,192},{64,0},{128,64},{192,128},{1,193},{65,1},{129,65},{193,129... | collective-permute-start | bytes 1572872 | tf_op jit(solution)/shard_map/ppermute | solution.py:280
  99.8 21.2 %all-to-all-start.2 = ((bf16[64,16,128]{2,1,0:T(8,128)(2,1)}), bf16[64,16,128]{2,1,0:T(8,128)(2,1)S(1)}, u32[]{:S(2)}, u32[]{:S(2)}) async-start(bf16[64,16,128]{2,1,0:T(8,128)(2,1)} %get-tuple-element.71), calls=%async_computation.2 | async-start | bytes 524288 | tf_op jit(solution)/shard_map/all_to_all | solution.py:349
  106.1 14.5 %collective-permute-start.9 = (bf16[64,16,128]{2,1,0:T(8,128)(2,1)}, bf16[64,16,128]{2,1,0:T(8,128)(2,1)S(1)}, u32[]{:S(2)}, u32[]{:S(2)}) collective-permute-start(bf16[64,16,128]{2,1,0:T(8,128)(2,1)} %get-tuple-element.79), channel_id=1, source_target_pairs={{0,64},{64,128},{128,192},{192,0},{1,65},{65,129},{129,193},{193,1... | collective-permute-start | bytes 786440 | tf_op jit(solution)/shard_map/ppermute | solution.py:280
  106.2 14.5 %collective-permute-start.10 = (bf16[64,16,128]{2,1,0:T(8,128)(2,1)}, bf16[64,16,128]{2,1,0:T(8,128)(2,1)S(1)}, u32[]{:S(2)}, u32[]{:S(2)}) collective-permute-start(bf16[64,16,128]{2,1,0:T(8,128)(2,1)} %get-tuple-element.80), channel_id=1, source_target_pairs={{0,128},{64,192},{128,0},{192,64},{1,129},{65,193},{129,1},{193,65... | collective-permute-start | bytes 786440 | tf_op jit(solution)/shard_map/ppermute | solution.py:280
  107.7 13.3 %collective-permute-start.11 = (bf16[64,16,128]{2,1,0:T(8,128)(2,1)}, bf16[64,16,128]{2,1,0:T(8,128)(2,1)S(1)}, u32[]{:S(2)}, u32[]{:S(2)}) collective-permute-start(bf16[64,16,128]{2,1,0:T(8,128)(2,1)} %get-tuple-element.81), channel_id=1, source_target_pairs={{0,192},{64,0},{128,64},{192,128},{1,193},{65,1},{129,65},{193,129... | collective-permute-start | bytes 786440 | tf_op jit(solution)/shard_map/ppermute | solution.py:280
  229.3 17.9 %all-to-all-start.8 = ((bf16[64,16,128]{2,1,0:T(8,128)(2,1)}), bf16[64,16,128]{2,1,0:T(8,128)(2,1)S(1)}, u32[]{:S(2)}, u32[]{:S(2)}) async-start(bf16[64,16,128]{2,1,0:T(8,128)(2,1)} %get-tuple-element.90), calls=%async_computation.8 | async-start | bytes 524288 | tf_op jit(solution)/shard_map/all_to_all | solution.py:349
  234.0 20.9 %collective-permute-start.15 = (bf16[64,16,128]{2,1,0:T(8,128)(2,1)S(1)}, bf16[64,16,128]{2,1,0:T(8,128)(2,1)S(1)}, u32[]{:S(2)}, u32[]{:S(2)}) collective-permute-start(bf16[64,16,128]{2,1,0:T(8,128)(2,1)S(1)} %get-tuple-element.97), channel_id=1, source_target_pairs={{0,64},{64,128},{128,192},{192,0},{1,65},{65,129},{129,193},{193,1... | collective-permute-start | bytes 786440 | tf_op jit(solution)/shard_map/ppermute | solution.py:280
  234.1 20.9 %collective-permute-start.16 = (bf16[64,16,128]{2,1,0:T(8,128)(2,1)S(1)}, bf16[64,16,128]{2,1,0:T(8,128)(2,1)S(1)}, u32[]{:S(2)}, u32[]{:S(2)}) collective-permute-start(bf16[64,16,128]{2,1,0:T(8,128)(2,1)S(1)} %get-tuple-element.98), channel_id=1, source_target_pairs={{0,128},{64,192},{128,0},{192,64},{1,129},{65,193},{129,1},{193,65... | collective-permute-start | bytes 786440 | tf_op jit(solution)/shard_map/ppermute | solution.py:280
  237.4 17.6 %collective-permute-start.17 = (bf16[64,16,128]{2,1,0:T(8,128)(2,1)S(1)}, bf16[64,16,128]{2,1,0:T(8,128)(2,1)S(1)}, u32[]{:S(2)}, u32[]{:S(2)}) collective-permute-start(bf16[64,16,128]{2,1,0:T(8,128)(2,1)S(1)} %get-tuple-element.99), channel_id=1, source_target_pairs={{0,192},{64,0},{128,64},{192,128},{1,193},{65,1},{129,65},{193,129... | collective-permute-start | bytes 786440 | tf_op jit(solution)/shard_map/ppermute | solution.py:280
  251.6 9.2 %collective-permute-start.12 = (bf16[1024,128]{1,0:T(8,128)(2,1)}, bf16[1024,128]{1,0:T(8,128)(2,1)S(1)}, u32[]{:S(2)}, u32[]{:S(2)}) collective-permute-start(bf16[1024,128]{1,0:T(8,128)(2,1)} %get-tuple-element.93), channel_id=1, source_target_pairs={{0,64},{64,128},{128,192},{192,0},{1,65},{65,129},{129,193},{193,1... | collective-permute-start | bytes 786440 | tf_op jit(solution)/shard_map/ppermute | solution.py:280
  251.7 15.3 %collective-permute-start.13 = (bf16[1024,128]{1,0:T(8,128)(2,1)}, bf16[1024,128]{1,0:T(8,128)(2,1)S(1)}, u32[]{:S(2)}, u32[]{:S(2)}) collective-permute-start(bf16[1024,128]{1,0:T(8,128)(2,1)} %get-tuple-element.94), channel_id=1, source_target_pairs={{0,128},{64,192},{128,0},{192,64},{1,129},{65,193},{129,1},{193,65... | collective-permute-start | bytes 786440 | tf_op jit(solution)/shard_map/ppermute | solution.py:280
  255.0 12.0 %collective-permute-start.14 = (bf16[1024,128]{1,0:T(8,128)(2,1)}, bf16[1024,128]{1,0:T(8,128)(2,1)S(1)}, u32[]{:S(2)}, u32[]{:S(2)}) collective-permute-start(bf16[1024,128]{1,0:T(8,128)(2,1)} %get-tuple-element.95), channel_id=1, source_target_pairs={{0,192},{64,0},{128,64},{192,128},{1,193},{65,1},{129,65},{193,129... | collective-permute-start | bytes 786440 | tf_op jit(solution)/shard_map/ppermute | solution.py:280
  (31 other events, 406.0 us)

commit v4 on v3

--- a/solution.py
+++ b/solution.py
@@ -72,20 +72,21 @@
         copy.wait()
 
 
-def first_kernel(firsts, inputs, out, block, chunks, weights, held, sems):
-    copies = moves(
-        [(firsts.at[row], weights.at[row]) for row in range(4)]
-        + [(inputs.at[row], held.at[row]) for row in range(4)],
-        sems,
-    )
+def first_kernel(firsts, inputs, out, block, chunks, weights, held, done, sems):
+    copies = moves([(firsts, weights), (inputs, held)], sems)
     for copy in copies:
         copy.wait()
+    written = []
     for part in range(4):
         lanes = slice(part * 128, (part + 1) * 128)
         for row in range(4):
             block[...] = dot(weights[row], held[row, :, lanes])
             spread(block, chunks, row)
-        out[:, part] = chunks[...].astype(BF).reshape(64, 16, 128)
+        done[part] = chunks[...].astype(BF).reshape(64, 16, 128)
+        written.append(pltpu.make_async_copy(done.at[part], out.at[:, part], sems.at[2 + part]))
+        written[-1].start()
+    for copy in written:
+        copy.wait()
 
 
 def gated(inputs, place, vectors, layer, rows):
@@ -251,14 +252,15 @@
 ANYWHERE = pl.BlockSpec(memory_space=pl.ANY)
 
 
-def call(kernel, count, out_shapes, scratch, flops, anywhere=0, copies=0, grant=VMEM_LIMIT):
+def call(kernel, count, out_shapes, scratch, flops, anywhere=0, copies=0, grant=VMEM_LIMIT, free=()):
     outs = [jax.ShapeDtypeStruct(s, d) for s, d in out_shapes]
     single = len(outs) == 1
+    specs = [ANYWHERE if i in free else IN_VMEM for i in range(len(outs))]
     return pl.pallas_call(
         kernel,
         in_specs=[IN_VMEM] * (count - anywhere) + [ANYWHERE] * anywhere,
         out_shape=outs[0] if single else outs,
-        out_specs=IN_VMEM if single else [IN_VMEM] * len(outs),
+        out_specs=specs[0] if single else specs,
         scratch_shapes=[pltpu.VMEM(*s) if isinstance(s[0], tuple) else pltpu.VMEM(s, F32) for s in scratch]
         + ([pltpu.SemaphoreType.DMA((copies,))] if copies else []),
         compiler_params=pltpu.CompilerParams(vmem_limit_bytes=grant),
@@ -301,16 +303,17 @@
         first_kernel,
         2,
         [((64, 4, 16, 128), BF)],
-        [BLOCK, TALL, FACTOR, ((4, 256, 512), BF)],
+        [BLOCK, TALL, FACTOR, ((4, 256, 512), BF), ((4, 64, 16, 128), BF)],
         4 * FLOPS,
         anywhere=2,
-        copies=8,
+        copies=6,
+        free=(0,),
         grant=LARGE_LIMIT,
     )(firsts, layer_inputs[0].reshape(4, 256, 512))
     firsts_cols = lax.all_to_all(firsts_out, "seq", 0, 0, tiled=True)
-    seconds_all = [seconds, passed(seconds, 1), passed(seconds, 3)]
-    firsts_cols, parts, firsts, seconds_all = lax.optimization_barrier(
-        (firsts_cols, parts, firsts, seconds_all)
+    right = passed(seconds, 3)
+    firsts_cols, parts, firsts, seconds, right = lax.optimization_barrier(
+        (firsts_cols, parts, firsts, seconds, right)
     )
     payload, held, vectors = call(
         gate_kernel,
@@ -321,12 +324,11 @@
         anywhere=7,
         copies=11,
         grant=LARGE_LIMIT,
-    )(seconds_all[0], firsts_cols, upstream, *parts)
+    )(seconds, firsts_cols, upstream, *parts)
     columns = [None] * 4
     columns[3] = lax.all_to_all(payload, "seq", 0, 0, tiled=True)
+    seconds_all = [seconds, passed(seconds, 1), right, passed(right, 3)]
     firsts_all = [firsts, passed(firsts, 1), passed(firsts, 3)]
-    firsts_all.append(passed(firsts_all[2], 3))
-    seconds_all.append(passed(seconds_all[1], 1))
     columns[3], firsts_all, seconds_all = lax.optimization_barrier((columns[3], firsts_all, seconds_all))
 
     results, mixed = [None] * 4, None
@@ -349,6 +351,7 @@
         received = lax.all_to_all(back, "seq", 0, 0, tiled=True)
         if l == 3:
             mixed = exchanged(made[1:])
+            firsts_all.append(passed(firsts_all[2], 3))
         if l == 0:
             grads = exchanged(made[1:])
         operands = [received, upstream, held, vectors, *firsts_all]

time: 269 us -> 268 us (level)
    ppermute x18, starting transfers between devices: 19 us -> 24.7 us  [passed(): lax.ppermute(value, 'segment', [(i, (i + step) % 4) for i in range(4)])]
    all_to_all x1, starting transfers between devices: 11.9 us -> 8.42 us  [body(): columns[3] = lax.all_to_all(payload, 'seq', 0, 0, tiled=True)]
    unnamed x66 -> x72, local copies, waits for them, and re-layouts: 5.49 us -> 3.66 us
  transfers between devices with their start and end apart: 22 -> 22, of which waited for: 11 -> 15; matrix products, arithmetic and copies ran while one was open for 0% -> 0% of each run, Pallas kernels for 3% -> 4%
where the time goes in v4:
time: 268 us; the launch traced here: 267 us
  blocking collectives  95.6 us (36%)
  waiting for transfers between devices  80.2 us (30%)
  starting transfers between devices  57.8 us (22%)
  Pallas kernels  28.6 us (11%)
  local copies, waits for them, and re-layouts  3.66 us (1%)
    ppermute x18, waiting for transfers between devices, passed(): lax.ppermute(value, 'segment', [(i, (i + step) % 4) for i in range(4)])  61.2 us
    all_to_all x3, blocking collectives, body(): columns[l] = lax.all_to_all(sends, 'seq', 0, 0, tiled=True)  60.2 us
    all_to_all x2, blocking collectives, body(): received = lax.all_to_all(back, 'seq', 0, 0, tiled=True)  35.5 us
    ppermute x18, starting transfers between devices, passed(): lax.ppermute(value, 'segment', [(i, (i + step) % 4) for i in range(4)])  24.7 us
    all_to_all x1, starting transfers between devices, body(): firsts_cols = lax.all_to_all(firsts_out, 'seq', 0, 0, tiled=True)  13.3 us
    all_to_all x2, starting transfers between devices, body(): received = lax.all_to_all(back, 'seq', 0, 0, tiled=True)  11.3 us
    pallas_call x4, Pallas kernels, body(): call(functools.partial(row_kernel, l) if l in (3, 0) else functools.parti...  10.9 us
    all_to_all x2, waiting for transfers between devices, body(): received = lax.all_to_all(back, 'seq', 0, 0, tiled=True)  8.94 us
  transfers between devices with their start and end apart: 22, of which 15 were waited for; matrix products, arithmetic and copies ran while one was open for 0% of the time, Pallas kernels for 4%

profile of v4, /device:TPU:1, one launch (start us, length us, event | category | flops | bytes accessed | tf_op | source)
XLA Modules:
  0.0 266.9 jit_solution(3657164064743590008)
XLA Ops:
  4.0 13.3 %all-to-all-start = ((bf16[64,4,16,128]{3,2,1,0:T(8,128)(2,1)}), bf16[64,4,16,128]{3,2,1,0:T(8,128)(2,1)S(1)}, u32[]{:S(2)}, u32[]{:S(2)}) async-start(bf16[64,4,16,128]{3,2,1,0:T(8,128)(2,1)} %shard_map.77), calls=%async_computation | async-start | bytes 2097152 | tf_op jit(solution)/shard_map/all_to_all | solution.py:313
  25.1 6.9 %collective-permute-done.near = bf16[1040,128]{1,0:T(8,128)(2,1)S(1)} collective-permute-done((bf16[1040,128]{1,0:T(8,128)(2,1)}, bf16[1040,128]{1,0:T(8,128)(2,1)S(1)}, u32[]{:S(2)}, u32[]{:S(2)}) %collective-permute-start) | collective-permute-done | bytes 266272 | tf_op jit(solution)/shard_map/ppermute | solution.py:282
  32.0 3.9 %collective-permute-done.1.far = bf16[1040,128]{1,0:T(8,128)(2,1)S(1)} collective-permute-done((bf16[1040,128]{1,0:T(8,128)(2,1)}, bf16[1040,128]{1,0:T(8,128)(2,1)S(1)}, u32[]{:S(2)}, u32[]{:S(2)}) %collective-permute-start.1) | collective-permute-done | bytes 266272 | tf_op jit(solution)/shard_map/ppermute | solution.py:282
  35.8 6.4 %collective-permute-done.2.last = bf16[1040,128]{1,0:T(8,128)(2,1)S(1)} collective-permute-done((bf16[1040,128]{1,0:T(8,128)(2,1)}, bf16[1040,128]{1,0:T(8,128)(2,1)S(1)}, u32[]{:S(2)}, u32[]{:S(2)}) %collective-permute-start.2) | collective-permute-done | bytes 266272 | tf_op jit(solution)/shard_map/ppermute | solution.py:282
  46.3 3.8 %shard_map.79 = (bf16[64,5,16,128]{3,2,1,0:T(8,128)(2,1)}, bf16[4,1024,128]{2,1,0:T(8,128)(2,1)}, f32[4,2,128]{2,1,0:T(2,128)}) custom-call(bf16[4,256,256]{2,1,0:T(8,128)(2,1)} %bitcast.6, bf16[64,4,16,128]{3,2,1,0:T(8,128)(2,1)} %copy-done.7, bf16[1024,128]{1,0:T(8,128)(2,1)} %get-tuple-element.55.upstream, bf16[1040,128]{1,0:T(8,128)(2,1)} %get-tuple-element.56.own, ...), custom_call_target="tpu_custom_call" | custom-call | flops 268435456 | bytes 2097152 | tf_op jit(solution)/shard_map/pallas_call | solution.py:318
  50.1 8.4 %all-to-all-start.1 = ((bf16[64,5,16,128]{3,2,1,0:T(8,128)(2,1)}), bf16[64,5,16,128]{3,2,1,0:T(8,128)(2,1)S(1)}, u32[]{:S(2)}, u32[]{:S(2)}) async-start(bf16[64,5,16,128]{3,2,1,0:T(8,128)(2,1)} %get-tuple-element.60), calls=%async_computation.1 | async-start | bytes 2621440 | tf_op jit(solution)/shard_map/all_to_all | solution.py:329
  63.5 9.4 %collective-permute-done.7.across = bf16[4,256,256]{2,1,0:T(8,128)(2,1)S(1)} collective-permute-done((bf16[4,256,256]{2,1,0:T(8,128)(2,1)S(1)}, bf16[4,256,256]{2,1,0:T(8,128)(2,1)S(1)}, u32[]{:S(2)}, u32[]{:S(2)}) %collective-permute-start.7) | collective-permute-done | bytes 524320 | tf_op jit(solution)/shard_map/ppermute | solution.py:282
  73.9 10.3 %collective-permute-done.5.right = bf16[4,256,256]{2,1,0:T(8,128)(2,1)S(1)} collective-permute-done((bf16[4,256,256]{2,1,0:T(8,128)(2,1)S(1)}, bf16[4,256,256]{2,1,0:T(8,128)(2,1)S(1)}, u32[]{:S(2)}, u32[]{:S(2)}) %collective-permute-start.5) | collective-permute-done | bytes 524320 | tf_op jit(solution)/shard_map/ppermute | solution.py:282
  85.2 7.0 %all-to-all-done.1.received.rest_2_ = bf16[64,5,16,128]{3,2,1,0:T(8,128)(2,1)S(1)} async-done(((bf16[64,5,16,128]{3,2,1,0:T(8,128)(2,1)}), bf16[64,5,16,128]{3,2,1,0:T(8,128)(2,1)S(1)}, u32[]{:S(2)}, u32[]{:S(2)}) %all-to-all-start.1) | async-done | bytes 1310752 | tf_op jit(solution)/shard_map/all_to_all | solution.py:329
  98.1 6.6 %all-to-all-start.2 = ((bf16[64,16,128]{2,1,0:T(8,128)(2,1)}), bf16[64,16,128]{2,1,0:T(8,128)(2,1)S(1)}, u32[]{:S(2)}, u32[]{:S(2)}) async-start(bf16[64,16,128]{2,1,0:T(8,128)(2,1)} %get-tuple-element.68), calls=%async_computation.2 | async-start | bytes 524288 | tf_op jit(solution)/shard_map/all_to_all | solution.py:351
  107.5 6.9 %collective-permute-done.9.rest_1_ = bf16[64,16,128]{2,1,0:T(8,128)(2,1)S(1)} collective-permute-done((bf16[64,16,128]{2,1,0:T(8,128)(2,1)}, bf16[64,16,128]{2,1,0:T(8,128)(2,1)S(1)}, u32[]{:S(2)}, u32[]{:S(2)}) %collective-permute-start.9) | collective-permute-done | bytes 262176 | tf_op jit(solution)/shard_map/ppermute | solution.py:282
  114.4 4.3 %collective-permute-done.10.rest_2_ = bf16[64,16,128]{2,1,0:T(8,128)(2,1)S(1)} collective-permute-done((bf16[64,16,128]{2,1,0:T(8,128)(2,1)}, bf16[64,16,128]{2,1,0:T(8,128)(2,1)S(1)}, u32[]{:S(2)}, u32[]{:S(2)}) %collective-permute-start.10) | collective-permute-done | bytes 262176 | tf_op jit(solution)/shard_map/ppermute | solution.py:282
  120.6 4.5 %shard_map.81 = (bf16[1024,128]{1,0:T(8,128)(2,1)}, bf16[64,16,128]{2,1,0:T(8,128)(2,1)}, bf16[4,64,16,128]{3,2,1,0:T(8,128)(2,1)}, bf16[4,1024,128]{2,1,0:T(8,128)(2,1)}, f32[4,2,128]{2,1,0:T(2,128)}) custom-call(bf16[64,16,128]{2,1,0:T(8,128)(2,1)} %copy-done.29, bf16[1024,128]{1,0:T(8,128)(2,1)} %get-tuple-element.55.upstream, ...), custom_call_target="tpu_custom_call" | custom-call | flops 67108864 | bytes 2097152 | tf_op jit(solution)/shard_map/pallas_call | solution.py:368
  125.1 24.8 %all_to_all.45.received.rest_1_ = bf16[64,16,128]{2,1,0:T(8,128)(2,1)S(1)} all-to-all(bf16[64,16,128]{2,1,0:T(8,128)(2,1)} %get-tuple-element.78), channel_id=1, replica_groups=mesh['segment'=4,'seq'=64] {'seq'}, dimensions={0} | all-to-all | bytes 524288 | tf_op jit(solution)/shard_map/all_to_all | solution.py:338
  150.6 17.8 %all_to_all.46.received = bf16[64,16,128]{2,1,0:T(8,128)(2,1)S(1)} all-to-all(bf16[64,16,128]{2,1,0:T(8,128)(2,1)S(1)} %shard_map.82), channel_id=1, replica_groups=mesh['segment'=4,'seq'=64] {'seq'}, dimensions={0} | all-to-all | bytes 524288 | tf_op jit(solution)/shard_map/all_to_all | solution.py:351
  170.8 17.7 %all_to_all.47.received.rest_0_ = bf16[64,16,128]{2,1,0:T(8,128)(2,1)S(1)} all-to-all(bf16[64,16,128]{2,1,0:T(8,128)(2,1)S(1)} %get-tuple-element.83), channel_id=1, replica_groups=mesh['segment'=4,'seq'=64] {'seq'}, dimensions={0} | all-to-all | bytes 524288 | tf_op jit(solution)/shard_map/all_to_all | solution.py:338
  189.0 17.7 %all_to_all.48.received = bf16[64,16,128]{2,1,0:T(8,128)(2,1)S(1)} all-to-all(bf16[64,16,128]{2,1,0:T(8,128)(2,1)S(1)} %shard_map.84), channel_id=1, replica_groups=mesh['segment'=4,'seq'=64] {'seq'}, dimensions={0} | all-to-all | bytes 524288 | tf_op jit(solution)/shard_map/all_to_all | solution.py:351
  208.1 17.7 %all_to_all.49.received = bf16[64,16,128]{2,1,0:T(8,128)(2,1)S(1)} all-to-all(bf16[64,16,128]{2,1,0:T(8,128)(2,1)S(1)} %get-tuple-element.85), channel_id=1, replica_groups=mesh['segment'=4,'seq'=64] {'seq'}, dimensions={0} | all-to-all | bytes 524288 | tf_op jit(solution)/shard_map/all_to_all | solution.py:338
  227.2 4.7 %all-to-all-start.8 = ((bf16[64,16,128]{2,1,0:T(8,128)(2,1)}), bf16[64,16,128]{2,1,0:T(8,128)(2,1)S(1)}, u32[]{:S(2)}, u32[]{:S(2)}) async-start(bf16[64,16,128]{2,1,0:T(8,128)(2,1)} %get-tuple-element.86), calls=%async_computation.8 | async-start | bytes 524288 | tf_op jit(solution)/shard_map/all_to_all | solution.py:351
  232.0 4.1 %collective-permute-start.16 = (bf16[64,16,128]{2,1,0:T(8,128)(2,1)S(1)}, bf16[64,16,128]{2,1,0:T(8,128)(2,1)S(1)}, u32[]{:S(2)}, u32[]{:S(2)}) collective-permute-start(bf16[64,16,128]{2,1,0:T(8,128)(2,1)S(1)} %get-tuple-element.94), channel_id=1, source_target_pairs={{0,128},{64,192},{128,0},{192,64},{1,129},{65,193},{129,1},{193,65... | collective-permute-start | bytes 786440 | tf_op jit(solution)/shard_map/ppermute | solution.py:282
  236.1 8.9 %all-to-all-done.8.received = bf16[64,16,128]{2,1,0:T(8,128)(2,1)S(1)} async-done(((bf16[64,16,128]{2,1,0:T(8,128)(2,1)}), bf16[64,16,128]{2,1,0:T(8,128)(2,1)S(1)}, u32[]{:S(2)}, u32[]{:S(2)}) %all-to-all-start.8) | async-done | bytes 262176 | tf_op jit(solution)/shard_map/all_to_all | solution.py:351
  249.6 4.1 %collective-permute-start.13 = (bf16[1024,128]{1,0:T(8,128)(2,1)}, bf16[1024,128]{1,0:T(8,128)(2,1)S(1)}, u32[]{:S(2)}, u32[]{:S(2)}) collective-permute-start(bf16[1024,128]{1,0:T(8,128)(2,1)} %get-tuple-element.90), channel_id=1, source_target_pairs={{0,128},{64,192},{128,0},{192,64},{1,129},{65,193},{129,1},{193,65... | collective-permute-start | bytes 786440 | tf_op jit(solution)/shard_map/ppermute | solution.py:282
  255.5 3.8 %collective-permute-done.12.near = bf16[1024,128]{1,0:T(8,128)(2,1)S(1)} collective-permute-done((bf16[1024,128]{1,0:T(8,128)(2,1)}, bf16[1024,128]{1,0:T(8,128)(2,1)S(1)}, u32[]{:S(2)}, u32[]{:S(2)}) %collective-permute-start.12) | collective-permute-done | bytes 262176 | tf_op jit(solution)/shard_map/ppermute | solution.py:282
  259.2 6.5 %collective-permute-done.13.far = bf16[1024,128]{1,0:T(8,128)(2,1)S(1)} collective-permute-done((bf16[1024,128]{1,0:T(8,128)(2,1)}, bf16[1024,128]{1,0:T(8,128)(2,1)S(1)}, u32[]{:S(2)}, u32[]{:S(2)}) %collective-permute-start.13) | collective-permute-done | bytes 262176 | tf_op jit(solution)/shard_map/ppermute | solution.py:282
  (110 shorter events, 46.5 us)
Async XLA Ops:
  4.0 41.3 %all-to-all-start = ((bf16[64,4,16,128]{3,2,1,0:T(8,128)(2,1)}), bf16[64,4,16,128]{3,2,1,0:T(8,128)(2,1)S(1)}, u32[]{:S(2)}, u32[]{:S(2)}) async-start(bf16[64,4,16,128]{3,2,1,0:T(8,128)(2,1)} %shard_map.77), calls=%async_computation | async-start | bytes 2097152 | tf_op jit(solution)/shard_map/all_to_all | solution.py:313
  17.4 24.9 %collective-permute-start.3 = (bf16[4,256,256]{2,1,0:T(8,128)(2,1)S(1)}, bf16[4,256,256]{2,1,0:T(8,128)(2,1)S(1)}, u32[]{:S(2)}, u32[]{:S(2)}) collective-permute-start(bf16[4,256,256]{2,1,0:T(8,128)(2,1)S(1)} %bitcast.8), channel_id=1, source_target_pairs={{0,192},{64,0},{128,64},{192,128},{1,193},{65,1},{129,65},{193,129... | collective-permute-start | bytes 1572872 | tf_op jit(solution)/shard_map/ppermute | solution.py:282
  22.3 9.6 %collective-permute-start = (bf16[1040,128]{1,0:T(8,128)(2,1)}, bf16[1040,128]{1,0:T(8,128)(2,1)S(1)}, u32[]{:S(2)}, u32[]{:S(2)}) collective-permute-start(bf16[1040,128]{1,0:T(8,128)(2,1)} %get-tuple-element.50), channel_id=1, source_target_pairs={{0,64},{64,128},{128,192},{192,0},{1,65},{65,129},{129,193},{193,1... | collective-permute-start | bytes 798728 | tf_op jit(solution)/shard_map/ppermute | solution.py:282
  22.4 13.4 %collective-permute-start.1 = (bf16[1040,128]{1,0:T(8,128)(2,1)}, bf16[1040,128]{1,0:T(8,128)(2,1)S(1)}, u32[]{:S(2)}, u32[]{:S(2)}) collective-permute-start(bf16[1040,128]{1,0:T(8,128)(2,1)} %get-tuple-element.51), channel_id=1, source_target_pairs={{0,128},{64,192},{128,0},{192,64},{1,129},{65,193},{129,1},{193,65... | collective-permute-start | bytes 798728 | tf_op jit(solution)/shard_map/ppermute | solution.py:282
  24.2 18.1 %collective-permute-start.2 = (bf16[1040,128]{1,0:T(8,128)(2,1)}, bf16[1040,128]{1,0:T(8,128)(2,1)S(1)}, u32[]{:S(2)}, u32[]{:S(2)}) collective-permute-start(bf16[1040,128]{1,0:T(8,128)(2,1)} %get-tuple-element.52), channel_id=1, source_target_pairs={{0,192},{64,0},{128,64},{192,128},{1,193},{65,1},{129,65},{193,129... | collective-permute-start | bytes 798728 | tf_op jit(solution)/shard_map/ppermute | solution.py:282
  50.1 42.0 %all-to-all-start.1 = ((bf16[64,5,16,128]{3,2,1,0:T(8,128)(2,1)}), bf16[64,5,16,128]{3,2,1,0:T(8,128)(2,1)S(1)}, u32[]{:S(2)}, u32[]{:S(2)}) async-start(bf16[64,5,16,128]{3,2,1,0:T(8,128)(2,1)} %get-tuple-element.60), calls=%async_computation.1 | async-start | bytes 2621440 | tf_op jit(solution)/shard_map/all_to_all | solution.py:329
  58.6 15.3 %collective-permute-start.6 = (bf16[4,256,256]{2,1,0:T(8,128)(2,1)S(1)}, bf16[4,256,256]{2,1,0:T(8,128)(2,1)S(1)}, u32[]{:S(2)}, u32[]{:S(2)}) collective-permute-start(bf16[4,256,256]{2,1,0:T(8,128)(2,1)S(1)} %bitcast.9), channel_id=1, source_target_pairs={{0,64},{64,128},{128,192},{192,0},{1,65},{65,129},{129,193},{193,1... | collective-permute-start | bytes 1572872 | tf_op jit(solution)/shard_map/ppermute | solution.py:282
  59.5 13.4 %collective-permute-start.7 = (bf16[4,256,256]{2,1,0:T(8,128)(2,1)S(1)}, bf16[4,256,256]{2,1,0:T(8,128)(2,1)S(1)}, u32[]{:S(2)}, u32[]{:S(2)}) collective-permute-start(bf16[4,256,256]{2,1,0:T(8,128)(2,1)S(1)} %copy-done.12), channel_id=1, source_target_pairs={{0,192},{64,0},{128,64},{192,128},{1,193},{65,1},{129,65},{193,129... | collective-permute-start | bytes 1572872 | tf_op jit(solution)/shard_map/ppermute | solution.py:282
  62.1 22.1 %collective-permute-start.5 = (bf16[4,256,256]{2,1,0:T(8,128)(2,1)S(1)}, bf16[4,256,256]{2,1,0:T(8,128)(2,1)S(1)}, u32[]{:S(2)}, u32[]{:S(2)}) collective-permute-start(bf16[4,256,256]{2,1,0:T(8,128)(2,1)S(1)} %bitcast.16), channel_id=1, source_target_pairs={{0,192},{64,0},{128,64},{192,128},{1,193},{65,1},{129,65},{193,129... | collective-permute-start | bytes 1572872 | tf_op jit(solution)/shard_map/ppermute | solution.py:282
  63.4 21.8 %collective-permute-start.4 = (bf16[4,256,256]{2,1,0:T(8,128)(2,1)S(1)}, bf16[4,256,256]{2,1,0:T(8,128)(2,1)}, u32[]{:S(2)}, u32[]{:S(2)}) collective-permute-start(bf16[4,256,256]{2,1,0:T(8,128)(2,1)S(1)} %bitcast.17), channel_id=1, source_target_pairs={{0,64},{64,128},{128,192},{192,0},{1,65},{65,129},{129,193},{193,1... | collective-permute-start | bytes 1572872 | tf_op jit(solution)/shard_map/ppermute | solution.py:282
  92.2 27.5 %collective-permute-start.8 = (bf16[4,256,256]{2,1,0:T(8,128)(2,1)S(1)}, bf16[4,256,256]{2,1,0:T(8,128)(2,1)S(1)}, u32[]{:S(2)}, u32[]{:S(2)}) collective-permute-start(bf16[4,256,256]{2,1,0:T(8,128)(2,1)S(1)} %collective-permute-done.5.right), channel_id=1, source_target_pairs={{0,192},{64,0},{128,64},{192,128},{1,193},{65,1},{129,65},{193,129... | collective-permute-start | bytes 1572872 | tf_op jit(solution)/shard_map/ppermute | solution.py:282
  98.1 21.5 %all-to-all-start.2 = ((bf16[64,16,128]{2,1,0:T(8,128)(2,1)}), bf16[64,16,128]{2,1,0:T(8,128)(2,1)S(1)}, u32[]{:S(2)}, u32[]{:S(2)}) async-start(bf16[64,16,128]{2,1,0:T(8,128)(2,1)} %get-tuple-element.68), calls=%async_computation.2 | async-start | bytes 524288 | tf_op jit(solution)/shard_map/all_to_all | solution.py:351
  104.8 9.6 %collective-permute-start.9 = (bf16[64,16,128]{2,1,0:T(8,128)(2,1)}, bf16[64,16,128]{2,1,0:T(8,128)(2,1)S(1)}, u32[]{:S(2)}, u32[]{:S(2)}) collective-permute-start(bf16[64,16,128]{2,1,0:T(8,128)(2,1)} %get-tuple-element.75), channel_id=1, source_target_pairs={{0,64},{64,128},{128,192},{192,0},{1,65},{65,129},{129,193},{193,1... | collective-permute-start | bytes 786440 | tf_op jit(solution)/shard_map/ppermute | solution.py:282
  104.9 13.8 %collective-permute-start.10 = (bf16[64,16,128]{2,1,0:T(8,128)(2,1)}, bf16[64,16,128]{2,1,0:T(8,128)(2,1)S(1)}, u32[]{:S(2)}, u32[]{:S(2)}) collective-permute-start(bf16[64,16,128]{2,1,0:T(8,128)(2,1)} %get-tuple-element.76), channel_id=1, source_target_pairs={{0,128},{64,192},{128,0},{192,64},{1,129},{65,193},{129,1},{193,65... | collective-permute-start | bytes 786440 | tf_op jit(solution)/shard_map/ppermute | solution.py:282
  106.8 12.8 %collective-permute-start.11 = (bf16[64,16,128]{2,1,0:T(8,128)(2,1)}, bf16[64,16,128]{2,1,0:T(8,128)(2,1)S(1)}, u32[]{:S(2)}, u32[]{:S(2)}) collective-permute-start(bf16[64,16,128]{2,1,0:T(8,128)(2,1)} %get-tuple-element.77), channel_id=1, source_target_pairs={{0,192},{64,0},{128,64},{192,128},{1,193},{65,1},{129,65},{193,129... | collective-permute-start | bytes 786440 | tf_op jit(solution)/shard_map/ppermute | solution.py:282
  125.1 43.3 %copy-start.22 = (bf16[4,256,256]{2,1,0:T(8,128)(2,1)S(1)}, bf16[4,256,256]{2,1,0:T(8,128)(2,1)}, u32[]{:S(2)}) copy-start(bf16[4,256,256]{2,1,0:T(8,128)(2,1)} %copy-done.21) | copy-start | bytes 1572868
  170.8 35.9 %copy-start.25 = (bf16[1024,128]{1,0:T(8,128)(2,1)}, bf16[1024,128]{1,0:T(8,128)(2,1)S(1)}, u32[]{:S(2)}) copy-start(bf16[1024,128]{1,0:T(8,128)(2,1)S(1)} %get-tuple-element.84.upstream.rest_2_) | copy-start | bytes 786436
  227.2 17.9 %all-to-all-start.8 = ((bf16[64,16,128]{2,1,0:T(8,128)(2,1)}), bf16[64,16,128]{2,1,0:T(8,128)(2,1)S(1)}, u32[]{:S(2)}, u32[]{:S(2)}) async-start(bf16[64,16,128]{2,1,0:T(8,128)(2,1)} %get-tuple-element.86), calls=%async_computation.8 | async-start | bytes 524288 | tf_op jit(solution)/shard_map/all_to_all | solution.py:351
  231.9 21.8 %collective-permute-start.15 = (bf16[64,16,128]{2,1,0:T(8,128)(2,1)S(1)}, bf16[64,16,128]{2,1,0:T(8,128)(2,1)S(1)}, u32[]{:S(2)}, u32[]{:S(2)}) collective-permute-start(bf16[64,16,128]{2,1,0:T(8,128)(2,1)S(1)} %get-tuple-element.93), channel_id=1, source_target_pairs={{0,64},{64,128},{128,192},{192,0},{1,65},{65,129},{129,193},{193,1... | collective-permute-start | bytes 786440 | tf_op jit(solution)/shard_map/ppermute | solution.py:282
  232.0 21.7 %collective-permute-start.16 = (bf16[64,16,128]{2,1,0:T(8,128)(2,1)S(1)}, bf16[64,16,128]{2,1,0:T(8,128)(2,1)S(1)}, u32[]{:S(2)}, u32[]{:S(2)}) collective-permute-start(bf16[64,16,128]{2,1,0:T(8,128)(2,1)S(1)} %get-tuple-element.94), channel_id=1, source_target_pairs={{0,128},{64,192},{128,0},{192,64},{1,129},{65,193},{129,1},{193,65... | collective-permute-start | bytes 786440 | tf_op jit(solution)/shard_map/ppermute | solution.py:282
  236.1 17.6 %collective-permute-start.17 = (bf16[64,16,128]{2,1,0:T(8,128)(2,1)S(1)}, bf16[64,16,128]{2,1,0:T(8,128)(2,1)S(1)}, u32[]{:S(2)}, u32[]{:S(2)}) collective-permute-start(bf16[64,16,128]{2,1,0:T(8,128)(2,1)S(1)} %get-tuple-element.95), channel_id=1, source_target_pairs={{0,192},{64,0},{128,64},{192,128},{1,193},{65,1},{129,65},{193,129... | collective-permute-start | bytes 786440 | tf_op jit(solution)/shard_map/ppermute | solution.py:282
  249.5 9.8 %collective-permute-start.12 = (bf16[1024,128]{1,0:T(8,128)(2,1)}, bf16[1024,128]{1,0:T(8,128)(2,1)S(1)}, u32[]{:S(2)}, u32[]{:S(2)}) collective-permute-start(bf16[1024,128]{1,0:T(8,128)(2,1)} %get-tuple-element.89), channel_id=1, source_target_pairs={{0,64},{64,128},{128,192},{192,0},{1,65},{65,129},{129,193},{193,1... | collective-permute-start | bytes 786440 | tf_op jit(solution)/shard_map/ppermute | solution.py:282
  249.6 16.1 %collective-permute-start.13 = (bf16[1024,128]{1,0:T(8,128)(2,1)}, bf16[1024,128]{1,0:T(8,128)(2,1)S(1)}, u32[]{:S(2)}, u32[]{:S(2)}) collective-permute-start(bf16[1024,128]{1,0:T(8,128)(2,1)} %get-tuple-element.90), channel_id=1, source_target_pairs={{0,128},{64,192},{128,0},{192,64},{1,129},{65,193},{129,1},{193,65... | collective-permute-start | bytes 786440 | tf_op jit(solution)/shard_map/ppermute | solution.py:282
  253.7 12.0 %collective-permute-start.14 = (bf16[1024,128]{1,0:T(8,128)(2,1)}, bf16[1024,128]{1,0:T(8,128)(2,1)S(1)}, u32[]{:S(2)}, u32[]{:S(2)}) collective-permute-start(bf16[1024,128]{1,0:T(8,128)(2,1)} %get-tuple-element.91), channel_id=1, source_target_pairs={{0,192},{64,0},{128,64},{192,128},{1,193},{65,1},{129,65},{193,129... | collective-permute-start | bytes 786440 | tf_op jit(solution)/shard_map/ppermute | solution.py:282
  (34 other events, 435.3 us)

commit v5 on v4

--- a/solution.py
+++ b/solution.py
@@ -178,7 +178,7 @@
     slots, rest = (rest[:4], rest[4:]) if layer == 3 else (rest[0], rest[1:])
     earlier, rest = ((None,) + rest[:3], rest[3:]) if layer == 0 else ((), rest)
     outs, rest = (rest[:4], rest[4:]) if layer == 0 else (rest[:2], rest[2:])
-    kept, rest = (rest[:3], rest[3:]) if layer == 3 else ((), rest)
+    kept, rest = (rest[0], rest[1:]) if layer == 3 else (None, rest)
     chunks, mixed_chunks, block, mixed_block, next_chunks, weights = rest[:6]
     sems = rest[-1]
     index = lax.axis_index("segment")
@@ -186,20 +186,19 @@
     choose("start", factors, RING, layer, weights, sems.at[0])
     place = layer
     if layer in (3, 0):
-        got, ups = rest[6:8]
-        pairs = [(received, got), (upstream, ups)]
+        got, ups, mixed, inputs, vector = rest[6:11]
+        pairs = [(received, got), (upstream, ups), (vectors, vector)]
         if layer == 3:
-            mixed, inputs, vector = kept
+            place = 1
+            pairs.append((held.at[2:4], inputs))
             for step, part in enumerate(slots):
                 pairs.append((part, mixed.at[(index + 4 - step) % 4]))
-            pairs += [(held, inputs), (vectors, vector)]
         else:
-            place = 0
-            mixed, inputs, vector = rest[8:11]
-            pairs += [(slots.at[0:1], mixed), (held.at[0:1], inputs), (vectors, vector)]
+            staged = rest[11]
+            pairs += [(slots.at[0:1], mixed), (held.at[0:1], inputs)]
         copies = moves(pairs, sems.at[5:])
         for step in range(len(earlier)):
-            pick("start", earlier, step, outs[step], sems.at[1 + step])
+            pick("start", earlier, step, staged.at[step], sems.at[1 + step])
         copies[0].wait()
         received, upstream, held, vectors = got, ups, inputs, vector
     else:
@@ -208,7 +207,22 @@
     if layer in (3, 0):
         for copy in copies[1:]:
             copy.wait()
-    mixed_chunks[...] = mixed[place].reshape(1024, 128).astype(F32)
+    if layer == 3:
+        write = pltpu.make_async_copy(mixed, kept, sems.at[13])
+        write.start()
+
+    def written(act, mine):
+        for step in range(4):
+            @pl.when(((index + step) % 4 == 0) == mine)
+            def _():
+                source = ups if mine else staged.at[step]
+                getattr(pltpu.make_async_copy(source, outs[step], sems.at[10 + step]), act)()
+
+    if layer == 0:
+        for step in range(4):
+            pick("wait", earlier, step, staged.at[step], sems.at[1 + step])
+        written("start", False)
+    mixed_chunks[...] = mixed[layer if layer else 0].reshape(1024, 128).astype(F32)
     choose("wait", factors, RING, layer, weights, sems.at[0])
     for row in range(4):
         rows = slice(row * 256, (row + 1) * 256)
@@ -221,10 +235,7 @@
         gate_grad = (slope * mixed_block[...]).astype(BF).astype(F32)
         result = (up + through + gate_grad * scale).astype(BF)
         if layer == 0:
-            for step in range(4):
-                @pl.when((index + step) % 4 == 0)
-                def _():
-                    outs[step][rows, :] = result
+            ups[rows, :] = result
         else:
             outs[0][rows, :] = result
             gate, _ = gated(held, place - 1, vectors, layer - 1, rows)
@@ -232,20 +243,26 @@
             spread(block, next_chunks, row)
     if layer > 0:
         outs[1][...] = next_chunks[...].astype(BF).reshape(64, 16, 128)
+        if layer == 3:
+            write.wait()
     else:
-        for step in range(4):
-            pick("wait", earlier, step, outs[step], sems.at[1 + step])
+        written("start", True)
+        written("wait", True)
+        written("wait", False)
 
 
 def middle_kernel(layer, received, upstream, held, vectors, mixed, own, left, right, across, *rest):
     row_kernel(layer, received, upstream, held, vectors, own, left, right, across, mixed, *rest)
 
 
-def final_kernel(own, near, far, last, out):
-    index = lax.axis_index("segment")
+def final_kernel(own, near, far, last, out, sems):
+    index = lax.axis_index("segment")
+    pairs = []
     for step, value in enumerate((own, near, far, last)):
         lanes = pl.ds(pl.multiple_of(((index + 4 - step) % 4) * 128, 128), 128)
-        out[:, lanes] = value[...]
+        pairs.append((value, out.at[:, lanes]))
+    for copy in moves(pairs, sems):
+        copy.wait()
 
 
 IN_VMEM = pl.BlockSpec(memory_space=pltpu.VMEM)
@@ -361,9 +378,10 @@
         if l in (3, 0):
             scratch += [(CHUNKS, BF), (TALL, BF)]
         if l == 3:
-            outs += [((4,) + CHUNKS, BF), ((4, 1024, 128), BF), ((4, 2, 128), F32)]
+            outs += [((4,) + CHUNKS, BF)]
+            scratch += [((4,) + CHUNKS, BF), ((2, 1024, 128), BF), (4, 2, 128)]
         if l == 0:
-            scratch += [((1,) + CHUNKS, BF), ((1, 1024, 128), BF), (4, 2, 128)]
+            scratch += [((1,) + CHUNKS, BF), ((1, 1024, 128), BF), (4, 2, 128), ((4, 1024, 128), BF)]
         order = [0, 1, 2, 3] + [8] * (l in (2, 1)) + [4, 5, 6, 7] + list(range(8 + (l in (2, 1)), len(operands)))
         made = call(
             functools.partial(row_kernel, l) if l in (3, 0) else functools.partial(middle_kernel, l),
@@ -374,16 +392,16 @@
             anywhere=len(operands) if l in (3, 0) else 4,
             copies=14,
             grant=grant,
+            free={3: (2,), 0: (0, 1, 2, 3)}.get(l, ()),
         )(*[operands[i] for i in order])
         if l == 3:
-            mixed, held, vectors = made[2:]
-            made = made[:2]
+            made, mixed = made[:2], made[2]
         if l > 0:
             upstream, sends = made
             results[l] = upstream
 
     second = call(second_kernel, 5, [((4, 256, 256), F32)], [TALL, TALL], 4 * FLOPS)(firsts_cols, *grads)
-    grads_out = call(final_kernel, 4, [((1024, 512), BF)], [], 1 << 20)(*exchanged(made))
+    grads_out = call(final_kernel, 4, [((1024, 512), BF)], [], 1 << 20, copies=4, free=(0,))(*exchanged(made))
     return grads_out[None], second[None]
 
 

time: 268 us -> 268 us (level)
  no operation moved by 1% of the time
where the time goes in v5:
time: 268 us; the launch traced here: 267 us
  blocking collectives  95.6 us (36%)
  waiting for transfers between devices  79.5 us (30%)
  starting transfers between devices  57.5 us (21%)
  Pallas kernels  28.5 us (11%)
  local copies, waits for them, and re-layouts  4.48 us (2%)
    ppermute x18, waiting for transfers between devices, passed(): lax.ppermute(value, 'segment', [(i, (i + step) % 4) for i in range(4)])  60.4 us
    all_to_all x3, blocking collectives, body(): columns[l] = lax.all_to_all(sends, 'seq', 0, 0, tiled=True)  60.2 us
    all_to_all x2, blocking collectives, body(): received = lax.all_to_all(back, 'seq', 0, 0, tiled=True)  35.5 us
    ppermute x18, starting transfers between devices, passed(): lax.ppermute(value, 'segment', [(i, (i + step) % 4) for i in range(4)])  24.5 us
    all_to_all x1, starting transfers between devices, body(): firsts_cols = lax.all_to_all(firsts_out, 'seq', 0, 0, tiled=True)  13.3 us
    all_to_all x2, starting transfers between devices, body(): received = lax.all_to_all(back, 'seq', 0, 0, tiled=True)  11.3 us
    pallas_call x4, Pallas kernels, body(): call(functools.partial(row_kernel, l) if l in (3, 0) else functools.parti...  9.91 us
    all_to_all x2, waiting for transfers between devices, body(): received = lax.all_to_all(back, 'seq', 0, 0, tiled=True)  9.08 us
  transfers between devices with their start and end apart: 22, of which 15 were waited for; matrix products, arithmetic and copies ran while one was open for 0% of the time, Pallas kernels for 4%

profile of v5, /device:TPU:1, one launch (start us, length us, event | category | flops | bytes accessed | tf_op | source)
XLA Modules:
  0.0 266.8 jit_solution(16144626152981800530)
XLA Ops:
  4.0 13.3 %all-to-all-start = ((bf16[64,4,16,128]{3,2,1,0:T(8,128)(2,1)}), bf16[64,4,16,128]{3,2,1,0:T(8,128)(2,1)S(1)}, u32[]{:S(2)}, u32[]{:S(2)}) async-start(bf16[64,4,16,128]{3,2,1,0:T(8,128)(2,1)} %shard_map.77), calls=%async_computation | async-start | bytes 2097152 | tf_op jit(solution)/shard_map/all_to_all | solution.py:330
  25.1 6.9 %collective-permute-done.near = bf16[1040,128]{1,0:T(8,128)(2,1)S(1)} collective-permute-done((bf16[1040,128]{1,0:T(8,128)(2,1)}, bf16[1040,128]{1,0:T(8,128)(2,1)S(1)}, u32[]{:S(2)}, u32[]{:S(2)}) %collective-permute-start) | collective-permute-done | bytes 266272 | tf_op jit(solution)/shard_map/ppermute | solution.py:299
  32.0 3.9 %collective-permute-done.1.far = bf16[1040,128]{1,0:T(8,128)(2,1)S(1)} collective-permute-done((bf16[1040,128]{1,0:T(8,128)(2,1)}, bf16[1040,128]{1,0:T(8,128)(2,1)S(1)}, u32[]{:S(2)}, u32[]{:S(2)}) %collective-permute-start.1) | collective-permute-done | bytes 266272 | tf_op jit(solution)/shard_map/ppermute | solution.py:299
  35.9 6.4 %collective-permute-done.2.last = bf16[1040,128]{1,0:T(8,128)(2,1)S(1)} collective-permute-done((bf16[1040,128]{1,0:T(8,128)(2,1)}, bf16[1040,128]{1,0:T(8,128)(2,1)S(1)}, u32[]{:S(2)}, u32[]{:S(2)}) %collective-permute-start.2) | collective-permute-done | bytes 266272 | tf_op jit(solution)/shard_map/ppermute | solution.py:299
  46.3 3.8 %shard_map.79 = (bf16[64,5,16,128]{3,2,1,0:T(8,128)(2,1)}, bf16[4,1024,128]{2,1,0:T(8,128)(2,1)}, f32[4,2,128]{2,1,0:T(2,128)}) custom-call(bf16[4,256,256]{2,1,0:T(8,128)(2,1)} %bitcast.6, bf16[64,4,16,128]{3,2,1,0:T(8,128)(2,1)} %copy-done.8, bf16[1024,128]{1,0:T(8,128)(2,1)} %get-tuple-element.53.upstream, bf16[1040,128]{1,0:T(8,128)(2,1)} %get-tuple-element.54.own, ...), custom_call_target="tpu_custom_call" | custom-call | flops 268435456 | bytes 2097152 | tf_op jit(solution)/shard_map/pallas_call | solution.py:335
  50.1 8.4 %all-to-all-start.1 = ((bf16[64,5,16,128]{3,2,1,0:T(8,128)(2,1)}), bf16[64,5,16,128]{3,2,1,0:T(8,128)(2,1)S(1)}, u32[]{:S(2)}, u32[]{:S(2)}) async-start(bf16[64,5,16,128]{3,2,1,0:T(8,128)(2,1)} %get-tuple-element.58), calls=%async_computation.1 | async-start | bytes 2621440 | tf_op jit(solution)/shard_map/all_to_all | solution.py:346
  63.5 9.7 %collective-permute-done.7.across = bf16[4,256,256]{2,1,0:T(8,128)(2,1)S(1)} collective-permute-done((bf16[4,256,256]{2,1,0:T(8,128)(2,1)}, bf16[4,256,256]{2,1,0:T(8,128)(2,1)S(1)}, u32[]{:S(2)}, u32[]{:S(2)}) %collective-permute-start.7) | collective-permute-done | bytes 524320 | tf_op jit(solution)/shard_map/ppermute | solution.py:299
  73.8 10.5 %collective-permute-done.5.right = bf16[4,256,256]{2,1,0:T(8,128)(2,1)S(1)} collective-permute-done((bf16[4,256,256]{2,1,0:T(8,128)(2,1)S(1)}, bf16[4,256,256]{2,1,0:T(8,128)(2,1)S(1)}, u32[]{:S(2)}, u32[]{:S(2)}) %collective-permute-start.5) | collective-permute-done | bytes 524320 | tf_op jit(solution)/shard_map/ppermute | solution.py:299
  85.2 7.0 %all-to-all-done.1.received.rest_2_ = bf16[64,5,16,128]{3,2,1,0:T(8,128)(2,1)S(1)} async-done(((bf16[64,5,16,128]{3,2,1,0:T(8,128)(2,1)}), bf16[64,5,16,128]{3,2,1,0:T(8,128)(2,1)S(1)}, u32[]{:S(2)}, u32[]{:S(2)}) %all-to-all-start.1) | async-done | bytes 1310752 | tf_op jit(solution)/shard_map/all_to_all | solution.py:346
  98.2 6.6 %all-to-all-start.2 = ((bf16[64,16,128]{2,1,0:T(8,128)(2,1)}), bf16[64,16,128]{2,1,0:T(8,128)(2,1)S(1)}, u32[]{:S(2)}, u32[]{:S(2)}) async-start(bf16[64,16,128]{2,1,0:T(8,128)(2,1)} %get-tuple-element.66), calls=%async_computation.2 | async-start | bytes 524288 | tf_op jit(solution)/shard_map/all_to_all | solution.py:368
  107.6 6.9 %collective-permute-done.9.rest_1_ = bf16[64,16,128]{2,1,0:T(8,128)(2,1)S(1)} collective-permute-done((bf16[64,16,128]{2,1,0:T(8,128)(2,1)}, bf16[64,16,128]{2,1,0:T(8,128)(2,1)S(1)}, u32[]{:S(2)}, u32[]{:S(2)}) %collective-permute-start.9) | collective-permute-done | bytes 262176 | tf_op jit(solution)/shard_map/ppermute | solution.py:299
  114.5 4.3 %collective-permute-done.10.rest_2_ = bf16[64,16,128]{2,1,0:T(8,128)(2,1)S(1)} collective-permute-done((bf16[64,16,128]{2,1,0:T(8,128)(2,1)}, bf16[64,16,128]{2,1,0:T(8,128)(2,1)S(1)}, u32[]{:S(2)}, u32[]{:S(2)}) %collective-permute-start.10) | collective-permute-done | bytes 262176 | tf_op jit(solution)/shard_map/ppermute | solution.py:299
  120.7 3.9 %shard_map.81 = (bf16[1024,128]{1,0:T(8,128)(2,1)}, bf16[64,16,128]{2,1,0:T(8,128)(2,1)}, bf16[4,64,16,128]{3,2,1,0:T(8,128)(2,1)}) custom-call(bf16[64,16,128]{2,1,0:T(8,128)(2,1)} %copy-done.25, bf16[1024,128]{1,0:T(8,128)(2,1)} %get-tuple-element.53.upstream, bf16[4,1024,128]{2,1,0:T(8,128)(2,1)} %get-tuple-element.67.held, ...), custom_call_target="tpu_custom_call" | custom-call | flops 67108864 | bytes 2097152 | tf_op jit(solution)/shard_map/pallas_call | solution.py:386
  124.7 24.8 %all_to_all.45.received.rest_1_ = bf16[64,16,128]{2,1,0:T(8,128)(2,1)S(1)} all-to-all(bf16[64,16,128]{2,1,0:T(8,128)(2,1)} %get-tuple-element.76), channel_id=1, replica_groups=mesh['segment'=4,'seq'=64] {'seq'}, dimensions={0} | all-to-all | bytes 524288 | tf_op jit(solution)/shard_map/all_to_all | solution.py:355
  150.1 17.8 %all_to_all.46.received = bf16[64,16,128]{2,1,0:T(8,128)(2,1)S(1)} all-to-all(bf16[64,16,128]{2,1,0:T(8,128)(2,1)S(1)} %shard_map.82), channel_id=1, replica_groups=mesh['segment'=4,'seq'=64] {'seq'}, dimensions={0} | all-to-all | bytes 524288 | tf_op jit(solution)/shard_map/all_to_all | solution.py:368
  170.3 17.7 %all_to_all.47.received.rest_0_ = bf16[64,16,128]{2,1,0:T(8,128)(2,1)S(1)} all-to-all(bf16[64,16,128]{2,1,0:T(8,128)(2,1)S(1)} %get-tuple-element.79), channel_id=1, replica_groups=mesh['segment'=4,'seq'=64] {'seq'}, dimensions={0} | all-to-all | bytes 524288 | tf_op jit(solution)/shard_map/all_to_all | solution.py:355
  189.5 17.7 %all_to_all.48.received = bf16[64,16,128]{2,1,0:T(8,128)(2,1)S(1)} all-to-all(bf16[64,16,128]{2,1,0:T(8,128)(2,1)S(1)} %shard_map.84), channel_id=1, replica_groups=mesh['segment'=4,'seq'=64] {'seq'}, dimensions={0} | all-to-all | bytes 524288 | tf_op jit(solution)/shard_map/all_to_all | solution.py:368
  208.6 17.7 %all_to_all.49.received = bf16[64,16,128]{2,1,0:T(8,128)(2,1)S(1)} all-to-all(bf16[64,16,128]{2,1,0:T(8,128)(2,1)S(1)} %get-tuple-element.81), channel_id=1, replica_groups=mesh['segment'=4,'seq'=64] {'seq'}, dimensions={0} | all-to-all | bytes 524288 | tf_op jit(solution)/shard_map/all_to_all | solution.py:355
  227.7 4.7 %all-to-all-start.8 = ((bf16[64,16,128]{2,1,0:T(8,128)(2,1)}), bf16[64,16,128]{2,1,0:T(8,128)(2,1)S(1)}, u32[]{:S(2)}, u32[]{:S(2)}) async-start(bf16[64,16,128]{2,1,0:T(8,128)(2,1)} %get-tuple-element.82), calls=%async_computation.8 | async-start | bytes 524288 | tf_op jit(solution)/shard_map/all_to_all | solution.py:368
  232.5 4.0 %collective-permute-start.16 = (bf16[64,16,128]{2,1,0:T(8,128)(2,1)S(1)}, bf16[64,16,128]{2,1,0:T(8,128)(2,1)S(1)}, u32[]{:S(2)}, u32[]{:S(2)}) collective-permute-start(bf16[64,16,128]{2,1,0:T(8,128)(2,1)S(1)} %get-tuple-element.90), channel_id=1, source_target_pairs={{0,128},{64,192},{128,0},{192,64},{1,129},{65,193},{129,1},{193,65... | collective-permute-start | bytes 786440 | tf_op jit(solution)/shard_map/ppermute | solution.py:299
  236.5 9.1 %all-to-all-done.8.received = bf16[64,16,128]{2,1,0:T(8,128)(2,1)S(1)} async-done(((bf16[64,16,128]{2,1,0:T(8,128)(2,1)}), bf16[64,16,128]{2,1,0:T(8,128)(2,1)S(1)}, u32[]{:S(2)}, u32[]{:S(2)}) %all-to-all-start.8) | async-done | bytes 262176 | tf_op jit(solution)/shard_map/all_to_all | solution.py:368
  249.6 4.0 %collective-permute-start.13 = (bf16[1024,128]{1,0:T(8,128)(2,1)}, bf16[1024,128]{1,0:T(8,128)(2,1)S(1)}, u32[]{:S(2)}, u32[]{:S(2)}) collective-permute-start(bf16[1024,128]{1,0:T(8,128)(2,1)} %get-tuple-element.86), channel_id=1, source_target_pairs={{0,128},{64,192},{128,0},{192,64},{1,129},{65,193},{129,1},{193,65... | collective-permute-start | bytes 786440 | tf_op jit(solution)/shard_map/ppermute | solution.py:299
  255.4 3.6 %collective-permute-done.12.near = bf16[1024,128]{1,0:T(8,128)(2,1)S(1)} collective-permute-done((bf16[1024,128]{1,0:T(8,128)(2,1)}, bf16[1024,128]{1,0:T(8,128)(2,1)S(1)}, u32[]{:S(2)}, u32[]{:S(2)}) %collective-permute-start.12) | collective-permute-done | bytes 262176 | tf_op jit(solution)/shard_map/ppermute | solution.py:299
  259.0 6.6 %collective-permute-done.13.far = bf16[1024,128]{1,0:T(8,128)(2,1)S(1)} collective-permute-done((bf16[1024,128]{1,0:T(8,128)(2,1)}, bf16[1024,128]{1,0:T(8,128)(2,1)S(1)}, u32[]{:S(2)}, u32[]{:S(2)}) %collective-permute-start.13) | collective-permute-done | bytes 262176 | tf_op jit(solution)/shard_map/ppermute | solution.py:299
  (102 shorter events, 46.5 us)
Async XLA Ops:
  4.0 41.3 %all-to-all-start = ((bf16[64,4,16,128]{3,2,1,0:T(8,128)(2,1)}), bf16[64,4,16,128]{3,2,1,0:T(8,128)(2,1)S(1)}, u32[]{:S(2)}, u32[]{:S(2)}) async-start(bf16[64,4,16,128]{3,2,1,0:T(8,128)(2,1)} %shard_map.77), calls=%async_computation | async-start | bytes 2097152 | tf_op jit(solution)/shard_map/all_to_all | solution.py:330
  17.4 24.9 %collective-permute-start.3 = (bf16[4,256,256]{2,1,0:T(8,128)(2,1)S(1)}, bf16[4,256,256]{2,1,0:T(8,128)(2,1)}, u32[]{:S(2)}, u32[]{:S(2)}) collective-permute-start(bf16[4,256,256]{2,1,0:T(8,128)(2,1)S(1)} %bitcast.8), channel_id=1, source_target_pairs={{0,192},{64,0},{128,64},{192,128},{1,193},{65,1},{129,65},{193,129... | collective-permute-start | bytes 1572872 | tf_op jit(solution)/shard_map/ppermute | solution.py:299
  22.4 9.6 %collective-permute-start = (bf16[1040,128]{1,0:T(8,128)(2,1)}, bf16[1040,128]{1,0:T(8,128)(2,1)S(1)}, u32[]{:S(2)}, u32[]{:S(2)}) collective-permute-start(bf16[1040,128]{1,0:T(8,128)(2,1)} %get-tuple-element.48), channel_id=1, source_target_pairs={{0,64},{64,128},{128,192},{192,0},{1,65},{65,129},{129,193},{193,1... | collective-permute-start | bytes 798728 | tf_op jit(solution)/shard_map/ppermute | solution.py:299
  22.5 13.4 %collective-permute-start.1 = (bf16[1040,128]{1,0:T(8,128)(2,1)}, bf16[1040,128]{1,0:T(8,128)(2,1)S(1)}, u32[]{:S(2)}, u32[]{:S(2)}) collective-permute-start(bf16[1040,128]{1,0:T(8,128)(2,1)} %get-tuple-element.49), channel_id=1, source_target_pairs={{0,128},{64,192},{128,0},{192,64},{1,129},{65,193},{129,1},{193,65... | collective-permute-start | bytes 798728 | tf_op jit(solution)/shard_map/ppermute | solution.py:299
  24.2 18.1 %collective-permute-start.2 = (bf16[1040,128]{1,0:T(8,128)(2,1)}, bf16[1040,128]{1,0:T(8,128)(2,1)S(1)}, u32[]{:S(2)}, u32[]{:S(2)}) collective-permute-start(bf16[1040,128]{1,0:T(8,128)(2,1)} %get-tuple-element.50), channel_id=1, source_target_pairs={{0,192},{64,0},{128,64},{192,128},{1,193},{65,1},{129,65},{193,129... | collective-permute-start | bytes 798728 | tf_op jit(solution)/shard_map/ppermute | solution.py:299
  50.1 42.0 %all-to-all-start.1 = ((bf16[64,5,16,128]{3,2,1,0:T(8,128)(2,1)}), bf16[64,5,16,128]{3,2,1,0:T(8,128)(2,1)S(1)}, u32[]{:S(2)}, u32[]{:S(2)}) async-start(bf16[64,5,16,128]{3,2,1,0:T(8,128)(2,1)} %get-tuple-element.58), calls=%async_computation.1 | async-start | bytes 2621440 | tf_op jit(solution)/shard_map/all_to_all | solution.py:346
  58.6 15.3 %collective-permute-start.6 = (bf16[4,256,256]{2,1,0:T(8,128)(2,1)S(1)}, bf16[4,256,256]{2,1,0:T(8,128)(2,1)S(1)}, u32[]{:S(2)}, u32[]{:S(2)}) collective-permute-start(bf16[4,256,256]{2,1,0:T(8,128)(2,1)S(1)} %bitcast.9), channel_id=1, source_target_pairs={{0,64},{64,128},{128,192},{192,0},{1,65},{65,129},{129,193},{193,1... | collective-permute-start | bytes 1572872 | tf_op jit(solution)/shard_map/ppermute | solution.py:299
  59.5 13.7 %collective-permute-start.7 = (bf16[4,256,256]{2,1,0:T(8,128)(2,1)}, bf16[4,256,256]{2,1,0:T(8,128)(2,1)S(1)}, u32[]{:S(2)}, u32[]{:S(2)}) collective-permute-start(bf16[4,256,256]{2,1,0:T(8,128)(2,1)} %collective-permute-done.3.right), channel_id=1, source_target_pairs={{0,192},{64,0},{128,64},{192,128},{1,193},{65,1},{129,65},{193,129... | collective-permute-start | bytes 1572872 | tf_op jit(solution)/shard_map/ppermute | solution.py:299
  62.0 22.3 %collective-permute-start.5 = (bf16[4,256,256]{2,1,0:T(8,128)(2,1)S(1)}, bf16[4,256,256]{2,1,0:T(8,128)(2,1)S(1)}, u32[]{:S(2)}, u32[]{:S(2)}) collective-permute-start(bf16[4,256,256]{2,1,0:T(8,128)(2,1)S(1)} %bitcast.16), channel_id=1, source_target_pairs={{0,192},{64,0},{128,64},{192,128},{1,193},{65,1},{129,65},{193,129... | collective-permute-start | bytes 1572872 | tf_op jit(solution)/shard_map/ppermute | solution.py:299
  63.4 21.8 %collective-permute-start.4 = (bf16[4,256,256]{2,1,0:T(8,128)(2,1)S(1)}, bf16[4,256,256]{2,1,0:T(8,128)(2,1)}, u32[]{:S(2)}, u32[]{:S(2)}) collective-permute-start(bf16[4,256,256]{2,1,0:T(8,128)(2,1)S(1)} %bitcast.17), channel_id=1, source_target_pairs={{0,64},{64,128},{128,192},{192,0},{1,65},{65,129},{129,193},{193,1... | collective-permute-start | bytes 1572872 | tf_op jit(solution)/shard_map/ppermute | solution.py:299
  92.2 27.6 %collective-permute-start.8 = (bf16[4,256,256]{2,1,0:T(8,128)(2,1)}, bf16[4,256,256]{2,1,0:T(8,128)(2,1)S(1)}, u32[]{:S(2)}, u32[]{:S(2)}) collective-permute-start(bf16[4,256,256]{2,1,0:T(8,128)(2,1)} %copy-done.15), channel_id=1, source_target_pairs={{0,192},{64,0},{128,64},{192,128},{1,193},{65,1},{129,65},{193,129... | collective-permute-start | bytes 1572872 | tf_op jit(solution)/shard_map/ppermute | solution.py:299
  98.2 21.5 %all-to-all-start.2 = ((bf16[64,16,128]{2,1,0:T(8,128)(2,1)}), bf16[64,16,128]{2,1,0:T(8,128)(2,1)S(1)}, u32[]{:S(2)}, u32[]{:S(2)}) async-start(bf16[64,16,128]{2,1,0:T(8,128)(2,1)} %get-tuple-element.66), calls=%async_computation.2 | async-start | bytes 524288 | tf_op jit(solution)/shard_map/all_to_all | solution.py:368
  104.8 9.6 %collective-permute-start.9 = (bf16[64,16,128]{2,1,0:T(8,128)(2,1)}, bf16[64,16,128]{2,1,0:T(8,128)(2,1)S(1)}, u32[]{:S(2)}, u32[]{:S(2)}) collective-permute-start(bf16[64,16,128]{2,1,0:T(8,128)(2,1)} %get-tuple-element.73), channel_id=1, source_target_pairs={{0,64},{64,128},{128,192},{192,0},{1,65},{65,129},{129,193},{193,1... | collective-permute-start | bytes 786440 | tf_op jit(solution)/shard_map/ppermute | solution.py:299
  104.9 13.8 %collective-permute-start.10 = (bf16[64,16,128]{2,1,0:T(8,128)(2,1)}, bf16[64,16,128]{2,1,0:T(8,128)(2,1)S(1)}, u32[]{:S(2)}, u32[]{:S(2)}) collective-permute-start(bf16[64,16,128]{2,1,0:T(8,128)(2,1)} %get-tuple-element.74), channel_id=1, source_target_pairs={{0,128},{64,192},{128,0},{192,64},{1,129},{65,193},{129,1},{193,65... | collective-permute-start | bytes 786440 | tf_op jit(solution)/shard_map/ppermute | solution.py:299
  106.9 12.8 %collective-permute-start.11 = (bf16[64,16,128]{2,1,0:T(8,128)(2,1)}, bf16[64,16,128]{2,1,0:T(8,128)(2,1)S(1)}, u32[]{:S(2)}, u32[]{:S(2)}) collective-permute-start(bf16[64,16,128]{2,1,0:T(8,128)(2,1)} %get-tuple-element.75), channel_id=1, source_target_pairs={{0,192},{64,0},{128,64},{192,128},{1,193},{65,1},{129,65},{193,129... | collective-permute-start | bytes 786440 | tf_op jit(solution)/shard_map/ppermute | solution.py:299
  120.7 47.2 %copy-start.23 = (f32[4,2,128]{2,1,0:T(2,128)S(1)}, f32[4,2,128]{2,1,0:T(2,128)}, u32[]{:S(2)}) copy-start(f32[4,2,128]{2,1,0:T(2,128)} %get-tuple-element.68.vectors) | copy-start | bytes 12292
  124.7 43.3 %copy-start.18 = (bf16[4,256,256]{2,1,0:T(8,128)(2,1)S(1)}, bf16[4,256,256]{2,1,0:T(8,128)(2,1)}, u32[]{:S(2)}) copy-start(bf16[4,256,256]{2,1,0:T(8,128)(2,1)} %copy-done.17) | copy-start | bytes 1572868
  227.7 17.9 %all-to-all-start.8 = ((bf16[64,16,128]{2,1,0:T(8,128)(2,1)}), bf16[64,16,128]{2,1,0:T(8,128)(2,1)S(1)}, u32[]{:S(2)}, u32[]{:S(2)}) async-start(bf16[64,16,128]{2,1,0:T(8,128)(2,1)} %get-tuple-element.82), calls=%async_computation.8 | async-start | bytes 524288 | tf_op jit(solution)/shard_map/all_to_all | solution.py:368
  232.4 21.2 %collective-permute-start.15 = (bf16[64,16,128]{2,1,0:T(8,128)(2,1)S(1)}, bf16[64,16,128]{2,1,0:T(8,128)(2,1)S(1)}, u32[]{:S(2)}, u32[]{:S(2)}) collective-permute-start(bf16[64,16,128]{2,1,0:T(8,128)(2,1)S(1)} %get-tuple-element.89), channel_id=1, source_target_pairs={{0,64},{64,128},{128,192},{192,0},{1,65},{65,129},{129,193},{193,1... | collective-permute-start | bytes 786440 | tf_op jit(solution)/shard_map/ppermute | solution.py:299
  232.5 21.1 %collective-permute-start.16 = (bf16[64,16,128]{2,1,0:T(8,128)(2,1)S(1)}, bf16[64,16,128]{2,1,0:T(8,128)(2,1)S(1)}, u32[]{:S(2)}, u32[]{:S(2)}) collective-permute-start(bf16[64,16,128]{2,1,0:T(8,128)(2,1)S(1)} %get-tuple-element.90), channel_id=1, source_target_pairs={{0,128},{64,192},{128,0},{192,64},{1,129},{65,193},{129,1},{193,65... | collective-permute-start | bytes 786440 | tf_op jit(solution)/shard_map/ppermute | solution.py:299
  236.5 17.1 %collective-permute-start.17 = (bf16[64,16,128]{2,1,0:T(8,128)(2,1)S(1)}, bf16[64,16,128]{2,1,0:T(8,128)(2,1)S(1)}, u32[]{:S(2)}, u32[]{:S(2)}) collective-permute-start(bf16[64,16,128]{2,1,0:T(8,128)(2,1)S(1)} %get-tuple-element.91), channel_id=1, source_target_pairs={{0,192},{64,0},{128,64},{192,128},{1,193},{65,1},{129,65},{193,129... | collective-permute-start | bytes 786440 | tf_op jit(solution)/shard_map/ppermute | solution.py:299
  249.5 9.5 %collective-permute-start.12 = (bf16[1024,128]{1,0:T(8,128)(2,1)}, bf16[1024,128]{1,0:T(8,128)(2,1)S(1)}, u32[]{:S(2)}, u32[]{:S(2)}) collective-permute-start(bf16[1024,128]{1,0:T(8,128)(2,1)} %get-tuple-element.85), channel_id=1, source_target_pairs={{0,64},{64,128},{128,192},{192,0},{1,65},{65,129},{129,193},{193,1... | collective-permute-start | bytes 786440 | tf_op jit(solution)/shard_map/ppermute | solution.py:299
  249.6 16.0 %collective-permute-start.13 = (bf16[1024,128]{1,0:T(8,128)(2,1)}, bf16[1024,128]{1,0:T(8,128)(2,1)S(1)}, u32[]{:S(2)}, u32[]{:S(2)}) collective-permute-start(bf16[1024,128]{1,0:T(8,128)(2,1)} %get-tuple-element.86), channel_id=1, source_target_pairs={{0,128},{64,192},{128,0},{192,64},{1,129},{65,193},{129,1},{193,65... | collective-permute-start | bytes 786440 | tf_op jit(solution)/shard_map/ppermute | solution.py:299
  253.6 12.0 %collective-permute-start.14 = (bf16[1024,128]{1,0:T(8,128)(2,1)}, bf16[1024,128]{1,0:T(8,128)(2,1)S(1)}, u32[]{:S(2)}, u32[]{:S(2)}) collective-permute-start(bf16[1024,128]{1,0:T(8,128)(2,1)} %get-tuple-element.87), channel_id=1, source_target_pairs={{0,192},{64,0},{128,64},{192,128},{1,193},{65,1},{129,65},{193,129... | collective-permute-start | bytes 786440 | tf_op jit(solution)/shard_map/ppermute | solution.py:299
  (30 other events, 373.4 us)

commit v6 on v5

--- a/solution.py
+++ b/solution.py
@@ -9,7 +9,7 @@
 
 BF = jnp.bfloat16
 F32 = jnp.float32
-VMEM_LIMIT = 8 * 1024 * 1024
+VMEM_LIMIT = 4 * 1024 * 1024
 LARGE_LIMIT = 58 * 1024 * 1024
 
 

time: 268 us -> 268 us (level)
  no operation moved by 1% of the time
where the time goes in v6:
time: 268 us; the launch traced here: 267 us
  blocking collectives  95.6 us (36%)
  waiting for transfers between devices  79.5 us (30%)
  starting transfers between devices  57.5 us (21%)
  Pallas kernels  28.5 us (11%)
  local copies, waits for them, and re-layouts  4.48 us (2%)
    ppermute x18, waiting for transfers between devices, passed(): lax.ppermute(value, 'segment', [(i, (i + step) % 4) for i in range(4)])  60.4 us
    all_to_all x3, blocking collectives, body(): columns[l] = lax.all_to_all(sends, 'seq', 0, 0, tiled=True)  60.2 us
    all_to_all x2, blocking collectives, body(): received = lax.all_to_all(back, 'seq', 0, 0, tiled=True)  35.5 us
    ppermute x18, starting transfers between devices, passed(): lax.ppermute(value, 'segment', [(i, (i + step) % 4) for i in range(4)])  24.5 us
    all_to_all x1, starting transfers between devices, body(): firsts_cols = lax.all_to_all(firsts_out, 'seq', 0, 0, tiled=True)  13.3 us
    all_to_all x2, starting transfers between devices, body(): received = lax.all_to_all(back, 'seq', 0, 0, tiled=True)  11.3 us
    pallas_call x4, Pallas kernels, body(): call(functools.partial(row_kernel, l) if l in (3, 0) else functools.parti...  9.91 us
    all_to_all x2, waiting for transfers between devices, body(): received = lax.all_to_all(back, 'seq', 0, 0, tiled=True)  9.08 us
  transfers between devices with their start and end apart: 22, of which 15 were waited for; matrix products, arithmetic and copies ran while one was open for 0% of the time, Pallas kernels for 4%

profile of v6, /device:TPU:1, one launch (start us, length us, event | category | flops | bytes accessed | tf_op | source)
XLA Modules:
  0.0 266.8 jit_solution(1202070945144163066)
XLA Ops:
  4.0 13.3 %all-to-all-start = ((bf16[64,4,16,128]{3,2,1,0:T(8,128)(2,1)}), bf16[64,4,16,128]{3,2,1,0:T(8,128)(2,1)S(1)}, u32[]{:S(2)}, u32[]{:S(2)}) async-start(bf16[64,4,16,128]{3,2,1,0:T(8,128)(2,1)} %shard_map.77), calls=%async_computation | async-start | bytes 2097152 | tf_op jit(solution)/shard_map/all_to_all | solution.py:330
  25.1 6.9 %collective-permute-done.near = bf16[1040,128]{1,0:T(8,128)(2,1)S(1)} collective-permute-done((bf16[1040,128]{1,0:T(8,128)(2,1)}, bf16[1040,128]{1,0:T(8,128)(2,1)S(1)}, u32[]{:S(2)}, u32[]{:S(2)}) %collective-permute-start) | collective-permute-done | bytes 266272 | tf_op jit(solution)/shard_map/ppermute | solution.py:299
  32.0 3.9 %collective-permute-done.1.far = bf16[1040,128]{1,0:T(8,128)(2,1)S(1)} collective-permute-done((bf16[1040,128]{1,0:T(8,128)(2,1)}, bf16[1040,128]{1,0:T(8,128)(2,1)S(1)}, u32[]{:S(2)}, u32[]{:S(2)}) %collective-permute-start.1) | collective-permute-done | bytes 266272 | tf_op jit(solution)/shard_map/ppermute | solution.py:299
  35.9 6.4 %collective-permute-done.2.last = bf16[1040,128]{1,0:T(8,128)(2,1)S(1)} collective-permute-done((bf16[1040,128]{1,0:T(8,128)(2,1)}, bf16[1040,128]{1,0:T(8,128)(2,1)S(1)}, u32[]{:S(2)}, u32[]{:S(2)}) %collective-permute-start.2) | collective-permute-done | bytes 266272 | tf_op jit(solution)/shard_map/ppermute | solution.py:299
  46.3 3.8 %shard_map.79 = (bf16[64,5,16,128]{3,2,1,0:T(8,128)(2,1)}, bf16[4,1024,128]{2,1,0:T(8,128)(2,1)}, f32[4,2,128]{2,1,0:T(2,128)}) custom-call(bf16[4,256,256]{2,1,0:T(8,128)(2,1)} %bitcast.6, bf16[64,4,16,128]{3,2,1,0:T(8,128)(2,1)} %copy-done.8, bf16[1024,128]{1,0:T(8,128)(2,1)} %get-tuple-element.53.upstream, bf16[1040,128]{1,0:T(8,128)(2,1)} %get-tuple-element.54.own, ...), custom_call_target="tpu_custom_call" | custom-call | flops 268435456 | bytes 2097152 | tf_op jit(solution)/shard_map/pallas_call | solution.py:335
  50.1 8.4 %all-to-all-start.1 = ((bf16[64,5,16,128]{3,2,1,0:T(8,128)(2,1)}), bf16[64,5,16,128]{3,2,1,0:T(8,128)(2,1)S(1)}, u32[]{:S(2)}, u32[]{:S(2)}) async-start(bf16[64,5,16,128]{3,2,1,0:T(8,128)(2,1)} %get-tuple-element.58), calls=%async_computation.1 | async-start | bytes 2621440 | tf_op jit(solution)/shard_map/all_to_all | solution.py:346
  63.5 9.7 %collective-permute-done.7.across = bf16[4,256,256]{2,1,0:T(8,128)(2,1)S(1)} collective-permute-done((bf16[4,256,256]{2,1,0:T(8,128)(2,1)}, bf16[4,256,256]{2,1,0:T(8,128)(2,1)S(1)}, u32[]{:S(2)}, u32[]{:S(2)}) %collective-permute-start.7) | collective-permute-done | bytes 524320 | tf_op jit(solution)/shard_map/ppermute | solution.py:299
  73.8 10.5 %collective-permute-done.5.right = bf16[4,256,256]{2,1,0:T(8,128)(2,1)S(1)} collective-permute-done((bf16[4,256,256]{2,1,0:T(8,128)(2,1)S(1)}, bf16[4,256,256]{2,1,0:T(8,128)(2,1)S(1)}, u32[]{:S(2)}, u32[]{:S(2)}) %collective-permute-start.5) | collective-permute-done | bytes 524320 | tf_op jit(solution)/shard_map/ppermute | solution.py:299
  85.2 7.0 %all-to-all-done.1.received.rest_2_ = bf16[64,5,16,128]{3,2,1,0:T(8,128)(2,1)S(1)} async-done(((bf16[64,5,16,128]{3,2,1,0:T(8,128)(2,1)}), bf16[64,5,16,128]{3,2,1,0:T(8,128)(2,1)S(1)}, u32[]{:S(2)}, u32[]{:S(2)}) %all-to-all-start.1) | async-done | bytes 1310752 | tf_op jit(solution)/shard_map/all_to_all | solution.py:346
  98.2 6.6 %all-to-all-start.2 = ((bf16[64,16,128]{2,1,0:T(8,128)(2,1)}), bf16[64,16,128]{2,1,0:T(8,128)(2,1)S(1)}, u32[]{:S(2)}, u32[]{:S(2)}) async-start(bf16[64,16,128]{2,1,0:T(8,128)(2,1)} %get-tuple-element.66), calls=%async_computation.2 | async-start | bytes 524288 | tf_op jit(solution)/shard_map/all_to_all | solution.py:368
  107.6 6.9 %collective-permute-done.9.rest_1_ = bf16[64,16,128]{2,1,0:T(8,128)(2,1)S(1)} collective-permute-done((bf16[64,16,128]{2,1,0:T(8,128)(2,1)}, bf16[64,16,128]{2,1,0:T(8,128)(2,1)S(1)}, u32[]{:S(2)}, u32[]{:S(2)}) %collective-permute-start.9) | collective-permute-done | bytes 262176 | tf_op jit(solution)/shard_map/ppermute | solution.py:299
  114.5 4.3 %collective-permute-done.10.rest_2_ = bf16[64,16,128]{2,1,0:T(8,128)(2,1)S(1)} collective-permute-done((bf16[64,16,128]{2,1,0:T(8,128)(2,1)}, bf16[64,16,128]{2,1,0:T(8,128)(2,1)S(1)}, u32[]{:S(2)}, u32[]{:S(2)}) %collective-permute-start.10) | collective-permute-done | bytes 262176 | tf_op jit(solution)/shard_map/ppermute | solution.py:299
  120.7 3.9 %shard_map.81 = (bf16[1024,128]{1,0:T(8,128)(2,1)}, bf16[64,16,128]{2,1,0:T(8,128)(2,1)}, bf16[4,64,16,128]{3,2,1,0:T(8,128)(2,1)}) custom-call(bf16[64,16,128]{2,1,0:T(8,128)(2,1)} %copy-done.25, bf16[1024,128]{1,0:T(8,128)(2,1)} %get-tuple-element.53.upstream, bf16[4,1024,128]{2,1,0:T(8,128)(2,1)} %get-tuple-element.67.held, ...), custom_call_target="tpu_custom_call" | custom-call | flops 67108864 | bytes 2097152 | tf_op jit(solution)/shard_map/pallas_call | solution.py:386
  124.7 24.8 %all_to_all.45.received.rest_1_ = bf16[64,16,128]{2,1,0:T(8,128)(2,1)S(1)} all-to-all(bf16[64,16,128]{2,1,0:T(8,128)(2,1)} %get-tuple-element.76), channel_id=1, replica_groups=mesh['segment'=4,'seq'=64] {'seq'}, dimensions={0} | all-to-all | bytes 524288 | tf_op jit(solution)/shard_map/all_to_all | solution.py:355
  150.1 17.8 %all_to_all.46.received = bf16[64,16,128]{2,1,0:T(8,128)(2,1)S(1)} all-to-all(bf16[64,16,128]{2,1,0:T(8,128)(2,1)S(1)} %shard_map.82), channel_id=1, replica_groups=mesh['segment'=4,'seq'=64] {'seq'}, dimensions={0} | all-to-all | bytes 524288 | tf_op jit(solution)/shard_map/all_to_all | solution.py:368
  170.3 17.7 %all_to_all.47.received.rest_0_ = bf16[64,16,128]{2,1,0:T(8,128)(2,1)S(1)} all-to-all(bf16[64,16,128]{2,1,0:T(8,128)(2,1)S(1)} %get-tuple-element.79), channel_id=1, replica_groups=mesh['segment'=4,'seq'=64] {'seq'}, dimensions={0} | all-to-all | bytes 524288 | tf_op jit(solution)/shard_map/all_to_all | solution.py:355
  189.5 17.7 %all_to_all.48.received = bf16[64,16,128]{2,1,0:T(8,128)(2,1)S(1)} all-to-all(bf16[64,16,128]{2,1,0:T(8,128)(2,1)S(1)} %shard_map.84), channel_id=1, replica_groups=mesh['segment'=4,'seq'=64] {'seq'}, dimensions={0} | all-to-all | bytes 524288 | tf_op jit(solution)/shard_map/all_to_all | solution.py:368
  208.6 17.7 %all_to_all.49.received = bf16[64,16,128]{2,1,0:T(8,128)(2,1)S(1)} all-to-all(bf16[64,16,128]{2,1,0:T(8,128)(2,1)S(1)} %get-tuple-element.81), channel_id=1, replica_groups=mesh['segment'=4,'seq'=64] {'seq'}, dimensions={0} | all-to-all | bytes 524288 | tf_op jit(solution)/shard_map/all_to_all | solution.py:355
  227.7 4.7 %all-to-all-start.8 = ((bf16[64,16,128]{2,1,0:T(8,128)(2,1)}), bf16[64,16,128]{2,1,0:T(8,128)(2,1)S(1)}, u32[]{:S(2)}, u32[]{:S(2)}) async-start(bf16[64,16,128]{2,1,0:T(8,128)(2,1)} %get-tuple-element.82), calls=%async_computation.8 | async-start | bytes 524288 | tf_op jit(solution)/shard_map/all_to_all | solution.py:368
  232.5 4.0 %collective-permute-start.16 = (bf16[64,16,128]{2,1,0:T(8,128)(2,1)S(1)}, bf16[64,16,128]{2,1,0:T(8,128)(2,1)S(1)}, u32[]{:S(2)}, u32[]{:S(2)}) collective-permute-start(bf16[64,16,128]{2,1,0:T(8,128)(2,1)S(1)} %get-tuple-element.90), channel_id=1, source_target_pairs={{0,128},{64,192},{128,0},{192,64},{1,129},{65,193},{129,1},{193,65... | collective-permute-start | bytes 786440 | tf_op jit(solution)/shard_map/ppermute | solution.py:299
  236.5 9.1 %all-to-all-done.8.received = bf16[64,16,128]{2,1,0:T(8,128)(2,1)S(1)} async-done(((bf16[64,16,128]{2,1,0:T(8,128)(2,1)}), bf16[64,16,128]{2,1,0:T(8,128)(2,1)S(1)}, u32[]{:S(2)}, u32[]{:S(2)}) %all-to-all-start.8) | async-done | bytes 262176 | tf_op jit(solution)/shard_map/all_to_all | solution.py:368
  249.6 4.0 %collective-permute-start.13 = (bf16[1024,128]{1,0:T(8,128)(2,1)}, bf16[1024,128]{1,0:T(8,128)(2,1)S(1)}, u32[]{:S(2)}, u32[]{:S(2)}) collective-permute-start(bf16[1024,128]{1,0:T(8,128)(2,1)} %get-tuple-element.86), channel_id=1, source_target_pairs={{0,128},{64,192},{128,0},{192,64},{1,129},{65,193},{129,1},{193,65... | collective-permute-start | bytes 786440 | tf_op jit(solution)/shard_map/ppermute | solution.py:299
  255.4 3.6 %collective-permute-done.12.near = bf16[1024,128]{1,0:T(8,128)(2,1)S(1)} collective-permute-done((bf16[1024,128]{1,0:T(8,128)(2,1)}, bf16[1024,128]{1,0:T(8,128)(2,1)S(1)}, u32[]{:S(2)}, u32[]{:S(2)}) %collective-permute-start.12) | collective-permute-done | bytes 262176 | tf_op jit(solution)/shard_map/ppermute | solution.py:299
  259.0 6.6 %collective-permute-done.13.far = bf16[1024,128]{1,0:T(8,128)(2,1)S(1)} collective-permute-done((bf16[1024,128]{1,0:T(8,128)(2,1)}, bf16[1024,128]{1,0:T(8,128)(2,1)S(1)}, u32[]{:S(2)}, u32[]{:S(2)}) %collective-permute-start.13) | collective-permute-done | bytes 262176 | tf_op jit(solution)/shard_map/ppermute | solution.py:299
  (102 shorter events, 46.5 us)
Async XLA Ops:
  4.0 41.3 %all-to-all-start = ((bf16[64,4,16,128]{3,2,1,0:T(8,128)(2,1)}), bf16[64,4,16,128]{3,2,1,0:T(8,128)(2,1)S(1)}, u32[]{:S(2)}, u32[]{:S(2)}) async-start(bf16[64,4,16,128]{3,2,1,0:T(8,128)(2,1)} %shard_map.77), calls=%async_computation | async-start | bytes 2097152 | tf_op jit(solution)/shard_map/all_to_all | solution.py:330
  17.4 24.9 %collective-permute-start.3 = (bf16[4,256,256]{2,1,0:T(8,128)(2,1)S(1)}, bf16[4,256,256]{2,1,0:T(8,128)(2,1)}, u32[]{:S(2)}, u32[]{:S(2)}) collective-permute-start(bf16[4,256,256]{2,1,0:T(8,128)(2,1)S(1)} %bitcast.8), channel_id=1, source_target_pairs={{0,192},{64,0},{128,64},{192,128},{1,193},{65,1},{129,65},{193,129... | collective-permute-start | bytes 1572872 | tf_op jit(solution)/shard_map/ppermute | solution.py:299
  22.4 9.6 %collective-permute-start = (bf16[1040,128]{1,0:T(8,128)(2,1)}, bf16[1040,128]{1,0:T(8,128)(2,1)S(1)}, u32[]{:S(2)}, u32[]{:S(2)}) collective-permute-start(bf16[1040,128]{1,0:T(8,128)(2,1)} %get-tuple-element.48), channel_id=1, source_target_pairs={{0,64},{64,128},{128,192},{192,0},{1,65},{65,129},{129,193},{193,1... | collective-permute-start | bytes 798728 | tf_op jit(solution)/shard_map/ppermute | solution.py:299
  22.5 13.4 %collective-permute-start.1 = (bf16[1040,128]{1,0:T(8,128)(2,1)}, bf16[1040,128]{1,0:T(8,128)(2,1)S(1)}, u32[]{:S(2)}, u32[]{:S(2)}) collective-permute-start(bf16[1040,128]{1,0:T(8,128)(2,1)} %get-tuple-element.49), channel_id=1, source_target_pairs={{0,128},{64,192},{128,0},{192,64},{1,129},{65,193},{129,1},{193,65... | collective-permute-start | bytes 798728 | tf_op jit(solution)/shard_map/ppermute | solution.py:299
  24.2 18.1 %collective-permute-start.2 = (bf16[1040,128]{1,0:T(8,128)(2,1)}, bf16[1040,128]{1,0:T(8,128)(2,1)S(1)}, u32[]{:S(2)}, u32[]{:S(2)}) collective-permute-start(bf16[1040,128]{1,0:T(8,128)(2,1)} %get-tuple-element.50), channel_id=1, source_target_pairs={{0,192},{64,0},{128,64},{192,128},{1,193},{65,1},{129,65},{193,129... | collective-permute-start | bytes 798728 | tf_op jit(solution)/shard_map/ppermute | solution.py:299
  50.1 42.0 %all-to-all-start.1 = ((bf16[64,5,16,128]{3,2,1,0:T(8,128)(2,1)}), bf16[64,5,16,128]{3,2,1,0:T(8,128)(2,1)S(1)}, u32[]{:S(2)}, u32[]{:S(2)}) async-start(bf16[64,5,16,128]{3,2,1,0:T(8,128)(2,1)} %get-tuple-element.58), calls=%async_computation.1 | async-start | bytes 2621440 | tf_op jit(solution)/shard_map/all_to_all | solution.py:346
  58.6 15.3 %collective-permute-start.6 = (bf16[4,256,256]{2,1,0:T(8,128)(2,1)S(1)}, bf16[4,256,256]{2,1,0:T(8,128)(2,1)S(1)}, u32[]{:S(2)}, u32[]{:S(2)}) collective-permute-start(bf16[4,256,256]{2,1,0:T(8,128)(2,1)S(1)} %bitcast.9), channel_id=1, source_target_pairs={{0,64},{64,128},{128,192},{192,0},{1,65},{65,129},{129,193},{193,1... | collective-permute-start | bytes 1572872 | tf_op jit(solution)/shard_map/ppermute | solution.py:299
  59.5 13.7 %collective-permute-start.7 = (bf16[4,256,256]{2,1,0:T(8,128)(2,1)}, bf16[4,256,256]{2,1,0:T(8,128)(2,1)S(1)}, u32[]{:S(2)}, u32[]{:S(2)}) collective-permute-start(bf16[4,256,256]{2,1,0:T(8,128)(2,1)} %collective-permute-done.3.right), channel_id=1, source_target_pairs={{0,192},{64,0},{128,64},{192,128},{1,193},{65,1},{129,65},{193,129... | collective-permute-start | bytes 1572872 | tf_op jit(solution)/shard_map/ppermute | solution.py:299
  62.0 22.3 %collective-permute-start.5 = (bf16[4,256,256]{2,1,0:T(8,128)(2,1)S(1)}, bf16[4,256,256]{2,1,0:T(8,128)(2,1)S(1)}, u32[]{:S(2)}, u32[]{:S(2)}) collective-permute-start(bf16[4,256,256]{2,1,0:T(8,128)(2,1)S(1)} %bitcast.16), channel_id=1, source_target_pairs={{0,192},{64,0},{128,64},{192,128},{1,193},{65,1},{129,65},{193,129... | collective-permute-start | bytes 1572872 | tf_op jit(solution)/shard_map/ppermute | solution.py:299
  63.4 21.8 %collective-permute-start.4 = (bf16[4,256,256]{2,1,0:T(8,128)(2,1)S(1)}, bf16[4,256,256]{2,1,0:T(8,128)(2,1)}, u32[]{:S(2)}, u32[]{:S(2)}) collective-permute-start(bf16[4,256,256]{2,1,0:T(8,128)(2,1)S(1)} %bitcast.17), channel_id=1, source_target_pairs={{0,64},{64,128},{128,192},{192,0},{1,65},{65,129},{129,193},{193,1... | collective-permute-start | bytes 1572872 | tf_op jit(solution)/shard_map/ppermute | solution.py:299
  92.2 27.6 %collective-permute-start.8 = (bf16[4,256,256]{2,1,0:T(8,128)(2,1)}, bf16[4,256,256]{2,1,0:T(8,128)(2,1)S(1)}, u32[]{:S(2)}, u32[]{:S(2)}) collective-permute-start(bf16[4,256,256]{2,1,0:T(8,128)(2,1)} %copy-done.15), channel_id=1, source_target_pairs={{0,192},{64,0},{128,64},{192,128},{1,193},{65,1},{129,65},{193,129... | collective-permute-start | bytes 1572872 | tf_op jit(solution)/shard_map/ppermute | solution.py:299
  98.2 21.5 %all-to-all-start.2 = ((bf16[64,16,128]{2,1,0:T(8,128)(2,1)}), bf16[64,16,128]{2,1,0:T(8,128)(2,1)S(1)}, u32[]{:S(2)}, u32[]{:S(2)}) async-start(bf16[64,16,128]{2,1,0:T(8,128)(2,1)} %get-tuple-element.66), calls=%async_computation.2 | async-start | bytes 524288 | tf_op jit(solution)/shard_map/all_to_all | solution.py:368
  104.8 9.6 %collective-permute-start.9 = (bf16[64,16,128]{2,1,0:T(8,128)(2,1)}, bf16[64,16,128]{2,1,0:T(8,128)(2,1)S(1)}, u32[]{:S(2)}, u32[]{:S(2)}) collective-permute-start(bf16[64,16,128]{2,1,0:T(8,128)(2,1)} %get-tuple-element.73), channel_id=1, source_target_pairs={{0,64},{64,128},{128,192},{192,0},{1,65},{65,129},{129,193},{193,1... | collective-permute-start | bytes 786440 | tf_op jit(solution)/shard_map/ppermute | solution.py:299
  104.9 13.8 %collective-permute-start.10 = (bf16[64,16,128]{2,1,0:T(8,128)(2,1)}, bf16[64,16,128]{2,1,0:T(8,128)(2,1)S(1)}, u32[]{:S(2)}, u32[]{:S(2)}) collective-permute-start(bf16[64,16,128]{2,1,0:T(8,128)(2,1)} %get-tuple-element.74), channel_id=1, source_target_pairs={{0,128},{64,192},{128,0},{192,64},{1,129},{65,193},{129,1},{193,65... | collective-permute-start | bytes 786440 | tf_op jit(solution)/shard_map/ppermute | solution.py:299
  106.9 12.8 %collective-permute-start.11 = (bf16[64,16,128]{2,1,0:T(8,128)(2,1)}, bf16[64,16,128]{2,1,0:T(8,128)(2,1)S(1)}, u32[]{:S(2)}, u32[]{:S(2)}) collective-permute-start(bf16[64,16,128]{2,1,0:T(8,128)(2,1)} %get-tuple-element.75), channel_id=1, source_target_pairs={{0,192},{64,0},{128,64},{192,128},{1,193},{65,1},{129,65},{193,129... | collective-permute-start | bytes 786440 | tf_op jit(solution)/shard_map/ppermute | solution.py:299
  120.7 47.2 %copy-start.23 = (f32[4,2,128]{2,1,0:T(2,128)S(1)}, f32[4,2,128]{2,1,0:T(2,128)}, u32[]{:S(2)}) copy-start(f32[4,2,128]{2,1,0:T(2,128)} %get-tuple-element.68.vectors) | copy-start | bytes 12292
  124.7 43.3 %copy-start.18 = (bf16[4,256,256]{2,1,0:T(8,128)(2,1)S(1)}, bf16[4,256,256]{2,1,0:T(8,128)(2,1)}, u32[]{:S(2)}) copy-start(bf16[4,256,256]{2,1,0:T(8,128)(2,1)} %copy-done.17) | copy-start | bytes 1572868
  227.7 17.9 %all-to-all-start.8 = ((bf16[64,16,128]{2,1,0:T(8,128)(2,1)}), bf16[64,16,128]{2,1,0:T(8,128)(2,1)S(1)}, u32[]{:S(2)}, u32[]{:S(2)}) async-start(bf16[64,16,128]{2,1,0:T(8,128)(2,1)} %get-tuple-element.82), calls=%async_computation.8 | async-start | bytes 524288 | tf_op jit(solution)/shard_map/all_to_all | solution.py:368
  232.4 21.2 %collective-permute-start.15 = (bf16[64,16,128]{2,1,0:T(8,128)(2,1)S(1)}, bf16[64,16,128]{2,1,0:T(8,128)(2,1)S(1)}, u32[]{:S(2)}, u32[]{:S(2)}) collective-permute-start(bf16[64,16,128]{2,1,0:T(8,128)(2,1)S(1)} %get-tuple-element.89), channel_id=1, source_target_pairs={{0,64},{64,128},{128,192},{192,0},{1,65},{65,129},{129,193},{193,1... | collective-permute-start | bytes 786440 | tf_op jit(solution)/shard_map/ppermute | solution.py:299
  232.5 21.1 %collective-permute-start.16 = (bf16[64,16,128]{2,1,0:T(8,128)(2,1)S(1)}, bf16[64,16,128]{2,1,0:T(8,128)(2,1)S(1)}, u32[]{:S(2)}, u32[]{:S(2)}) collective-permute-start(bf16[64,16,128]{2,1,0:T(8,128)(2,1)S(1)} %get-tuple-element.90), channel_id=1, source_target_pairs={{0,128},{64,192},{128,0},{192,64},{1,129},{65,193},{129,1},{193,65... | collective-permute-start | bytes 786440 | tf_op jit(solution)/shard_map/ppermute | solution.py:299
  236.5 17.1 %collective-permute-start.17 = (bf16[64,16,128]{2,1,0:T(8,128)(2,1)S(1)}, bf16[64,16,128]{2,1,0:T(8,128)(2,1)S(1)}, u32[]{:S(2)}, u32[]{:S(2)}) collective-permute-start(bf16[64,16,128]{2,1,0:T(8,128)(2,1)S(1)} %get-tuple-element.91), channel_id=1, source_target_pairs={{0,192},{64,0},{128,64},{192,128},{1,193},{65,1},{129,65},{193,129... | collective-permute-start | bytes 786440 | tf_op jit(solution)/shard_map/ppermute | solution.py:299
  249.5 9.5 %collective-permute-start.12 = (bf16[1024,128]{1,0:T(8,128)(2,1)}, bf16[1024,128]{1,0:T(8,128)(2,1)S(1)}, u32[]{:S(2)}, u32[]{:S(2)}) collective-permute-start(bf16[1024,128]{1,0:T(8,128)(2,1)} %get-tuple-element.85), channel_id=1, source_target_pairs={{0,64},{64,128},{128,192},{192,0},{1,65},{65,129},{129,193},{193,1... | collective-permute-start | bytes 786440 | tf_op jit(solution)/shard_map/ppermute | solution.py:299
  249.6 16.0 %collective-permute-start.13 = (bf16[1024,128]{1,0:T(8,128)(2,1)}, bf16[1024,128]{1,0:T(8,128)(2,1)S(1)}, u32[]{:S(2)}, u32[]{:S(2)}) collective-permute-start(bf16[1024,128]{1,0:T(8,128)(2,1)} %get-tuple-element.86), channel_id=1, source_target_pairs={{0,128},{64,192},{128,0},{192,64},{1,129},{65,193},{129,1},{193,65... | collective-permute-start | bytes 786440 | tf_op jit(solution)/shard_map/ppermute | solution.py:299
  253.6 12.0 %collective-permute-start.14 = (bf16[1024,128]{1,0:T(8,128)(2,1)}, bf16[1024,128]{1,0:T(8,128)(2,1)S(1)}, u32[]{:S(2)}, u32[]{:S(2)}) collective-permute-start(bf16[1024,128]{1,0:T(8,128)(2,1)} %get-tuple-element.87), channel_id=1, source_target_pairs={{0,192},{64,0},{128,64},{192,128},{1,193},{65,1},{129,65},{193,129... | collective-permute-start | bytes 786440 | tf_op jit(solution)/shard_map/ppermute | solution.py:299
  (30 other events, 373.4 us)
